TPU v7x, 128 devices: a whole 4x4x4 slice. The times are simulated.
128 devices in a mesh: grid: 32 (over x, y, core), mesh: 4 (over z).
Axes of the slice: x: 4, y: 4, z: 4, core: 2. Of those that a mesh axis runs over, the one named last changes fastest.
Arguments:
- grid_latent: bfloat16 [131072, 512], P(('grid', 'mesh')), may hold values from -6 to 6
- mesh_latent: bfloat16 [20480, 512], P(('grid', 'mesh')), may hold values from -6 to 6
- enc_source: int32 [262144], P(('grid', 'mesh')), may hold values from 0 to 1023
- enc_slot: int32 [262144], P(('grid', 'mesh')), may hold values from 0 to 1023, as said below
- enc_geometry: float32 [4, 262144], P(None, ('grid', 'mesh')), may hold values from -6 to 6
- edge_count: int32 [128], P(('grid', 'mesh')), may hold values from 512 to 2048, as said below
- slot_row: int32 [128, 2, 4, 128], P(('grid', 'mesh')), may hold values from 0 to 159
- halo_rows: int32 [128, 128, 8], P(('grid', 'mesh')), may hold values from 0 to 159
- proc_source: int32 [163840], P(('grid', 'mesh')), may hold values from 0 to 1183
- proc_target: int32 [163840], P(('grid', 'mesh')), may hold values from 0 to 159
- proc_geometry: float32 [4, 163840], P(None, ('grid', 'mesh')), may hold values from -6 to 6
- return_rows: int32 [128, 2, 4, 128], P(('grid', 'mesh')), may hold values from 0 to 159
- dec_source: int32 [131072, 3], P(('grid', 'mesh')), may hold values from 0 to 1023, as said below
- dec_geometry: float32 [4, 3, 131072], P(None, None, ('grid', 'mesh')), may hold values from -6 to 6
- enc_weights: bfloat16 [5, 512, 512], replicated, may hold values from -0.25 to 0.25
- enc_lift: float32 [4, 512], replicated, may hold values from -3 to 3
- proc_weights: bfloat16 [2, 6, 512, 512], replicated, may hold values from -0.25 to 0.25
- proc_lift: float32 [2, 4, 512], replicated, may hold values from -3 to 3
- dec_weights: bfloat16 [3, 512, 512], replicated, may hold values from -0.25 to 0.25
- dec_lift: float32 [4, 512], replicated, may hold values from -3 to 3
Outputs:
- grid_out: bfloat16 [131072, 512], P(('grid', 'mesh'))
- mesh_out: bfloat16 [20480, 512], P(('grid', 'mesh'))
Inputs may be any that keep to these rules, and one draw needn't show every extreme that they name: An edge of a device in strip g feeds strip g + enc_slot // (4 * 128), one of its own strip and the next (2 strips); devices of the last strip use only their own strip. `edge_count`: some device has all 2048 edges live. A grid node of strip g reads from strip g + dec_source // (4 * 128), its own or the next; nodes of the last strip read only from their own strip.
All inputs are finite; a program needn't handle non-finite values.
Results may differ from a plain program's by a relative error of at most 0.02.
Values may be sent and summed in bfloat16 or wider, within the bound.
No kernel may reach another device: no remote copies, remote signals or barrier semaphores. Data moves between devices by JAX's collectives and lax.ppermute only.
A program may use at most 64 MiB of HBM per device.

v0:
```python
import functools

import jax
import jax.numpy as jnp
from jax import lax
from jax.experimental import pallas as pl
from jax.experimental.pallas import tpu as pltpu
from jax.sharding import PartitionSpec as P

BF = jnp.bfloat16
F32 = jnp.float32
VM = pl.BlockSpec(memory_space=pltpu.VMEM)
SM = pl.BlockSpec(memory_space=pltpu.SMEM)
HB = pl.BlockSpec(memory_space=pltpu.HBM)
ANY = pl.BlockSpec(memory_space=pl.ANY)
MIB = 1024 * 1024
BLOCK = 256


def mm(a, b):
    return lax.dot_general(a, b, (((1,), (0,)), ((), ())), preferred_element_type=F32)


def mm_tn(a, b):
    return lax.dot_general(a, b, (((0,), (0,)), ((), ())), preferred_element_type=F32)


def to_columns(row):
    n = row.shape[1]
    parts = [jnp.broadcast_to(row[:, at:at + 128], (128, 128)).T for at in range(0, n, 128)]
    return jnp.concatenate(parts, axis=0) if len(parts) > 1 else parts[0]


def lane_hits(columns, at):
    return columns - jnp.int16(at) == lax.broadcasted_iota(jnp.int16, columns.shape, 1)


def as_ones(hits):
    return jnp.where(hits, jnp.ones(hits.shape, BF), jnp.zeros(hits.shape, BF))


def pick_matrix(columns, width):
    col = columns.astype(jnp.int16)
    return jnp.concatenate([as_ones(lane_hits(col, at)) for at in range(0, width, 128)], axis=1)


def add_matrix(row, height):
    n = row.shape[1]
    wide = jnp.broadcast_to(row, (16, n)).astype(jnp.int16)
    wide = jnp.broadcast_to(wide[None], (height // 16, 16, n)).reshape(height, n)
    return as_ones(wide == lax.broadcasted_iota(jnp.int16, (height, n), 0))


def split3(x):
    a = x.astype(BF).astype(F32)
    r = x - a
    b = r.astype(BF).astype(F32)
    return a, b, r - b


def lift(geometry, right):
    a, b, c = split3(geometry)
    return mm_tn(jnp.concatenate([a, a, b, b, a, c], axis=0).astype(BF), right)


def lift_right(weight):
    a, b, c = split3(weight)
    return jnp.concatenate([a, b, a, b, c, a], axis=0).astype(BF)


def half_silu(half):
    return half + half * jnp.tanh(half)


def norm(v):
    c = v - jnp.mean(v, axis=-1, keepdims=True)
    return c * lax.rsqrt(jnp.mean(c * c, axis=-1, keepdims=True) + 1e-05)


def node_update(latent, total, w_self, w_total, w_out):
    inner = mm(latent, w_self) + mm(total.astype(BF), w_total)
    hidden = half_silu(inner * 0.5).astype(BF)
    return (latent.astype(F32) + norm(mm(hidden, w_out))).astype(BF)


def pick_rows(row, table):
    rows = table.shape[0]
    wide = -(-rows // 128) * 128
    if wide > rows:
        table = jnp.concatenate([table, jnp.zeros((wide - rows, table.shape[1]), BF)], axis=0)
    parts = []
    for at in range(0, row.shape[1], BLOCK):
        cut = row[:, at:at + BLOCK]
        parts.append(mm(pick_matrix(to_columns(cut), wide), table).astype(BF))
    return jnp.concatenate(parts, axis=0) if len(parts) > 1 else parts[0]


def lanes(ref, at, count):
    return jnp.concatenate([ref[r:r + 1, :] for r in range(at // 128, (at + count) // 128)], axis=1)


class Held:
    def __init__(self, sems, **pairs):
        self.copies, self.refs = {}, {}
        for at, (name, (src, dst)) in enumerate(pairs.items()):
            self.refs[name] = dst
            self.copies[name] = pltpu.make_async_copy(src, dst, sems.at[at])
            self.copies[name].start()

    def __call__(self, name):
        if name in self.copies:
            self.copies.pop(name).wait()
        return self.refs[name]


def turned(index, count, me):
    return lax.bitwise_and(index - me, count - 1)


def row_of(rows, at):
    out = None
    for s in range(rows.shape[0]):
        part = jnp.where(at == s, rows[s:s + 1, :], 0)
        out = part if out is None else out + part
    return out


def rows_from(rows, me):
    count = rows.shape[0]
    return jnp.concatenate([row_of(rows, lax.bitwise_and(me - dz, count - 1)) for dz in range(count)], axis=1)


def rows_to(rows, me):
    count = rows.shape[0]
    return jnp.concatenate([row_of(rows, lax.bitwise_and(me + dz, count - 1)) for dz in range(count)], axis=1)


def slot_sums(slot, part, n_mesh, message, outs):
    count = outs[0].shape[0]
    band = n_mesh * count
    me = lax.axis_index("mesh")
    local = slot - part * band
    turn = turned(lax.div(local, count), n_mesh, me) * count + lax.bitwise_and(local, count - 1)
    turn = jnp.where((local >= 0) & (local < band), turn, -1)
    total = mm(add_matrix(turn, band), message)
    for dz in range(n_mesh):
        outs[dz][...] = total[dz * count:(dz + 1) * count].astype(BF)


def encode_kernel(
    count_ref, grid_hbm, src_hbm, slot_hbm, geo_hbm, w_hbm, lift_hbm, feeds_hbm, returns_hbm, message_ref, slot_out, rows_out, *rest
):
    outs, (grid_ref, src_ref, slot_ref, geo_ref, w0_ref, w1_ref, lift_ref, table_ref, sems) = rest[:4], rest[4:]
    held = Held(
        sems, grid=(grid_hbm, grid_ref), w0=(w_hbm.at[0], w0_ref), src=(src_hbm, src_ref), geo=(geo_hbm, geo_ref),
        lift=(lift_hbm, lift_ref), w1=(w_hbm.at[1], w1_ref), slot=(slot_hbm, slot_ref),
        feeds=(feeds_hbm.at[1], rows_out.at[0]), returns=(returns_hbm.at[1], rows_out.at[1]),
    )
    edges = message_ref.shape[0]
    grid = held("grid")[...]
    table_ref[...] = (mm(grid, held("w0")[...]) * 0.5).astype(BF)
    nodes = grid.shape[0]
    held("src"), held("geo"), held("w1")
    right = lift_right(held("lift")[...] * 0.5)
    for at in range(0, edges, BLOCK):
        cut = slice(at, at + BLOCK)
        half = mm(pick_matrix(to_columns(lanes(src_ref, at, BLOCK)), nodes), table_ref[...]) + lift(geo_ref[:, cut], right)
        message_ref[cut, :] = norm(mm(half_silu(half).astype(BF), w1_ref[...])).astype(BF)
    slot = lanes(held("slot"), 0, edges)
    slot = jnp.where(lax.broadcasted_iota(jnp.int32, slot.shape, 1) < count_ref[0], slot, -1)
    slot_out[...] = slot
    held("feeds"), held("returns")
    slot_sums(slot, 1, len(outs), message_ref[...], outs)


def near_kernel(message_ref, slot_ref, *outs):
    slot_sums(slot_ref[...], 0, len(outs), message_ref[...], outs)


def far_kernel(*refs):
    *blocks, rows_ref, _, low_ref, high_ref = refs
    rows = rows_from(rows_ref[0], lax.axis_index("mesh"))
    table = jnp.concatenate([b[...] for b in blocks], axis=0)
    total = mm(add_matrix(rows, 2 * low_ref.shape[0]), table).astype(BF)
    low_ref[...] = total[:low_ref.shape[0]]
    high_ref[...] = total[low_ref.shape[0]:]


def first_kernel(*refs):
    *blocks, low_ref, high_ref, rows_ref, halo_ref, latent_hbm, w_hbm, next_hbm, out_ref, sender_ref, sent_ref = refs[:-6]
    latent_ref, wa_ref, wb_ref, wc_ref, wn_ref, sems = refs[-6:]
    held = Held(
        sems, latent=(latent_hbm, latent_ref), wa=(w_hbm.at[2], wa_ref), wb=(w_hbm.at[3], wb_ref),
        wc=(w_hbm.at[4], wc_ref), wn=(next_hbm.at[0, 0], wn_ref),
    )
    rows = rows_from(rows_ref[0], lax.axis_index("mesh"))
    table = jnp.concatenate([b[...] for b in blocks], axis=0)
    total = mm(add_matrix(rows, out_ref.shape[0]), table)
    total = total + jnp.concatenate([low_ref[...], high_ref[...]], axis=0).astype(F32)
    latent = node_update(held("latent")[...], total, held("wa")[...], held("wb")[...], held("wc")[...])
    out_ref[...] = latent
    sender = (mm(latent, held("wn")[...]) * 0.5).astype(BF)
    sender_ref[...] = sender
    sent_ref[...] = pick_rows(halo_ref[...], sender)


def before_kernel(latent_ref, sender_ref, src_hbm, tgt_hbm, geo_hbm, lift_hbm, w_hbm, base_hbm, own_ref, src_out, tgt_out,
                  geo_ref, lift_ref, wb_ref, wd_ref, base_ref, sems, out_sems, *, layer):
    held = Held(
        sems, wb=(w_hbm.at[layer, 1], wb_ref), src=(src_hbm, src_out), tgt=(tgt_hbm, tgt_out), geo=(geo_hbm, geo_ref),
        lift=(lift_hbm.at[layer], lift_ref), wd=(w_hbm.at[layer, 3], wd_ref),
    )
    latent = latent_ref[...]
    rows = latent.shape[0]
    target = (mm(latent, held("wb")[...]) * 0.5).astype(BF)
    wide = -(-2 * rows // 128) * 128
    pieces = [sender_ref[...], target]
    if wide > 2 * rows:
        pieces.append(jnp.zeros((wide - 2 * rows, latent.shape[1]), BF))
    table = jnp.concatenate(pieces, axis=0)
    held("src"), held("tgt"), held("geo")
    right = lift_right(held("lift")[...] * 0.5)
    sent = []
    for at in range(0, base_ref.shape[0], BLOCK):
        cut = slice(at, at + BLOCK)
        src = lanes(src_out, at, BLOCK)
        src_col = to_columns(jnp.where(src < rows, src, -1)).astype(jnp.int16)
        tgt_col = to_columns(lanes(tgt_out, at, BLOCK) + rows).astype(jnp.int16)
        groups = [as_ones(lane_hits(src_col, lane) | lane_hits(tgt_col, lane)) for lane in range(0, wide, 128)]
        base_ref[cut, :] = mm(jnp.concatenate(groups, axis=1), table) + lift(geo_ref[:, cut], right)
        sent.append(pltpu.make_async_copy(base_ref.at[cut, :], base_hbm.at[cut, :], out_sems.at[at // BLOCK]))
        sent[-1].start()
    own_ref[...] = mm(latent, held("wd")[...])
    for copy in sent:
        copy.wait()


def layer_kernel(latent_ref, came_ref, base_hbm, own_ref, src_ref, tgt_ref, pick_ref, w_hbm, next_hbm, *rest, layer, last):
    outs, (message_ref, wc_ref, we_ref, wf_ref, wn_ref, base_ref, sems, in_sems) = rest[:-8], rest[-8:]
    cuts = [slice(at, at + BLOCK) for at in range(0, base_ref.shape[0], BLOCK)]
    bases = Held(in_sems, **{f"b{i}": (base_hbm.at[cut, :], base_ref.at[cut, :]) for i, cut in enumerate(cuts)})
    held = Held(
        sems, wc=(w_hbm.at[layer, 2], wc_ref), we=(w_hbm.at[layer, 4], we_ref), wf=(w_hbm.at[layer, 5], wf_ref),
        wn=(next_hbm.at[0] if last else next_hbm.at[layer + 1, 0], wn_ref),
    )
    latent = latent_ref[...]
    rows = latent.shape[0]
    halo = came_ref.shape[0]
    for at in range(0, base_ref.shape[0], BLOCK):
        cut = slice(at, at + BLOCK)
        half = mm(pick_matrix(to_columns(lanes(src_ref, at, BLOCK) - rows), halo), came_ref[...]) + bases(f"b{at // BLOCK}")[...]
        message_ref[cut, :] = norm(mm(half_silu(half).astype(BF), held("wc")[...])).astype(BF)
    total = mm(add_matrix(lanes(tgt_ref, 0, base_ref.shape[0]), rows), message_ref[...])
    inner = own_ref[...] + mm(total.astype(BF), held("we")[...])
    hidden = half_silu(inner * 0.5).astype(BF)
    latent = (latent.astype(F32) + norm(mm(hidden, held("wf")[...]))).astype(BF)
    outs[0][...] = latent
    onward = mm(latent, held("wn")[...])
    if last:
        onward = onward.astype(BF)
        outs[1][...] = onward
        spread(rows_to(pick_ref[0], lax.axis_index("mesh")), onward, outs[2:])
    else:
        onward = (onward * 0.5).astype(BF)
        outs[1][...] = onward
        outs[2][...] = pick_rows(pick_ref[...], onward)


def spread(row, table, outs):
    picked = pick_rows(row, table)
    count = outs[0].shape[0]
    for dz, out in enumerate(outs):
        out[...] = picked[dz * count:(dz + 1) * count]


def spread_kernel(table_ref, rows_ref, *outs):
    spread(rows_to(rows_ref[1], lax.axis_index("mesh")), table_ref[...], outs)


def place_columns(place, part, n_mesh, count):
    me = lax.axis_index("mesh")
    local = place - part * n_mesh * count
    turn = lax.bitwise_and(me - lax.div(local, count), n_mesh - 1) * count + lax.bitwise_and(local, count - 1)
    return to_columns(jnp.where((local >= 0) & (local < n_mesh * count), turn, -1))


def decode_near_kernel(*refs):
    *blocks, grid_hbm, src_hbm, geo_hbm, lift_hbm, w_hbm, base_ref, grid_ref, src_ref, geo_ref, lift_ref, w_ref, own_ref, sems = refs
    held = Held(
        sems, grid=(grid_hbm, grid_ref), w=(w_hbm.at[1], w_ref), src=(src_hbm, src_ref), geo=(geo_hbm, geo_ref),
        lift=(lift_hbm, lift_ref),
    )
    own_ref[...] = mm(held("grid")[...], held("w")[...]) * 0.5
    table = jnp.concatenate([b[...] for b in blocks], axis=0) * 0.5
    count = blocks[0].shape[0]
    right = lift_right(held("lift")[...] * 0.5)
    held("src"), held("geo")
    for at in range(0, own_ref.shape[0], BLOCK):
        cut = slice(at, at + BLOCK)
        for which in range(src_ref.shape[0]):
            columns = place_columns(src_ref[which:which + 1, cut], 0, len(blocks), count)
            chosen = mm(pick_matrix(columns, table.shape[0]), table)
            base_ref[which, cut, :] = chosen + lift(geo_ref[which, :, cut], right) + own_ref[cut, :]


def decode_kernel(*refs):
    *blocks, base_ref, grid_hbm, src_hbm, w_hbm, out_ref, grid_ref, src_ref, w_ref, sems = refs
    held = Held(sems, src=(src_hbm, src_ref), w=(w_hbm.at[2], w_ref), grid=(grid_hbm, grid_ref))
    table = jnp.concatenate([b[...] for b in blocks], axis=0) * 0.5
    count = blocks[0].shape[0]
    held("src")
    for at in range(0, out_ref.shape[0], BLOCK):
        cut = slice(at, at + BLOCK)
        hidden = None
        for which in range(src_ref.shape[0]):
            columns = place_columns(src_ref[which:which + 1, cut], 1, len(blocks), count)
            more = half_silu(base_ref[which, cut, :] + mm(pick_matrix(columns, table.shape[0]), table))
            hidden = more if hidden is None else hidden + more
        update = norm(mm(hidden.astype(BF), held("w")[...]))
        out_ref[cut, :] = (held("grid")[cut, :].astype(F32) + update).astype(BF)


def call(kernel, name, out, specs, args, scratch=(), flops=0, limit=24, outs=None, copies=0):
    if scratch:
        scratch = list(scratch) + [pltpu.SemaphoreType.DMA((16,))]
    if copies:
        scratch.append(pltpu.SemaphoreType.DMA((copies,)))
    args = [pltpu.with_memory_space_constraint(a, pltpu.HBM) if s is HB else a for s, a in zip(specs, args)]
    return pl.pallas_call(
        kernel,
        out_shape=out,
        in_specs=specs,
        out_specs=jax.tree.map(lambda _: VM, out) if outs is None else tuple(outs),
        scratch_shapes=scratch,
        compiler_params=pltpu.CompilerParams(vmem_limit_bytes=limit * MIB),
        cost_estimate=pl.CostEstimate(flops=flops, bytes_accessed=4 * MIB, transcendentals=0),
        name=name,
    )(*args)


def strip_shift(value, by):
    length = lax.axis_size("grid")
    pairs = [(i, i + by) for i in range(length) if 0 <= i + by < length]
    return lax.ppermute(value, "grid", pairs)


def exchange(blocks):
    length = len(blocks)
    moved = [blocks[0]]
    for dz in range(1, length):
        moved.append(lax.ppermute(blocks[dz], "mesh", [(i, (i + dz) % length) for i in range(length)]))
    return moved


def shards(
    grid_latent,
    mesh_latent,
    enc_source,
    enc_slot,
    enc_geometry,
    edge_count,
    slot_row,
    halo_rows,
    proc_source,
    proc_target,
    proc_geometry,
    return_rows,
    dec_source,
    dec_geometry,
    enc_weights,
    enc_lift,
    proc_weights,
    proc_lift,
    dec_weights,
    dec_lift,
):
    nodes, width = grid_latent.shape
    mesh_rows = mesh_latent.shape[0]
    n_mesh = lax.axis_size("mesh")
    count = slot_row.shape[3]
    edges, links = enc_source.shape[0], proc_source.shape[0]
    near_of = dec_source.shape[1]
    shape = jax.ShapeDtypeStruct
    block = shape((count, width), BF)
    row = shape((mesh_rows, width), BF)
    square = pltpu.VMEM((width, width), BF)
    lifts = pltpu.VMEM(enc_lift.shape, F32)
    message, slot, above, *far = call(
        encode_kernel, "encode", (shape((edges, width), BF), shape((1, edges), jnp.int32), shape((2, n_mesh, count), jnp.int32)) + (block,) * n_mesh,
        [SM] + [HB] * 8,
        (edge_count, grid_latent, enc_source.reshape(-1, 128), enc_slot.reshape(-1, 128), enc_geometry, enc_weights, enc_lift, slot_row[0], return_rows[0]),
        [pltpu.VMEM((nodes, width), BF), pltpu.VMEM((edges // 128, 128), jnp.int32), pltpu.VMEM((edges // 128, 128), jnp.int32),
         pltpu.VMEM((4, edges), F32), square, square, lifts, pltpu.VMEM((nodes, width), BF)],
        flops=5 * 10**9,
    )
    above = strip_shift(above, -1)
    far = exchange(far)
    near = call(near_kernel, "near", (block,) * n_mesh, [VM] * 2, (message, slot), flops=10**9)
    half = shape((mesh_rows // 2, width), BF)
    up = call(far_kernel, "far", (half, half), [VM] * (n_mesh + 1) + [ANY], (*far, above, near[0]), flops=10**8)
    near = exchange(near)
    cut = mesh_rows // 2
    up = [strip_shift(up[0], 1), strip_shift(up[1], 1)]
    halo = halo_rows.reshape(1, -1)
    sends = shape((halo.shape[1], width), BF)
    latent, sender, sent = call(
        first_kernel, "first", (row, row, sends), [VM] * (n_mesh + 4) + [HB] * 3,
        (*near, *up, slot_row[0], halo, mesh_latent, enc_weights, proc_weights),
        [pltpu.VMEM((mesh_rows, width), BF)] + [square] * 4, flops=10**9,
    )
    layers = proc_weights.shape[0]
    index = shape((links // 128, 128), jnp.int32)
    for layer in range(layers):
        came = lax.all_to_all(
            sent.reshape(lax.axis_size("grid") * n_mesh, -1, width), ("grid", "mesh"), split_axis=0, concat_axis=0, tiled=True
        ).reshape(sent.shape)
        base, own, src, tgt = call(
            functools.partial(before_kernel, layer=layer), "before",
            (pltpu.HBM((links, width), F32), shape((mesh_rows, width), F32), index, index), [VM] * 2 + [HB] * 5,
            (latent, sender, proc_source.reshape(-1, 128), proc_target.reshape(-1, 128), proc_geometry, proc_lift, proc_weights),
            [pltpu.VMEM((4, links), F32), lifts, square, square, pltpu.VMEM((links, width), F32)],
            flops=10**9, outs=[HB, VM, VM, VM], copies=links // BLOCK,
        )
        last = layer + 1 == layers
        out = call(
            functools.partial(layer_kernel, layer=layer, last=last), "layer",
            (row, row) + ((block,) * n_mesh if last else (sends,)), [VM, VM, HB, VM, VM, VM, VM, HB, HB],
            (latent, came, base, own, src, tgt, return_rows[0] if last else halo, proc_weights,
             dec_weights if last else proc_weights),
            [pltpu.VMEM((links, width), BF)] + [square] * 4 + [pltpu.VMEM((links, width), F32)], flops=4 * 10**9,
            copies=links // BLOCK,
        )
        if last:
            latent, proj, *back = out
        else:
            latent, sender, sent = out
    proj = strip_shift(proj, -1)
    back = exchange(back)
    ahead = exchange(call(spread_kernel, "spread", (block,) * n_mesh, [VM] * 2, (proj, above), flops=10**8))
    sources = dec_source.T
    base = call(
        decode_near_kernel, "decode_near", shape((near_of, nodes, width), F32), [VM] * n_mesh + [HB] * 5,
        (*back, grid_latent, sources, dec_geometry.transpose(1, 0, 2), dec_lift, dec_weights),
        [pltpu.VMEM((nodes, width), BF), pltpu.VMEM((near_of, nodes), jnp.int32), pltpu.VMEM((near_of, 4, nodes), F32),
         lifts, square, pltpu.VMEM((nodes, width), F32)],
        flops=3 * 10**9,
    )
    grid_out = call(
        decode_kernel, "decode", shape(grid_latent.shape, BF), [VM] * (n_mesh + 1) + [HB] * 3,
        (*ahead, base, grid_latent, sources, dec_weights),
        [pltpu.VMEM((nodes, width), BF), pltpu.VMEM((near_of, nodes), jnp.int32), square],
        flops=3 * 10**9,
    )
    return (grid_out, latent)


def solution(mesh):
    placed = (
        P(("grid", "mesh"), None),
        P(("grid", "mesh"), None),
        P(("grid", "mesh")),
        P(("grid", "mesh")),
        P(None, ("grid", "mesh")),
        P(("grid", "mesh")),
        P(("grid", "mesh"), None, None, None),
        P(("grid", "mesh"), None, None),
        P(("grid", "mesh")),
        P(("grid", "mesh")),
        P(None, ("grid", "mesh")),
        P(("grid", "mesh"), None, None, None),
        P(("grid", "mesh"), None),
        P(None, None, ("grid", "mesh")),
        P(),
        P(),
        P(),
        P(),
        P(),
        P(),
    )
    return jax.shard_map(
        shards,
        mesh=mesh,
        in_specs=placed,
        out_specs=(P(("grid", "mesh"), None), P(("grid", "mesh"), None)),
        check_vma=False,
    )
```

profile of v0, /device:TPU:1, one launch (start us, length us, event | category | flops | bytes accessed | tf_op | source)
XLA Modules:
  0.0 130.7 jit_solution(17828074489198896783)
XLA Ops:
  1.3 8.4 %encode.1 = (bf16[2048,512]{1,0:T(8,128)(2,1)S(1)}, s32[1,2048]{1,0:T(1,128)S(1)}, s32[2,4,128]{2,1,0:T(4,128)S(1)}, bf16[128,512]{1,0:T(8,128)(2,1)S(1)}, bf16[...) custom-call(s32[1]{0:T(128)S(6)} %copy.24.count_ref, ...), custom_call_target="tpu_custom_call" | custom-call | flops 5000000000 | bytes 4194304 | tf_op jit(solution)/shard_map/encode/pallas_call | solution.py:329
  9.7 2.5 %collective-permute-start.3 = (bf16[128,512]{1,0:T(8,128)(2,1)S(1)}, bf16[128,512]{1,0:T(8,128)(2,1)S(1)}, u32[]{:S(2)}, u32[]{:S(2)}) collective-permute-start(bf16[128,512]{1,0:T(8,128)(2,1)S(1)} %get-tuple-element.46), channel_id=1, source_target_pairs={{0,1},{1,2},{2,3},{3,0},{4,5},{5,6},{6,7},{7,4},{8,9},{9,10},{10,1... | collective-permute-start | bytes 393224 | tf_op jit(solution)/shard_map/ppermute | solution.py:351
  12.2 2.8 %collective-permute-start.6 = (s32[2,4,128]{2,1,0:T(4,128)S(1)}, s32[2,4,128]{2,1,0:T(4,128)S(1)}, u32[]{:S(2)}, u32[]{:S(2)}) collective-permute-start(s32[2,4,128]{2,1,0:T(4,128)S(1)} %get-tuple-element.49), channel_id=1, source_target_pairs={{4,0},{8,4},{12,8},{16,12},{20,16},{24,20},{28,24},{32,28},{36,32}... | collective-permute-start | bytes 12296 | tf_op jit(solution)/shard_map/ppermute | solution.py:344
  15.1 3.4 %collective-permute-start.4 = (bf16[128,512]{1,0:T(8,128)(2,1)S(1)}, bf16[128,512]{1,0:T(8,128)(2,1)S(1)}, u32[]{:S(2)}, u32[]{:S(2)}) collective-permute-start(bf16[128,512]{1,0:T(8,128)(2,1)S(1)} %get-tuple-element.47), channel_id=1, source_target_pairs={{0,2},{1,3},{2,0},{3,1},{4,6},{5,7},{6,4},{7,5},{8,10},{9,11},{10,... | collective-permute-start | bytes 393224 | tf_op jit(solution)/shard_map/ppermute | solution.py:351
  18.5 0.7 collective-permute-start.5
  19.2 1.2 near.1
  20.4 0.8 collective-permute-start
  21.7 2.0 %collective-permute-start.2 = (bf16[128,512]{1,0:T(8,128)(2,1)S(1)}, bf16[128,512]{1,0:T(8,128)(2,1)S(1)}, u32[]{:S(2)}, u32[]{:S(2)}) collective-permute-start(bf16[128,512]{1,0:T(8,128)(2,1)S(1)} %get-tuple-element.44), channel_id=1, source_target_pairs={{0,3},{1,0},{2,1},{3,2},{4,7},{5,4},{6,5},{7,6},{8,11},{9,8},{10,9... | collective-permute-start | bytes 393224 | tf_op jit(solution)/shard_map/ppermute | solution.py:351
  24.4 3.8 %collective-permute-start.7 = (bf16[80,512]{1,0:T(8,128)(2,1)S(1)}, bf16[80,512]{1,0:T(8,128)(2,1)S(1)}, u32[]{:S(2)}, u32[]{:S(2)}) collective-permute-start(bf16[80,512]{1,0:T(8,128)(2,1)S(1)} %get-tuple-element.50), channel_id=1, source_target_pairs={{0,4},{4,8},{8,12},{12,16},{16,20},{20,24},{24,28},{28,32},{32,36}... | collective-permute-start | bytes 245768 | tf_op jit(solution)/shard_map/ppermute | solution.py:344
  28.2 1.9 %collective-permute-start.8 = (bf16[80,512]{1,0:T(8,128)(2,1)S(1)}, bf16[80,512]{1,0:T(8,128)(2,1)S(1)}, u32[]{:S(2)}, u32[]{:S(2)}) collective-permute-start(bf16[80,512]{1,0:T(8,128)(2,1)S(1)} %get-tuple-element.51), channel_id=1, source_target_pairs={{0,4},{4,8},{8,12},{12,16},{16,20},{20,24},{24,28},{28,32},{32,36}... | collective-permute-start | bytes 245768 | tf_op jit(solution)/shard_map/ppermute | solution.py:344
  30.4 1.2 collective-permute-done.8.refs_5_
  31.6 4.0 %first.1 = (bf16[160,512]{1,0:T(8,128)(2,1)S(1)}, bf16[160,512]{1,0:T(8,128)(2,1)S(1)}, bf16[1024,512]{1,0:T(8,128)(2,1)}) custom-call(bf16[128,512]{1,0:T(8,128)(2,1)S(1)} %get-tuple-element.41.refs_5_.refs_0_, bf16[128,512]{1,0:T(8,128)(2,1)S(1)} %collective-permute-done.refs_1_, bf16[128,512]{1,0:T(8,128)(2,1)S(1)} %collective-permute-done.1.refs_2_, ...), custom_call_target="tpu_custom_call" | custom-call | flops 1000000000 | bytes 4194304 | tf_op jit(solution)/shard_map/first/pallas_call | solution.py:329
  35.7 11.8 %all-to-all-start = ((bf16[128,8,512]{2,1,0:T(8,128)(2,1)}), bf16[128,8,512]{2,1,0:T(8,128)(2,1)S(1)}, u32[]{:S(2)}, u32[]{:S(2)}) async-start(bf16[128,8,512]{2,1,0:T(8,128)(2,1)} %bitcast.4), calls=%async_computation | async-start | bytes 2097152 | tf_op jit(solution)/shard_map/all_to_all | solution.py:414
  47.5 3.5 %before.2 = (f32[1280,512]{1,0:T(8,128)}, f32[160,512]{1,0:T(8,128)S(1)}, s32[10,128]{1,0:T(8,128)S(1)}, s32[10,128]{1,0:T(8,128)S(1)}) custom-call(bf16[160,512]{1,0:T(8,128)(2,1)S(1)} %get-tuple-element.52.latent_ref, bf16[160,512]{1,0:T(8,128)(2,1)S(1)} %get-tuple-element.54.sender_ref, s32[10,128]{1,0:T(8,128)} %bitcast.18, s32[10,128]{1,0:T(8,128)} %bitcast.20, ...), custom_call_target="tpu_custom_call" | custom-call | flops 1000000000 | bytes 4194304 | tf_op jit(solution)/shard_map/before/pallas_call | solution.py:329
  51.1 16.0 %all-to-all-done = bf16[128,8,512]{2,1,0:T(8,128)(2,1)S(1)} async-done(((bf16[128,8,512]{2,1,0:T(8,128)(2,1)}), bf16[128,8,512]{2,1,0:T(8,128)(2,1)S(1)}, u32[]{:S(2)}, u32[]{:S(2)}) %all-to-all-start) | async-done | bytes 1048608 | tf_op jit(solution)/shard_map/all_to_all | solution.py:414
  67.1 8.3 %layer.2 = (bf16[160,512]{1,0:T(8,128)(2,1)S(1)}, bf16[160,512]{1,0:T(8,128)(2,1)S(1)}, bf16[1024,512]{1,0:T(8,128)(2,1)}) custom-call(bf16[160,512]{1,0:T(8,128)(2,1)S(1)} %get-tuple-element.52.latent_ref, bf16[1024,512]{1,0:T(8,128)(2,1)S(1)} %bitcast.12, f32[1280,512]{1,0:T(8,128)} %get-tuple-element.55.base_hbm, ...), custom_call_target="tpu_custom_call" | custom-call | flops 4000000000 | bytes 4194304 | tf_op jit(solution)/shard_map/layer/pallas_call | solution.py:329
  75.4 3.9 %all-to-all-start.1 = ((bf16[128,8,512]{2,1,0:T(8,128)(2,1)}), bf16[128,8,512]{2,1,0:T(8,128)(2,1)S(1)}, u32[]{:S(2)}, u32[]{:S(2)}) async-start(bf16[128,8,512]{2,1,0:T(8,128)(2,1)} %bitcast.8), calls=%async_computation.1 | async-start | bytes 2097152 | tf_op jit(solution)/shard_map/all_to_all | solution.py:414
  79.3 3.5 %before.3 = (f32[1280,512]{1,0:T(8,128)}, f32[160,512]{1,0:T(8,128)S(1)}, s32[10,128]{1,0:T(8,128)S(1)}, s32[10,128]{1,0:T(8,128)S(1)}) custom-call(bf16[160,512]{1,0:T(8,128)(2,1)S(1)} %get-tuple-element.59.latent_ref, bf16[160,512]{1,0:T(8,128)(2,1)S(1)} %get-tuple-element.61.sender_ref, s32[10,128]{1,0:T(8,128)} %bitcast.19, s32[10,128]{1,0:T(8,128)} %bitcast.21, ...), custom_call_target="tpu_custom_call" | custom-call | flops 1000000000 | bytes 4194304 | tf_op jit(solution)/shard_map/before/pallas_call | solution.py:329
  82.8 16.1 %all-to-all-done.1 = bf16[128,8,512]{2,1,0:T(8,128)(2,1)S(1)} async-done(((bf16[128,8,512]{2,1,0:T(8,128)(2,1)}), bf16[128,8,512]{2,1,0:T(8,128)(2,1)S(1)}, u32[]{:S(2)}, u32[]{:S(2)}) %all-to-all-start.1) | async-done | bytes 1048608 | tf_op jit(solution)/shard_map/all_to_all | solution.py:414
  99.0 7.7 %layer.3 = (bf16[160,512]{1,0:T(8,128)(2,1)}, bf16[160,512]{1,0:T(8,128)(2,1)S(1)}, bf16[128,512]{1,0:T(8,128)(2,1)S(1)}, bf16[128,512]{1,0:T(8,128)(2,1)S(1)}, ...) custom-call(bf16[160,512]{1,0:T(8,128)(2,1)S(1)} %get-tuple-element.59.latent_ref, ...), custom_call_target="tpu_custom_call" | custom-call | flops 4000000000 | bytes 4194304 | tf_op jit(solution)/shard_map/layer/pallas_call | solution.py:329
  106.7 2.3 %collective-permute-start.9 = (bf16[160,512]{1,0:T(8,128)(2,1)S(1)}, bf16[160,512]{1,0:T(8,128)(2,1)S(1)}, u32[]{:S(2)}, u32[]{:S(2)}) collective-permute-start(bf16[160,512]{1,0:T(8,128)(2,1)S(1)} %get-tuple-element.66), channel_id=1, source_target_pairs={{4,0},{8,4},{12,8},{16,12},{20,16},{24,20},{28,24},{32,28},{36,32}... | collective-permute-start | bytes 491528 | tf_op jit(solution)/shard_map/ppermute | solution.py:344
  109.0 0.6 collective-permute-start.13
  109.6 1.5 %collective-permute-start.14 = (bf16[128,512]{1,0:T(8,128)(2,1)S(1)}, bf16[128,512]{1,0:T(8,128)(2,1)S(1)}, u32[]{:S(2)}, u32[]{:S(2)}) collective-permute-start(bf16[128,512]{1,0:T(8,128)(2,1)S(1)} %get-tuple-element.73), channel_id=1, source_target_pairs={{0,2},{1,3},{2,0},{3,1},{4,6},{5,7},{6,4},{7,5},{8,10},{9,11},{10,... | collective-permute-start | bytes 393224 | tf_op jit(solution)/shard_map/ppermute | solution.py:351
  111.1 1.0 collective-permute-start.15
  112.1 1.5 %collective-permute-done.9.table_ref = bf16[160,512]{1,0:T(8,128)(2,1)S(1)} collective-permute-done((bf16[160,512]{1,0:T(8,128)(2,1)S(1)}, bf16[160,512]{1,0:T(8,128)(2,1)S(1)}, u32[]{:S(2)}, u32[]{:S(2)}) %collective-permute-start.9) | collective-permute-done | bytes 163872 | tf_op jit(solution)/shard_map/ppermute | solution.py:344
  114.0 0.6 collective-permute-start.10
  114.6 1.1 collective-permute-start.11
  115.7 2.9 %collective-permute-done.13.refs_1_ = bf16[128,512]{1,0:T(8,128)(2,1)S(1)} collective-permute-done((bf16[128,512]{1,0:T(8,128)(2,1)S(1)}, bf16[128,512]{1,0:T(8,128)(2,1)S(1)}, u32[]{:S(2)}, u32[]{:S(2)}) %collective-permute-start.13) | collective-permute-done | bytes 131104 | tf_op jit(solution)/shard_map/ppermute | solution.py:351
  118.6 0.5 collective-permute-done.15.refs_3_
  119.1 4.9 %decode_near.1.refs_4_ = f32[3,1024,512]{2,1,0:T(8,128)S(1)} custom-call(bf16[128,512]{1,0:T(8,128)(2,1)S(1)} %get-tuple-element.71.refs_0_, bf16[128,512]{1,0:T(8,128)(2,1)S(1)} %collective-permute-done.13.refs_1_, bf16[128,512]{1,0:T(8,128)(2,1)S(1)} %collective-permute-done.14.refs_2_, bf16[128,512]{1,0:T(8,128)(2,1)S(1)} %collective-permute-done.15.refs_3_, ...), custom_call_target="tpu_custom_call" | custom-call | flops 3000000000 | bytes 4194304 | tf_op jit(solution)/shard_map/decode_near/pallas_call | solution.py:329
  124.1 0.7 collective-permute-done.12.refs_3_
  124.8 5.8 %decode.1 = bf16[1024,512]{1,0:T(8,128)(2,1)} custom-call(bf16[128,512]{1,0:T(8,128)(2,1)S(1)} %get-tuple-element.67.refs_0_, bf16[128,512]{1,0:T(8,128)(2,1)S(1)} %collective-permute-done.10.refs_1_, bf16[128,512]{1,0:T(8,128)(2,1)S(1)} %collective-permute-done.11.refs_2_, bf16[128,512]{1,0:T(8,128)(2,1)S(1)} %collective-permute-done.12.refs_3_, ...), custom_call_target="tpu_custom_call" | custom-call | flops 3000000000 | bytes 4194304 | tf_op jit(solution)/shard_map/decode/pallas_call | solution.py:329
  (23 shorter events, 1.7 us)
Async XLA Ops:
  9.7 20.5 %copy-start.2 = (s32[1,128,8]{1,2,0:T(8,128)S(1)}, s32[1,128,8]{1,2,0:T(8,128)}, u32[]{:S(2)}) copy-start(s32[1,128,8]{1,2,0:T(8,128)} %param.27) | copy-start | bytes 12292
  9.7 22.0 %copy-start = (s32[1,2,4,128]{3,2,1,0:T(4,128)S(1)}, s32[1,2,4,128]{3,2,1,0:T(4,128)}, u32[]{:S(2)}) copy-start(s32[1,2,4,128]{3,2,1,0:T(4,128)} %param.26) | copy-start | bytes 12292
  9.7 12.0 %collective-permute-start.3 = (bf16[128,512]{1,0:T(8,128)(2,1)S(1)}, bf16[128,512]{1,0:T(8,128)(2,1)S(1)}, u32[]{:S(2)}, u32[]{:S(2)}) collective-permute-start(bf16[128,512]{1,0:T(8,128)(2,1)S(1)} %get-tuple-element.46), channel_id=1, source_target_pairs={{0,1},{1,2},{2,3},{3,0},{4,5},{5,6},{6,7},{7,4},{8,9},{9,10},{10,1... | collective-permute-start | bytes 393224 | tf_op jit(solution)/shard_map/ppermute | solution.py:351
  12.2 9.0 %collective-permute-start.6 = (s32[2,4,128]{2,1,0:T(4,128)S(1)}, s32[2,4,128]{2,1,0:T(4,128)S(1)}, u32[]{:S(2)}, u32[]{:S(2)}) collective-permute-start(s32[2,4,128]{2,1,0:T(4,128)S(1)} %get-tuple-element.49), channel_id=1, source_target_pairs={{4,0},{8,4},{12,8},{16,12},{20,16},{24,20},{28,24},{32,28},{36,32}... | collective-permute-start | bytes 12296 | tf_op jit(solution)/shard_map/ppermute | solution.py:344
  15.1 8.7 %collective-permute-start.4 = (bf16[128,512]{1,0:T(8,128)(2,1)S(1)}, bf16[128,512]{1,0:T(8,128)(2,1)S(1)}, u32[]{:S(2)}, u32[]{:S(2)}) collective-permute-start(bf16[128,512]{1,0:T(8,128)(2,1)S(1)} %get-tuple-element.47), channel_id=1, source_target_pairs={{0,2},{1,3},{2,0},{3,1},{4,6},{5,7},{6,4},{7,5},{8,10},{9,11},{10,... | collective-permute-start | bytes 393224 | tf_op jit(solution)/shard_map/ppermute | solution.py:351
  18.5 5.7 %collective-permute-start.5 = (bf16[128,512]{1,0:T(8,128)(2,1)S(1)}, bf16[128,512]{1,0:T(8,128)(2,1)S(1)}, u32[]{:S(2)}, u32[]{:S(2)}) collective-permute-start(bf16[128,512]{1,0:T(8,128)(2,1)S(1)} %get-tuple-element.48), channel_id=1, source_target_pairs={{0,3},{1,0},{2,1},{3,2},{4,7},{5,4},{6,5},{7,6},{8,11},{9,8},{10,9... | collective-permute-start | bytes 393224 | tf_op jit(solution)/shard_map/ppermute | solution.py:351
  20.4 9.9 %collective-permute-start = (bf16[128,512]{1,0:T(8,128)(2,1)S(1)}, bf16[128,512]{1,0:T(8,128)(2,1)S(1)}, u32[]{:S(2)}, u32[]{:S(2)}) collective-permute-start(bf16[128,512]{1,0:T(8,128)(2,1)S(1)} %get-tuple-element.42), channel_id=1, source_target_pairs={{0,1},{1,2},{2,3},{3,0},{4,5},{5,6},{6,7},{7,4},{8,9},{9,10},{10,1... | collective-permute-start | bytes 393224 | tf_op jit(solution)/shard_map/ppermute | solution.py:351
  21.3 9.1 %collective-permute-start.1 = (bf16[128,512]{1,0:T(8,128)(2,1)S(1)}, bf16[128,512]{1,0:T(8,128)(2,1)S(1)}, u32[]{:S(2)}, u32[]{:S(2)}) collective-permute-start(bf16[128,512]{1,0:T(8,128)(2,1)S(1)} %get-tuple-element.43), channel_id=1, source_target_pairs={{0,2},{1,3},{2,0},{3,1},{4,6},{5,7},{6,4},{7,5},{8,10},{9,11},{10,... | collective-permute-start | bytes 393224 | tf_op jit(solution)/shard_map/ppermute | solution.py:351
  21.7 8.7 %collective-permute-start.2 = (bf16[128,512]{1,0:T(8,128)(2,1)S(1)}, bf16[128,512]{1,0:T(8,128)(2,1)S(1)}, u32[]{:S(2)}, u32[]{:S(2)}) collective-permute-start(bf16[128,512]{1,0:T(8,128)(2,1)S(1)} %get-tuple-element.44), channel_id=1, source_target_pairs={{0,3},{1,0},{2,1},{3,2},{4,7},{5,4},{6,5},{7,6},{8,11},{9,8},{10,9... | collective-permute-start | bytes 393224 | tf_op jit(solution)/shard_map/ppermute | solution.py:351
  24.4 6.0 %collective-permute-start.7 = (bf16[80,512]{1,0:T(8,128)(2,1)S(1)}, bf16[80,512]{1,0:T(8,128)(2,1)S(1)}, u32[]{:S(2)}, u32[]{:S(2)}) collective-permute-start(bf16[80,512]{1,0:T(8,128)(2,1)S(1)} %get-tuple-element.50), channel_id=1, source_target_pairs={{0,4},{4,8},{8,12},{12,16},{16,20},{20,24},{24,28},{28,32},{32,36}... | collective-permute-start | bytes 245768 | tf_op jit(solution)/shard_map/ppermute | solution.py:344
  28.2 3.4 %collective-permute-start.8 = (bf16[80,512]{1,0:T(8,128)(2,1)S(1)}, bf16[80,512]{1,0:T(8,128)(2,1)S(1)}, u32[]{:S(2)}, u32[]{:S(2)}) collective-permute-start(bf16[80,512]{1,0:T(8,128)(2,1)S(1)} %get-tuple-element.51), channel_id=1, source_target_pairs={{0,4},{4,8},{8,12},{12,16},{16,20},{20,24},{24,28},{28,32},{32,36}... | collective-permute-start | bytes 245768 | tf_op jit(solution)/shard_map/ppermute | solution.py:344
  35.7 31.4 %all-to-all-start = ((bf16[128,8,512]{2,1,0:T(8,128)(2,1)}), bf16[128,8,512]{2,1,0:T(8,128)(2,1)S(1)}, u32[]{:S(2)}, u32[]{:S(2)}) async-start(bf16[128,8,512]{2,1,0:T(8,128)(2,1)} %bitcast.4), calls=%async_computation | async-start | bytes 2097152 | tf_op jit(solution)/shard_map/all_to_all | solution.py:414
  75.4 23.6 %all-to-all-start.1 = ((bf16[128,8,512]{2,1,0:T(8,128)(2,1)}), bf16[128,8,512]{2,1,0:T(8,128)(2,1)S(1)}, u32[]{:S(2)}, u32[]{:S(2)}) async-start(bf16[128,8,512]{2,1,0:T(8,128)(2,1)} %bitcast.8), calls=%async_computation.1 | async-start | bytes 2097152 | tf_op jit(solution)/shard_map/all_to_all | solution.py:414
  79.3 19.7 %copy-start.1 = (s32[1,2,4,128]{3,2,1,0:T(4,128)S(1)}, s32[1,2,4,128]{3,2,1,0:T(4,128)}, u32[]{:S(2)}) copy-start(s32[1,2,4,128]{3,2,1,0:T(4,128)} %param.31) | copy-start | bytes 12292
  106.7 6.9 %collective-permute-start.9 = (bf16[160,512]{1,0:T(8,128)(2,1)S(1)}, bf16[160,512]{1,0:T(8,128)(2,1)S(1)}, u32[]{:S(2)}, u32[]{:S(2)}) collective-permute-start(bf16[160,512]{1,0:T(8,128)(2,1)S(1)} %get-tuple-element.66), channel_id=1, source_target_pairs={{4,0},{8,4},{12,8},{16,12},{20,16},{24,20},{28,24},{32,28},{36,32}... | collective-permute-start | bytes 491528 | tf_op jit(solution)/shard_map/ppermute | solution.py:344
  109.0 9.6 %collective-permute-start.13 = (bf16[128,512]{1,0:T(8,128)(2,1)S(1)}, bf16[128,512]{1,0:T(8,128)(2,1)S(1)}, u32[]{:S(2)}, u32[]{:S(2)}) collective-permute-start(bf16[128,512]{1,0:T(8,128)(2,1)S(1)} %get-tuple-element.72), channel_id=1, source_target_pairs={{0,1},{1,2},{2,3},{3,0},{4,5},{5,6},{6,7},{7,4},{8,9},{9,10},{10,1... | collective-permute-start | bytes 393224 | tf_op jit(solution)/shard_map/ppermute | solution.py:351
  109.6 9.0 %collective-permute-start.14 = (bf16[128,512]{1,0:T(8,128)(2,1)S(1)}, bf16[128,512]{1,0:T(8,128)(2,1)S(1)}, u32[]{:S(2)}, u32[]{:S(2)}) collective-permute-start(bf16[128,512]{1,0:T(8,128)(2,1)S(1)} %get-tuple-element.73), channel_id=1, source_target_pairs={{0,2},{1,3},{2,0},{3,1},{4,6},{5,7},{6,4},{7,5},{8,10},{9,11},{10,... | collective-permute-start | bytes 393224 | tf_op jit(solution)/shard_map/ppermute | solution.py:351
  111.1 8.0 %collective-permute-start.15 = (bf16[128,512]{1,0:T(8,128)(2,1)S(1)}, bf16[128,512]{1,0:T(8,128)(2,1)S(1)}, u32[]{:S(2)}, u32[]{:S(2)}) collective-permute-start(bf16[128,512]{1,0:T(8,128)(2,1)S(1)} %get-tuple-element.74), channel_id=1, source_target_pairs={{0,3},{1,0},{2,1},{3,2},{4,7},{5,4},{6,5},{7,6},{8,11},{9,8},{10,9... | collective-permute-start | bytes 393224 | tf_op jit(solution)/shard_map/ppermute | solution.py:351
  114.0 10.1 %collective-permute-start.10 = (bf16[128,512]{1,0:T(8,128)(2,1)S(1)}, bf16[128,512]{1,0:T(8,128)(2,1)S(1)}, u32[]{:S(2)}, u32[]{:S(2)}) collective-permute-start(bf16[128,512]{1,0:T(8,128)(2,1)S(1)} %get-tuple-element.68), channel_id=1, source_target_pairs={{0,1},{1,2},{2,3},{3,0},{4,5},{5,6},{6,7},{7,4},{8,9},{9,10},{10,1... | collective-permute-start | bytes 393224 | tf_op jit(solution)/shard_map/ppermute | solution.py:351
  114.6 9.5 %collective-permute-start.11 = (bf16[128,512]{1,0:T(8,128)(2,1)S(1)}, bf16[128,512]{1,0:T(8,128)(2,1)S(1)}, u32[]{:S(2)}, u32[]{:S(2)}) collective-permute-start(bf16[128,512]{1,0:T(8,128)(2,1)S(1)} %get-tuple-element.69), channel_id=1, source_target_pairs={{0,2},{1,3},{2,0},{3,1},{4,6},{5,7},{6,4},{7,5},{8,10},{9,11},{10,... | collective-permute-start | bytes 393224 | tf_op jit(solution)/shard_map/ppermute | solution.py:351
  118.6 6.1 %collective-permute-start.12 = (bf16[128,512]{1,0:T(8,128)(2,1)S(1)}, bf16[128,512]{1,0:T(8,128)(2,1)S(1)}, u32[]{:S(2)}, u32[]{:S(2)}) collective-permute-start(bf16[128,512]{1,0:T(8,128)(2,1)S(1)} %get-tuple-element.70), channel_id=1, source_target_pairs={{0,3},{1,0},{2,1},{3,2},{4,7},{5,4},{6,5},{7,6},{8,11},{9,8},{10,9... | collective-permute-start | bytes 393224 | tf_op jit(solution)/shard_map/ppermute | solution.py:351
where the time goes:
time: 131 us
  Pallas kernels  48.1 us (37%)
  starting transfers between devices  41.3 us (32%)
  waiting for transfers between devices  39.4 us (30%)
  between operations  1.67 us (1%)
    pallas_call x11, Pallas kernels, call(): pl.pallas_call(kernel, out_shape=out, in_specs=specs, out_specs=jax.tree....  48.1 us
    all_to_all x2, waiting for transfers between devices, shards(): lax.all_to_all(sent.reshape(lax.axis_size('grid') * n_mesh, -1, width), (...  32.2 us
    all_to_all x2, starting transfers between devices, shards(): lax.all_to_all(sent.reshape(lax.axis_size('grid') * n_mesh, -1, width), (...  15.7 us
    ppermute x12, starting transfers between devices, exchange(): lax.ppermute(blocks[dz], 'mesh', [(i, (i + dz) % length) for i in range(l...  14.8 us
    ppermute x4, starting transfers between devices, strip_shift(): return lax.ppermute(value, 'grid', pairs)  10.9 us
    ppermute x12, waiting for transfers between devices, exchange(): lax.ppermute(blocks[dz], 'mesh', [(i, (i + dz) % length) for i in range(l...  4.49 us
    ppermute x4, waiting for transfers between devices, strip_shift(): return lax.ppermute(value, 'grid', pairs)  2.73 us
  transfers between devices with their start and end apart: 18, of which 8 were waited for; matrix products, arithmetic and copies ran while one was open for 0% of the time, Pallas kernels for 11%

commit v1 on v0

v1 whole, which is shorter than its diff:
```python
import functools

import jax
import jax.numpy as jnp
from jax import lax
from jax.experimental import pallas as pl
from jax.experimental.pallas import tpu as pltpu
from jax.sharding import PartitionSpec as P

BF = jnp.bfloat16
F32 = jnp.float32
VM = pl.BlockSpec(memory_space=pltpu.VMEM)
SM = pl.BlockSpec(memory_space=pltpu.SMEM)
HB = pl.BlockSpec(memory_space=pltpu.HBM)
ANY = pl.BlockSpec(memory_space=pl.ANY)
MIB = 1024 * 1024
BLOCK = 512


def mm(a, b):
    return lax.dot_general(a, b, (((1,), (0,)), ((), ())), preferred_element_type=F32)


def mm_tn(a, b):
    return lax.dot_general(a, b, (((0,), (0,)), ((), ())), preferred_element_type=F32)


def to_columns(row):
    n = row.shape[1]
    parts = [jnp.broadcast_to(row[:, at:at + 128], (128, 128)).T for at in range(0, n, 128)]
    return jnp.concatenate(parts, axis=0) if len(parts) > 1 else parts[0]


def lane_hits(columns, at):
    return columns - jnp.int16(at) == lax.broadcasted_iota(jnp.int16, columns.shape, 1)


def as_ones(hits):
    return jnp.where(hits, jnp.ones(hits.shape, BF), jnp.zeros(hits.shape, BF))


def pick_matrix(columns, width):
    col = columns.astype(jnp.int16)
    return jnp.concatenate([as_ones(lane_hits(col, at)) for at in range(0, width, 128)], axis=1)


def add_matrix(row, height):
    n = row.shape[1]
    wide = jnp.broadcast_to(row, (16, n)).astype(jnp.int16)
    wide = jnp.broadcast_to(wide[None], (height // 16, 16, n)).reshape(height, n)
    return as_ones(wide == lax.broadcasted_iota(jnp.int16, (height, n), 0))


def split3(x):
    a = x.astype(BF).astype(F32)
    r = x - a
    b = r.astype(BF).astype(F32)
    return a, b, r - b


def lift(geometry, right):
    a, b, c = split3(geometry)
    return mm_tn(jnp.concatenate([a, a, b, b, a, c], axis=0).astype(BF), right)


def lift_right(weight):
    a, b, c = split3(weight)
    return jnp.concatenate([a, b, a, b, c, a], axis=0).astype(BF)


def half_silu(half):
    return half + half * jnp.tanh(half)


def centered(weight):
    wide = weight.astype(F32)
    return (wide - jnp.mean(wide, axis=-1, keepdims=True)).astype(BF)


def scaled(v):
    return v * lax.rsqrt(jnp.mean(v * v, axis=-1, keepdims=True) + 1e-05)


def norm(v):
    c = v - jnp.mean(v, axis=-1, keepdims=True)
    return c * lax.rsqrt(jnp.mean(c * c, axis=-1, keepdims=True) + 1e-05)


def node_update(latent, own, total, w_total, w_out):
    inner = own + mm(total.astype(BF), w_total)
    hidden = half_silu(inner * 0.5).astype(BF)
    return (latent.astype(F32) + scaled(mm(hidden, w_out))).astype(BF)


def padded(table, rows):
    return jnp.concatenate([table, jnp.zeros((rows - table.shape[0], table.shape[1]), BF)], axis=0)


def pick_rows(row, table):
    wide = -(-table.shape[0] // 128) * 128
    return mm(pick_matrix(to_columns(row), wide), padded(table, wide)).astype(BF)


def lanes(ref, at, count):
    return jnp.concatenate([ref[r:r + 1, :] for r in range(at // 128, (at + count) // 128)], axis=1)


class Held:
    def __init__(self, sems, **pairs):
        self.copies, self.refs = {}, {}
        for at, (name, (src, dst)) in enumerate(pairs.items()):
            self.refs[name] = dst
            self.copies[name] = pltpu.make_async_copy(src, dst, sems.at[at])
            self.copies[name].start()

    def __call__(self, name):
        if name in self.copies:
            self.copies.pop(name).wait()
        return self.refs[name]


class Sent:
    def __init__(self, sems):
        self.sems, self.copies = sems, []

    def __call__(self, src, dst):
        self.copies.append(pltpu.make_async_copy(src, dst, self.sems.at[len(self.copies)]))
        self.copies[-1].start()

    def wait(self):
        for copy in self.copies:
            copy.wait()


def turned(index, count, me):
    return lax.bitwise_and(index - me, count - 1)


def row_of(rows, at):
    out = None
    for s in range(rows.shape[0]):
        part = jnp.where(at == s, rows[s:s + 1, :], 0)
        out = part if out is None else out + part
    return out


def rows_from(rows, me):
    count = rows.shape[0]
    return jnp.concatenate([row_of(rows, lax.bitwise_and(me - dz, count - 1)) for dz in range(count)], axis=1)


def rows_to(rows, me):
    count = rows.shape[0]
    return jnp.concatenate([row_of(rows, lax.bitwise_and(me + dz, count - 1)) for dz in range(count)], axis=1)


def slot_sums(slot, part, n_mesh, message, outs):
    count = outs[0].shape[0]
    band = n_mesh * count
    me = lax.axis_index("mesh")
    local = slot - part * band
    turn = turned(lax.div(local, count), n_mesh, me) * count + lax.bitwise_and(local, count - 1)
    turn = jnp.where((local >= 0) & (local < band), turn, -1)
    total = mm(add_matrix(turn, band), message)
    for dz in range(n_mesh):
        outs[dz][...] = total[dz * count:(dz + 1) * count].astype(BF)


def encode_kernel(count_ref, grid_hbm, src_hbm, slot_hbm, geo_hbm, w_hbm, lift_hbm, message_ref, slot_out, *rest):
    outs, (grid_ref, src_ref, slot_ref, geo_ref, w0_ref, w1_ref, lift_ref, table_ref, sems) = rest[:4], rest[4:]
    nodes, edges = grid_ref.shape[0], message_ref.shape[0]
    cuts = [slice(at, at + 256) for at in range(0, nodes, 256)]
    held = Held(
        sems, w0=(w_hbm.at[0], w0_ref), **{f"g{i}": (grid_hbm.at[cut, :], grid_ref.at[cut, :]) for i, cut in enumerate(cuts)},
        src=(src_hbm, src_ref), geo=(geo_hbm, geo_ref), lift=(lift_hbm, lift_ref), w1=(w_hbm.at[1], w1_ref),
        slot=(slot_hbm, slot_ref),
    )
    held("w0")
    for i, cut in enumerate(cuts):
        table_ref[cut, :] = (mm(held(f"g{i}")[...], w0_ref[...]) * 0.5).astype(BF)
    held("src"), held("geo"), held("w1")
    right = lift_right(held("lift")[...] * 0.5)
    for at in range(0, edges, BLOCK):
        cut = slice(at, at + BLOCK)
        half = mm(pick_matrix(to_columns(lanes(src_ref, at, BLOCK)), nodes), table_ref[...]) + lift(geo_ref[:, cut], right)
        message_ref[cut, :] = norm(mm(half_silu(half).astype(BF), w1_ref[...])).astype(BF)
    slot = lanes(held("slot"), 0, edges)
    slot = jnp.where(lax.broadcasted_iota(jnp.int32, slot.shape, 1) < count_ref[0], slot, -1)
    slot_out[...] = slot
    slot_sums(slot, 1, len(outs), message_ref[...], outs)


def near_kernel(message_ref, slot_ref, halo_hbm, latent_hbm, w_hbm, next_hbm, *rest):
    outs, (latent_out, own_ref, wb_out, wc_out, wn_out, hot_ref, hot_hbm, halo_ref, wa_ref, wc_ref, sems, out_sems) = rest[:4], rest[4:]
    held = Held(
        sems, halo=(halo_hbm, halo_ref), latent=(latent_hbm, latent_out), wa=(w_hbm.at[2], wa_ref), wc=(w_hbm.at[4], wc_ref),
        wb=(w_hbm.at[3], wb_out), wn=(next_hbm.at[0, 0], wn_out),
    )
    slot_sums(slot_ref[...], 0, len(outs), message_ref[...], outs)
    halo = held("halo")[...].astype(F32).astype(BF)
    places, owners = halo.shape
    row = lax.broadcasted_iota(jnp.int32, (places * owners, 128), 0)
    lane = lax.broadcasted_iota(jnp.int32, row.shape, 1)
    owner = jnp.where(lax.div(row, places) == lane, 1.0, 0.0).astype(BF)
    each = lax.dot_general(owner, halo, (((1,), (1,)), ((), ())), preferred_element_type=F32)
    mine = jnp.where(lax.bitwise_and(row, places - 1)[:, :places] == lane[:, :places], each, 0.0)
    column = jnp.broadcast_to(jnp.sum(mine, axis=1, keepdims=True), row.shape).astype(jnp.int32)
    hot_ref[...] = pick_matrix(column, hot_ref.shape[1])
    sent = Sent(out_sems)
    sent(hot_ref, hot_hbm)
    own_ref[...] = mm(held("latent")[...], held("wa")[...])
    wc_out[...] = centered(held("wc")[...])
    held("wb"), held("wn")
    sent.wait()


def far_kernel(*refs):
    *blocks, rows_ref, _, low_ref, high_ref = refs
    rows = rows_from(rows_ref[1], lax.axis_index("mesh"))
    table = jnp.concatenate([b[...] for b in blocks], axis=0)
    total = mm(add_matrix(rows, 2 * low_ref.shape[0]), table).astype(BF)
    low_ref[...] = total[:low_ref.shape[0]]
    high_ref[...] = total[low_ref.shape[0]:]


def first_kernel(*refs):
    *blocks, low_ref, high_ref, rows_ref, latent_ref, own_ref, wb_ref, wc_ref, wn_ref, hot_ref, out_ref, sender_ref, sent_ref = refs
    rows = rows_from(rows_ref[0], lax.axis_index("mesh"))
    table = jnp.concatenate([b[...] for b in blocks], axis=0)
    total = mm(add_matrix(rows, out_ref.shape[0]), table)
    total = total + jnp.concatenate([low_ref[...], high_ref[...]], axis=0).astype(F32)
    latent = node_update(latent_ref[...], own_ref[...], total, wb_ref[...], wc_ref[...])
    out_ref[...] = latent
    sender = (mm(latent, wn_ref[...]) * 0.5).astype(BF)
    sender_ref[...] = sender
    sent_ref[...] = mm(hot_ref[...], padded(sender, hot_ref.shape[1])).astype(BF)


def before_kernel(latent_ref, sender_ref, src_hbm, tgt_hbm, geo_hbm, lift_hbm, w_hbm, *rest, layer, last):
    if last:
        (grid_hbm, decgeo_hbm, declift_hbm, dec_hbm), rest = rest[:4], rest[4:]
        (*shares, decw_out), rest = rest[:4], rest[4:]
    own_ref, src_ref, tgt_ref, *bases = rest[:5]
    (wc_out, wf_out), rest = rest[5:7], rest[7:]
    if last:
        (grid_ref, decgeo_ref, declift_ref, decv_ref, decw_ref, total_ref, share_ref), rest = rest[:7], rest[7:]
    geo_ref, lift_ref, wb_ref, wd_ref, wc_ref, wf_ref, sems, out_sems = rest
    more = {}
    if last:
        more = dict(
            grid=(grid_hbm, grid_ref), decgeo=(decgeo_hbm, decgeo_ref), declift=(declift_hbm, declift_ref),
            decv=(dec_hbm.at[1], decv_ref), decw=(dec_hbm.at[2], decw_ref),
        )
    held = Held(
        sems, wb=(w_hbm.at[layer, 1], wb_ref), src=(src_hbm, src_ref), tgt=(tgt_hbm, tgt_ref), geo=(geo_hbm, geo_ref),
        lift=(lift_hbm.at[layer], lift_ref), wd=(w_hbm.at[layer, 3], wd_ref), wc=(w_hbm.at[layer, 2], wc_ref),
        wf=(w_hbm.at[layer, 5], wf_ref), **more,
    )
    sent = Sent(out_sems)
    latent = latent_ref[...]
    rows = latent.shape[0]
    target = (mm(latent, held("wb")[...]) * 0.5).astype(BF)
    wide = -(-2 * rows // 128) * 128
    table = padded(jnp.concatenate([sender_ref[...], target], axis=0), wide)
    held("src"), held("tgt"), held("geo")
    right = lift_right(held("lift")[...] * 0.5)
    for part, base_ref in enumerate(bases):
        for at in range(0, base_ref.shape[0], 128):
            near = part * base_ref.shape[0] + at
            src = to_columns(lanes(src_ref, near, 128))
            src_col = jnp.where(src < rows, src, -1).astype(jnp.int16)
            tgt_col = to_columns(lanes(tgt_ref, near, 128) + rows).astype(jnp.int16)
            groups = [as_ones(lane_hits(src_col, lane) | lane_hits(tgt_col, lane)) for lane in range(0, wide, 128)]
            base = mm(jnp.concatenate(groups, axis=1), table) + lift(geo_ref[:, near:near + 128], right)
            base_ref[at:at + 128, :] = base.astype(BF)
    own_ref[...] = mm(latent, held("wd")[...])
    wc_ref[...] = centered(held("wc")[...])
    sent(wc_ref, wc_out)
    wf_ref[...] = centered(held("wf")[...])
    sent(wf_ref, wf_out)
    if last:
        right = lift_right(held("declift")[...] * 0.5)
        total_ref[...] = mm(held("grid")[...], held("decv")[...]) * 0.5
        decw_ref[...] = centered(held("decw")[...])
        sent(decw_ref, decw_out)
        held("decgeo")
        for which, out in enumerate(shares):
            for at in range(0, out.shape[0], 256):
                cut = slice(at, at + 256)
                share_ref[which, cut, :] = (lift(decgeo_ref[which, :, cut], right) + total_ref[cut, :]).astype(BF)
            sent(share_ref.at[which], out)
    sent.wait()


def layer_kernel(latent_ref, came_ref, own_ref, src_ref, tgt_ref, *rest, layer, last):
    (*bases, wc_hbm, wf_hbm, w_hbm, next_hbm, pick_ref, _), rest = rest[:8], rest[8:]
    outs, (message_ref, wc_ref, we_ref, wf_ref, wn_ref, hot_ref, sems) = rest[:-7], rest[-7:]
    more = {} if last else dict(hot=(pick_ref, hot_ref))
    held = Held(
        sems, wc=(wc_hbm, wc_ref), we=(w_hbm.at[layer, 4], we_ref), wf=(wf_hbm, wf_ref),
        wn=(next_hbm.at[0] if last else next_hbm.at[layer + 1, 0], wn_ref), **more,
    )
    rows = latent_ref.shape[0]
    for part, base_ref in enumerate(bases):
        count = base_ref.shape[0]
        hits = pick_matrix(to_columns(lanes(src_ref, part * count, count) - rows), came_ref.shape[0])
        half = mm(hits, came_ref[...]) + base_ref[...].astype(F32)
        message = scaled(mm(half_silu(half).astype(BF), held("wc")[...]))
        message_ref[part * count:(part + 1) * count, :] = message.astype(BF)
    total = mm(add_matrix(lanes(tgt_ref, 0, message_ref.shape[0]), rows), message_ref[...])
    latent = node_update(latent_ref[...], own_ref[...], total, held("we")[...], held("wf")[...])
    outs[0][...] = latent
    onward = mm(latent, held("wn")[...])
    if last:
        onward = onward.astype(BF)
        outs[1][...] = onward
        spread(rows_to(pick_ref[0], lax.axis_index("mesh")), onward, outs[2:])
    else:
        onward = (onward * 0.5).astype(BF)
        outs[1][...] = onward
        outs[2][...] = mm(held("hot")[...], padded(onward, hot_ref.shape[1])).astype(BF)


def spread(row, table, outs):
    picked = pick_rows(row, table)
    count = outs[0].shape[0]
    for dz, out in enumerate(outs):
        out[...] = picked[dz * count:(dz + 1) * count]


def spread_kernel(table_ref, rows_ref, *outs):
    spread(rows_to(rows_ref[1], lax.axis_index("mesh")), table_ref[...], outs)


def place_columns(place, part, n_mesh, count):
    me = lax.axis_index("mesh")
    local = place - part * n_mesh * count
    turn = lax.bitwise_and(me - lax.div(local, count), n_mesh - 1) * count + lax.bitwise_and(local, count - 1)
    return to_columns(jnp.where((local >= 0) & (local < n_mesh * count), turn, -1))


def decode_near_kernel(*refs):
    *blocks, dec0, dec1, dec2, src_hbm, base_ref, hot0, hot1, hot2, src_ref, share_ref, sems = refs
    held = Held(sems, src=(src_hbm, src_ref), **{
        f"d{i}": (dec, share_ref.at[i]) for i, dec in enumerate((dec0, dec1, dec2))
    })
    table = jnp.concatenate([b[...] for b in blocks], axis=0) * 0.5
    count = blocks[0].shape[0]
    held("src")
    for which, hot in enumerate((hot0, hot1, hot2)):
        for at in range(0, base_ref.shape[1], BLOCK):
            cut = slice(at, at + BLOCK)
            place = src_ref[which:which + 1, cut]
            hits = pick_matrix(place_columns(place, 0, len(blocks), count), table.shape[0])
            near = mm(hits, table)
            held(f"d{which}")
            base_ref[which, cut, :] = near + share_ref[which, cut, :].astype(F32)
            hot[cut, :] = pick_matrix(place_columns(place, 1, len(blocks), count), table.shape[0])


def decode_kernel(*refs):
    *blocks, base_ref, hot0, hot1, hot2, w_hbm, grid_hbm, out_hbm, w_ref, grid_ref, out_ref, sems, out_sems = refs
    held = Held(sems, w=(w_hbm, w_ref), grid=(grid_hbm, grid_ref))
    table = jnp.concatenate([b[...] for b in blocks], axis=0) * 0.5
    step = out_ref.shape[0] // out_sems.shape[0]
    sent = []
    for at in range(0, out_ref.shape[0], step):
        cut = slice(at, at + step)
        hidden = None
        for which, hot in enumerate((hot0, hot1, hot2)):
            more = half_silu(base_ref[which, cut, :] + mm(hot[cut, :], table))
            hidden = more if hidden is None else hidden + more
        update = scaled(mm(hidden.astype(BF), held("w")[...]))
        out_ref[cut, :] = (held("grid")[cut, :].astype(F32) + update).astype(BF)
        sent.append(pltpu.make_async_copy(out_ref.at[cut, :], out_hbm.at[cut, :], out_sems.at[at // step]))
        sent[-1].start()
    for copy in sent:
        copy.wait()


def call(kernel, name, out, specs, args, scratch=(), flops=0, limit=24, outs=None, copies=0, wait=True):
    if scratch and wait:
        scratch = list(scratch) + [pltpu.SemaphoreType.DMA((16,))]
    if copies:
        scratch.append(pltpu.SemaphoreType.DMA((copies,)))
    args = [pltpu.with_memory_space_constraint(a, pltpu.HBM) if s is HB else a for s, a in zip(specs, args)]
    return pl.pallas_call(
        kernel,
        out_shape=out,
        in_specs=specs,
        out_specs=jax.tree.map(lambda _: VM, out) if outs is None else outs,
        scratch_shapes=scratch,
        compiler_params=pltpu.CompilerParams(vmem_limit_bytes=limit * MIB),
        cost_estimate=pl.CostEstimate(flops=flops, bytes_accessed=4 * MIB, transcendentals=0),
        name=name,
    )(*args)


def strip_shift(value, by):
    length = lax.axis_size("grid")
    pairs = [(i, i + by) for i in range(length) if 0 <= i + by < length]
    return lax.ppermute(value, "grid", pairs)


def exchange(blocks):
    length = len(blocks)
    moved = [blocks[0]]
    for dz in range(1, length):
        moved.append(lax.ppermute(blocks[dz], "mesh", [(i, (i + dz) % length) for i in range(length)]))
    return moved


def shards(
    grid_latent,
    mesh_latent,
    enc_source,
    enc_slot,
    enc_geometry,
    edge_count,
    slot_row,
    halo_rows,
    proc_source,
    proc_target,
    proc_geometry,
    return_rows,
    dec_source,
    dec_geometry,
    enc_weights,
    enc_lift,
    proc_weights,
    proc_lift,
    dec_weights,
    dec_lift,
):
    nodes, width = grid_latent.shape
    mesh_rows = mesh_latent.shape[0]
    n_mesh = lax.axis_size("mesh")
    count = slot_row.shape[3]
    edges, links = enc_source.shape[0], proc_source.shape[0]
    near_of = dec_source.shape[1]
    shape = jax.ShapeDtypeStruct
    block = shape((count, width), BF)
    row = shape((mesh_rows, width), BF)
    wide_row = shape((mesh_rows, width), F32)
    weight = shape((width, width), BF)
    square = pltpu.VMEM((width, width), BF)
    lifts = pltpu.VMEM(enc_lift.shape, F32)
    above = strip_shift(slot_row[0], -1)
    message, slot, *far = call(
        encode_kernel, "encode", (shape((edges, width), BF), shape((1, edges), jnp.int32)) + (block,) * n_mesh, [SM] + [HB] * 6,
        (edge_count, grid_latent, enc_source.reshape(-1, 128), enc_slot.reshape(-1, 128), enc_geometry, enc_weights, enc_lift),
        [pltpu.VMEM((nodes, width), BF), pltpu.VMEM((edges // 128, 128), jnp.int32),
         pltpu.VMEM((edges // 128, 128), jnp.int32), pltpu.VMEM((4, edges), F32), square, square, lifts,
         pltpu.VMEM((nodes, width), BF)],
        flops=5 * 10**9,
    )
    far = exchange(far)
    halo = halo_rows[0].T
    sends = shape((halo.size, width), BF)
    hot = shape((halo.size, -(-mesh_rows // 128) * 128), BF)
    *near, start, own, wb, wc, wn, hot, hot_far = call(
        near_kernel, "near", (block,) * n_mesh + (row, wide_row, weight, weight, weight, hot, pltpu.HBM(hot.shape, BF)),
        [VM] * 2 + [HB] * 4, (message, slot, halo, mesh_latent, enc_weights, proc_weights),
        [pltpu.VMEM(halo.shape, jnp.int32), square, square], flops=10**9, outs=(VM,) * (n_mesh + 6) + (HB,), copies=1,
    )
    part = shape((mesh_rows // 2, width), BF)
    up = call(far_kernel, "far", (part, part), [VM] * (n_mesh + 1) + [ANY], (*far, above, near[0]), flops=10**8)
    near = exchange(near)
    up = [strip_shift(up[0], 1), strip_shift(up[1], 1)]
    latent, sender, sent = call(
        first_kernel, "first", (row, row, sends), [VM] * (n_mesh + 9),
        (*near, *up, slot_row[0], start, own, wb, wc, wn, hot), flops=10**9,
    )
    layers = proc_weights.shape[0]
    half = shape((links // 2, width), BF)
    index = shape((links // 128, 128), jnp.int32)
    for layer in range(layers):
        came = lax.all_to_all(
            sent.reshape(lax.axis_size("grid") * n_mesh, -1, width), ("grid", "mesh"), split_axis=0, concat_axis=0, tiled=True
        ).reshape(sent.shape)
        last = layer + 1 == layers
        operands = [
            latent, sender, proc_source.reshape(-1, 128), proc_target.reshape(-1, 128), proc_geometry, proc_lift, proc_weights,
        ]
        outs = (wide_row, index, index, half, half) + (pltpu.HBM(weight.shape, BF),) * 2
        out_specs = (VM,) * 5 + (HB,) * 2
        scratch = [pltpu.VMEM((4, links), F32), lifts, square, square, square, square]
        specs = [VM] * 2 + [HB] * 5
        if last:
            operands += [grid_latent, dec_geometry.transpose(1, 0, 2), dec_lift, dec_weights]
            specs += [HB] * 4
            outs = (pltpu.HBM((nodes, width), BF),) * near_of + (pltpu.HBM(weight.shape, BF),) + outs
            out_specs = (HB,) * (near_of + 1) + out_specs
            scratch = [
                pltpu.VMEM((nodes, width), BF), pltpu.VMEM((near_of, 4, nodes), F32), lifts, square, square,
                pltpu.VMEM((nodes, width), F32), pltpu.VMEM((near_of, nodes, width), BF),
            ] + scratch
        held = list(call(
            functools.partial(before_kernel, layer=layer, last=last), "before", outs, specs, operands, scratch, flops=10**9,
            outs=out_specs, copies=3 + near_of,
        ))
        if last:
            *shares, dec_out = held[:near_of + 1]
            held = held[near_of + 1:]
        if layer == 0:
            places, held[0] = lax.optimization_barrier((return_rows[0], held[0]))
            places = strip_shift(places, -1)
        out = call(
            functools.partial(layer_kernel, layer=layer, last=last), "layer",
            (row, row) + ((block,) * n_mesh if last else (sends,)), [VM] * 7 + [HB] * 4 + [VM if last else HB, ANY],
            (latent, came, *held, proc_weights, dec_weights if last else proc_weights, return_rows[0] if last else hot_far, places),
            [pltpu.VMEM((links, width), BF)] + [square] * 4 + [pltpu.VMEM(hot.shape, BF)], flops=4 * 10**9,
        )
        if last:
            latent, proj, *back = out
        else:
            latent, sender, sent = out
    proj = strip_shift(proj, -1)
    back = exchange(back)
    ahead = exchange(call(spread_kernel, "spread", (block,) * n_mesh, [VM] * 2, (proj, places), flops=10**8))
    base, *hots = call(
        decode_near_kernel, "decode_near",
        (shape((near_of, nodes, width), F32),) + (shape((nodes, n_mesh * count), BF),) * near_of,
        [VM] * n_mesh + [HB] * (near_of + 1), (*back, *shares, dec_source.T),
        [pltpu.VMEM((near_of, nodes), jnp.int32), pltpu.VMEM((near_of, nodes, width), BF)], flops=3 * 10**9,
    )
    grid_out = call(
        decode_kernel, "decode", pltpu.HBM(grid_latent.shape, BF), [VM] * (n_mesh + 4) + [HB] * 2,
        (*ahead, base, *hots, dec_out, grid_latent),
        [square, pltpu.VMEM((nodes, width), BF), pltpu.VMEM((nodes, width), BF)],
        flops=3 * 10**9, outs=HB, copies=4,
    )
    return (grid_out, latent)


def solution(mesh):
    placed = (
        P(("grid", "mesh"), None),
        P(("grid", "mesh"), None),
        P(("grid", "mesh")),
        P(("grid", "mesh")),
        P(None, ("grid", "mesh")),
        P(("grid", "mesh")),
        P(("grid", "mesh"), None, None, None),
        P(("grid", "mesh"), None, None),
        P(("grid", "mesh")),
        P(("grid", "mesh")),
        P(None, ("grid", "mesh")),
        P(("grid", "mesh"), None, None, None),
        P(("grid", "mesh"), None),
        P(None, None, ("grid", "mesh")),
        P(),
        P(),
        P(),
        P(),
        P(),
        P(),
    )
    return jax.shard_map(
        shards,
        mesh=mesh,
        in_specs=placed,
        out_specs=(P(("grid", "mesh"), None), P(("grid", "mesh"), None)),
        check_vma=False,
    )
```

time: 131 us -> 122 us (0.931)
  Pallas kernels: 48.1 us -> 42.6 us
  waiting for transfers between devices: 39.4 us -> 34 us
  starting transfers between devices: 41.3 us -> 43.6 us
    all_to_all x2, waiting for transfers between devices: 32.2 us -> 23.4 us  [shards(): lax.all_to_all(sent.reshape(lax.axis_size('grid') * n_mesh, -1, width), (...]
    pallas_call x11, Pallas kernels: 48.1 us -> 42.6 us  [call(): pl.pallas_call(kernel, out_shape=out, in_specs=specs, out_specs=jax.tree....]
    ppermute x4 -> x5, starting transfers between devices: 10.9 us -> 14.5 us  [strip_shift(): return lax.ppermute(value, 'grid', pairs)]
    ppermute x12, waiting for transfers between devices: 4.49 us -> 6.45 us  [exchange(): lax.ppermute(blocks[dz], 'mesh', [(i, (i + dz) % length) for i in range(l...]
    ppermute x4 -> x5, waiting for transfers between devices: 2.73 us -> 4.19 us  [strip_shift(): return lax.ppermute(value, 'grid', pairs)]
  transfers between devices with their start and end apart: 18 -> 19, of which waited for: 8 -> 11; matrix products, arithmetic and copies ran while one was open for 0% -> 0% of each run, Pallas kernels for 11% -> 15%
where the time goes in v1:
time: 122 us
  starting transfers between devices  43.6 us (36%)
  Pallas kernels  42.6 us (35%)
  waiting for transfers between devices  34 us (28%)
  between operations  1.63 us (1%)
    pallas_call x11, Pallas kernels, call(): pl.pallas_call(kernel, out_shape=out, in_specs=specs, out_specs=jax.tree....  42.6 us
    all_to_all x2, waiting for transfers between devices, shards(): lax.all_to_all(sent.reshape(lax.axis_size('grid') * n_mesh, -1, width), (...  23.4 us
    ppermute x12, starting transfers between devices, exchange(): lax.ppermute(blocks[dz], 'mesh', [(i, (i + dz) % length) for i in range(l...  14.7 us
    ppermute x5, starting transfers between devices, strip_shift(): return lax.ppermute(value, 'grid', pairs)  14.5 us
    all_to_all x2, starting transfers between devices, shards(): lax.all_to_all(sent.reshape(lax.axis_size('grid') * n_mesh, -1, width), (...  14.5 us
    ppermute x12, waiting for transfers between devices, exchange(): lax.ppermute(blocks[dz], 'mesh', [(i, (i + dz) % length) for i in range(l...  6.45 us
    ppermute x5, waiting for transfers between devices, strip_shift(): return lax.ppermute(value, 'grid', pairs)  4.19 us
  transfers between devices with their start and end apart: 19, of which 11 were waited for; matrix products, arithmetic and copies ran while one was open for 0% of the time, Pallas kernels for 15%

profile of v1, /device:TPU:1, one launch (start us, length us, event | category | flops | bytes accessed | tf_op | source)
XLA Modules:
  0.0 121.9 jit_solution(6821425583355811698)
XLA Ops:
  1.3 8.1 %encode.1 = (bf16[2048,512]{1,0:T(8,128)(2,1)S(1)}, s32[1,2048]{1,0:T(1,128)S(1)}, bf16[128,512]{1,0:T(8,128)(2,1)S(1)}, bf16[128,512]{1,0:T(8,128)(2,1)S(1)}, b...) custom-call(s32[1]{0:T(128)S(6)} %copy.22.count_ref, bf16[1024,512]{1,0:T(8,128)(2,1)} %refs_9_.1, ...), custom_call_target="tpu_custom_call" | custom-call | flops 5000000000 | bytes 4194304 | tf_op jit(solution)/shard_map/encode/pallas_call | solution.py:387
  9.4 2.5 %collective-permute-start.3 = (bf16[128,512]{1,0:T(8,128)(2,1)S(1)}, bf16[128,512]{1,0:T(8,128)(2,1)S(1)}, u32[]{:S(2)}, u32[]{:S(2)}) collective-permute-start(bf16[128,512]{1,0:T(8,128)(2,1)S(1)} %get-tuple-element.68), channel_id=1, source_target_pairs={{0,1},{1,2},{2,3},{3,0},{4,5},{5,6},{6,7},{7,4},{8,9},{9,10},{10,1... | collective-permute-start | bytes 393224 | tf_op jit(solution)/shard_map/ppermute | solution.py:409
  11.9 3.3 %collective-permute-start.4 = (bf16[128,512]{1,0:T(8,128)(2,1)S(1)}, bf16[128,512]{1,0:T(8,128)(2,1)S(1)}, u32[]{:S(2)}, u32[]{:S(2)}) collective-permute-start(bf16[128,512]{1,0:T(8,128)(2,1)S(1)} %get-tuple-element.69), channel_id=1, source_target_pairs={{0,2},{1,3},{2,0},{3,1},{4,6},{5,7},{6,4},{7,5},{8,10},{9,11},{10,... | collective-permute-start | bytes 393224 | tf_op jit(solution)/shard_map/ppermute | solution.py:409
  15.2 0.7 collective-permute-start.5
  16.0 3.4 %collective-permute-start.6 = (s32[2,4,128]{2,1,0:T(4,128)S(1)}, s32[2,4,128]{2,1,0:T(4,128)S(1)}, u32[]{:S(2)}, u32[]{:S(2)}) collective-permute-start(s32[2,4,128]{2,1,0:T(4,128)S(1)} %bitcast.17), channel_id=1, source_target_pairs={{4,0},{8,4},{12,8},{16,12},{20,16},{24,20},{28,24},{32,28},{36,32}... | collective-permute-start | bytes 12296 | tf_op jit(solution)/shard_map/ppermute | solution.py:402
  19.4 3.0 %near.1 = (bf16[128,512]{1,0:T(8,128)(2,1)S(1)}, bf16[128,512]{1,0:T(8,128)(2,1)S(1)}, bf16[128,512]{1,0:T(8,128)(2,1)S(1)}, bf16[128,512]{1,0:T(8,128)(2,1)S(1)...) custom-call(bf16[2048,512]{1,0:T(8,128)(2,1)S(1)} %get-tuple-element, ...), custom_call_target="tpu_custom_call" | custom-call | flops 1000000000 | bytes 4194304 | tf_op jit(solution)/shard_map/near/pallas_call | solution.py:387
  22.4 0.8 collective-permute-start
  23.4 2.3 %collective-permute-start.2 = (bf16[128,512]{1,0:T(8,128)(2,1)S(1)}, bf16[128,512]{1,0:T(8,128)(2,1)S(1)}, u32[]{:S(2)}, u32[]{:S(2)}) collective-permute-start(bf16[128,512]{1,0:T(8,128)(2,1)S(1)} %get-tuple-element.66), channel_id=1, source_target_pairs={{0,3},{1,0},{2,1},{3,2},{4,7},{5,4},{6,5},{7,6},{8,11},{9,8},{10,9... | collective-permute-start | bytes 393224 | tf_op jit(solution)/shard_map/ppermute | solution.py:409
  26.0 3.7 %collective-permute-start.7 = (bf16[80,512]{1,0:T(8,128)(2,1)S(1)}, bf16[80,512]{1,0:T(8,128)(2,1)S(1)}, u32[]{:S(2)}, u32[]{:S(2)}) collective-permute-start(bf16[80,512]{1,0:T(8,128)(2,1)S(1)} %get-tuple-element.71), channel_id=1, source_target_pairs={{0,4},{4,8},{8,12},{12,16},{16,20},{20,24},{24,28},{28,32},{32,36}... | collective-permute-start | bytes 245768 | tf_op jit(solution)/shard_map/ppermute | solution.py:402
  29.7 1.9 %collective-permute-start.8 = (bf16[80,512]{1,0:T(8,128)(2,1)S(1)}, bf16[80,512]{1,0:T(8,128)(2,1)S(1)}, u32[]{:S(2)}, u32[]{:S(2)}) collective-permute-start(bf16[80,512]{1,0:T(8,128)(2,1)S(1)} %get-tuple-element.72), channel_id=1, source_target_pairs={{0,4},{4,8},{8,12},{12,16},{16,20},{20,24},{24,28},{28,32},{32,36}... | collective-permute-start | bytes 245768 | tf_op jit(solution)/shard_map/ppermute | solution.py:402
  31.7 0.8 collective-permute-done.2.refs_3_
  33.1 2.3 %first.1 = (bf16[160,512]{1,0:T(8,128)(2,1)S(1)}, bf16[160,512]{1,0:T(8,128)(2,1)S(1)}, bf16[1024,512]{1,0:T(8,128)(2,1)}) custom-call(bf16[128,512]{1,0:T(8,128)(2,1)S(1)} %get-tuple-element.63.refs_5_.refs_0_, bf16[128,512]{1,0:T(8,128)(2,1)S(1)} %collective-permute-done.refs_1_, bf16[128,512]{1,0:T(8,128)(2,1)S(1)} %collective-permute-done.1.refs_2_, ...), custom_call_target="tpu_custom_call" | custom-call | flops 1000000000 | bytes 4194304 | tf_op jit(solution)/shard_map/first/pallas_call | solution.py:387
  35.4 10.6 %all-to-all-start = ((bf16[128,8,512]{2,1,0:T(8,128)(2,1)}), bf16[128,8,512]{2,1,0:T(8,128)(2,1)S(1)}, u32[]{:S(2)}, u32[]{:S(2)}) async-start(bf16[128,8,512]{2,1,0:T(8,128)(2,1)} %bitcast.5), calls=%async_computation | async-start | bytes 2097152 | tf_op jit(solution)/shard_map/all_to_all | solution.py:478
  46.0 4.2 %before.2 = (f32[160,512]{1,0:T(8,128)S(1)}, s32[10,128]{1,0:T(8,128)S(1)}, s32[10,128]{1,0:T(8,128)S(1)}, bf16[640,512]{1,0:T(8,128)(2,1)S(1)}, bf16[640,512]{1...) custom-call(bf16[160,512]{1,0:T(8,128)(2,1)S(1)} %get-tuple-element.79.latent_ref, ...), custom_call_target="tpu_custom_call" | custom-call | flops 1000000000 | bytes 4194304 | tf_op jit(solution)/shard_map/before/pallas_call | solution.py:387
  50.2 3.2 %collective-permute-start.9 = (s32[2,4,128]{2,1,0:T(4,128)S(1)}, s32[2,4,128]{2,1,0:T(4,128)S(1)}, u32[]{:S(2)}, u32[]{:S(2)}) collective-permute-start(s32[2,4,128]{2,1,0:T(4,128)S(1)} %bitcast.19), channel_id=1, source_target_pairs={{4,0},{8,4},{12,8},{16,12},{20,16},{24,20},{28,24},{32,28},{36,32}... | collective-permute-start | bytes 12296 | tf_op jit(solution)/shard_map/ppermute | solution.py:402
  53.4 2.1 %collective-permute-done.9.rest_7_.rows_ref = s32[2,4,128]{2,1,0:T(4,128)S(1)} collective-permute-done((s32[2,4,128]{2,1,0:T(4,128)S(1)}, s32[2,4,128]{2,1,0:T(4,128)S(1)}, u32[]{:S(2)}, u32[]{:S(2)}) %collective-permute-start.9) | collective-permute-done | bytes 4128 | tf_op jit(solution)/shard_map/ppermute | solution.py:402
  55.5 10.1 %all-to-all-done = bf16[128,8,512]{2,1,0:T(8,128)(2,1)S(1)} async-done(((bf16[128,8,512]{2,1,0:T(8,128)(2,1)}), bf16[128,8,512]{2,1,0:T(8,128)(2,1)S(1)}, u32[]{:S(2)}, u32[]{:S(2)}) %all-to-all-start) | async-done | bytes 1048608 | tf_op jit(solution)/shard_map/all_to_all | solution.py:478
  65.6 5.3 %layer.2 = (bf16[160,512]{1,0:T(8,128)(2,1)S(1)}, bf16[160,512]{1,0:T(8,128)(2,1)S(1)}, bf16[1024,512]{1,0:T(8,128)(2,1)}) custom-call(bf16[160,512]{1,0:T(8,128)(2,1)S(1)} %get-tuple-element.79.latent_ref, bf16[1024,512]{1,0:T(8,128)(2,1)S(1)} %bitcast.15, f32[160,512]{1,0:T(8,128)S(1)} %get-tuple-element.83.own_ref, ...), custom_call_target="tpu_custom_call" | custom-call | flops 4000000000 | bytes 4194304 | tf_op jit(solution)/shard_map/layer/pallas_call | solution.py:387
  70.9 3.9 %all-to-all-start.1 = ((bf16[128,8,512]{2,1,0:T(8,128)(2,1)}), bf16[128,8,512]{2,1,0:T(8,128)(2,1)S(1)}, u32[]{:S(2)}, u32[]{:S(2)}) async-start(bf16[128,8,512]{2,1,0:T(8,128)(2,1)} %bitcast.10), calls=%async_computation.1 | async-start | bytes 2097152 | tf_op jit(solution)/shard_map/all_to_all | solution.py:478
  74.8 6.4 %before.3 = (bf16[1024,512]{1,0:T(8,128)(2,1)}, bf16[1024,512]{1,0:T(8,128)(2,1)}, bf16[1024,512]{1,0:T(8,128)(2,1)}, bf16[512,512]{1,0:T(8,128)(2,1)}, f32[160,...) custom-call(bf16[160,512]{1,0:T(8,128)(2,1)S(1)} %get-tuple-element., ...), custom_call_target="tpu_custom_call" | custom-call | flops 1000000000 | bytes 4194304 | tf_op jit(solution)/shard_map/before/pallas_call | solution.py:387
  81.2 13.3 %all-to-all-done.1 = bf16[128,8,512]{2,1,0:T(8,128)(2,1)S(1)} async-done(((bf16[128,8,512]{2,1,0:T(8,128)(2,1)}), bf16[128,8,512]{2,1,0:T(8,128)(2,1)S(1)}, u32[]{:S(2)}, u32[]{:S(2)}) %all-to-all-start.1) | async-done | bytes 1048608 | tf_op jit(solution)/shard_map/all_to_all | solution.py:478
  94.5 4.4 %layer.3 = (bf16[160,512]{1,0:T(8,128)(2,1)}, bf16[160,512]{1,0:T(8,128)(2,1)S(1)}, bf16[128,512]{1,0:T(8,128)(2,1)S(1)}, bf16[128,512]{1,0:T(8,128)(2,1)S(1)}, ...) custom-call(bf16[160,512]{1,0:T(8,128)(2,1)S(1)} %get-tuple-element.92.latent_ref, ...), custom_call_target="tpu_custom_call" | custom-call | flops 4000000000 | bytes 4194304 | tf_op jit(solution)/shard_map/layer/pallas_call | solution.py:387
  98.9 2.3 %collective-permute-start.10 = (bf16[160,512]{1,0:T(8,128)(2,1)S(1)}, bf16[160,512]{1,0:T(8,128)(2,1)S(1)}, u32[]{:S(2)}, u32[]{:S(2)}) collective-permute-start(bf16[160,512]{1,0:T(8,128)(2,1)S(1)} %get-tuple-element.102), channel_id=1, source_target_pairs={{4,0},{8,4},{12,8},{16,12},{20,16},{24,20},{28,24},{32,28},{36,32}... | collective-permute-start | bytes 491528 | tf_op jit(solution)/shard_map/ppermute | solution.py:402
  101.9 1.5 %collective-permute-start.15 = (bf16[128,512]{1,0:T(8,128)(2,1)S(1)}, bf16[128,512]{1,0:T(8,128)(2,1)S(1)}, u32[]{:S(2)}, u32[]{:S(2)}) collective-permute-start(bf16[128,512]{1,0:T(8,128)(2,1)S(1)} %get-tuple-element.109), channel_id=1, source_target_pairs={{0,2},{1,3},{2,0},{3,1},{4,6},{5,7},{6,4},{7,5},{8,10},{9,11},{10,... | collective-permute-start | bytes 393224 | tf_op jit(solution)/shard_map/ppermute | solution.py:409
  103.4 1.0 collective-permute-start.16
  104.4 1.5 %collective-permute-done.10.table_ref = bf16[160,512]{1,0:T(8,128)(2,1)S(1)} collective-permute-done((bf16[160,512]{1,0:T(8,128)(2,1)S(1)}, bf16[160,512]{1,0:T(8,128)(2,1)S(1)}, u32[]{:S(2)}, u32[]{:S(2)}) %collective-permute-start.10) | collective-permute-done | bytes 163872 | tf_op jit(solution)/shard_map/ppermute | solution.py:402
  106.9 1.1 collective-permute-start.12
  107.9 2.9 %collective-permute-done.14.refs_1_ = bf16[128,512]{1,0:T(8,128)(2,1)S(1)} collective-permute-done((bf16[128,512]{1,0:T(8,128)(2,1)S(1)}, bf16[128,512]{1,0:T(8,128)(2,1)S(1)}, u32[]{:S(2)}, u32[]{:S(2)}) %collective-permute-start.14) | collective-permute-done | bytes 131104 | tf_op jit(solution)/shard_map/ppermute | solution.py:409
  111.4 3.6 %decode_near.1 = (f32[3,1024,512]{2,1,0:T(8,128)S(1)}, bf16[1024,512]{1,0:T(8,128)(2,1)S(1)}, bf16[1024,512]{1,0:T(8,128)(2,1)S(1)}, bf16[1024,512]{1,0:T(8,128)(2,1)S(1)}) custom-call(bf16[128,512]{1,0:T(8,128)(2,1)S(1)} %get-tuple-element.107.refs_0_, bf16[128,512]{1,0:T(8,128)(2,1)S(1)} %collective-permute-done.14.refs_1_, ...), custom_call_target="tpu_custom_call" | custom-call | flops 3000000000 | bytes 4194304 | tf_op jit(solution)/shard_map/decode_near/pallas_call | solution.py:387
  114.9 1.2 %collective-permute-done.11.refs_1_ = bf16[128,512]{1,0:T(8,128)(2,1)S(1)} collective-permute-done((bf16[128,512]{1,0:T(8,128)(2,1)S(1)}, bf16[128,512]{1,0:T(8,128)(2,1)S(1)}, u32[]{:S(2)}, u32[]{:S(2)}) %collective-permute-start.11) | collective-permute-done | bytes 131104 | tf_op jit(solution)/shard_map/ppermute | solution.py:409
  116.2 0.8 collective-permute-done.13.refs_3_
  117.0 4.7 %decode.1 = bf16[1024,512]{1,0:T(8,128)(2,1)} custom-call(bf16[128,512]{1,0:T(8,128)(2,1)S(1)} %get-tuple-element.103.refs_0_, bf16[128,512]{1,0:T(8,128)(2,1)S(1)} %collective-permute-done.11.refs_1_, bf16[128,512]{1,0:T(8,128)(2,1)S(1)} %collective-permute-done.12.refs_2_, bf16[128,512]{1,0:T(8,128)(2,1)S(1)} %collective-permute-done.13.refs_3_, ...), custom_call_target="tpu_custom_call" | custom-call | flops 3000000000 | bytes 4194304 | tf_op jit(solution)/shard_map/decode/pallas_call | solution.py:387
  (21 shorter events, 3.2 us)
Async XLA Ops:
  1.3 14.7 %copy-start = (s32[1,2,4,128]{3,2,1,0:T(4,128)S(1)}, s32[1,2,4,128]{3,2,1,0:T(4,128)}, u32[]{:S(2)}) copy-start(s32[1,2,4,128]{3,2,1,0:T(4,128)} %param.26) | copy-start | bytes 12292
  9.4 14.0 %collective-permute-start.3 = (bf16[128,512]{1,0:T(8,128)(2,1)S(1)}, bf16[128,512]{1,0:T(8,128)(2,1)S(1)}, u32[]{:S(2)}, u32[]{:S(2)}) collective-permute-start(bf16[128,512]{1,0:T(8,128)(2,1)S(1)} %get-tuple-element.68), channel_id=1, source_target_pairs={{0,1},{1,2},{2,3},{3,0},{4,5},{5,6},{6,7},{7,4},{8,9},{9,10},{10,1... | collective-permute-start | bytes 393224 | tf_op jit(solution)/shard_map/ppermute | solution.py:409
  11.9 13.8 %collective-permute-start.4 = (bf16[128,512]{1,0:T(8,128)(2,1)S(1)}, bf16[128,512]{1,0:T(8,128)(2,1)S(1)}, u32[]{:S(2)}, u32[]{:S(2)}) collective-permute-start(bf16[128,512]{1,0:T(8,128)(2,1)S(1)} %get-tuple-element.69), channel_id=1, source_target_pairs={{0,2},{1,3},{2,0},{3,1},{4,6},{5,7},{6,4},{7,5},{8,10},{9,11},{10,... | collective-permute-start | bytes 393224 | tf_op jit(solution)/shard_map/ppermute | solution.py:409
  15.2 10.5 %collective-permute-start.5 = (bf16[128,512]{1,0:T(8,128)(2,1)S(1)}, bf16[128,512]{1,0:T(8,128)(2,1)S(1)}, u32[]{:S(2)}, u32[]{:S(2)}) collective-permute-start(bf16[128,512]{1,0:T(8,128)(2,1)S(1)} %get-tuple-element.70), channel_id=1, source_target_pairs={{0,3},{1,0},{2,1},{3,2},{4,7},{5,4},{6,5},{7,6},{8,11},{9,8},{10,9... | collective-permute-start | bytes 393224 | tf_op jit(solution)/shard_map/ppermute | solution.py:409
  16.0 7.3 %collective-permute-start.6 = (s32[2,4,128]{2,1,0:T(4,128)S(1)}, s32[2,4,128]{2,1,0:T(4,128)S(1)}, u32[]{:S(2)}, u32[]{:S(2)}) collective-permute-start(s32[2,4,128]{2,1,0:T(4,128)S(1)} %bitcast.17), channel_id=1, source_target_pairs={{4,0},{8,4},{12,8},{16,12},{20,16},{24,20},{28,24},{32,28},{36,32}... | collective-permute-start | bytes 12296 | tf_op jit(solution)/shard_map/ppermute | solution.py:402
  22.4 9.3 %collective-permute-start = (bf16[128,512]{1,0:T(8,128)(2,1)S(1)}, bf16[128,512]{1,0:T(8,128)(2,1)S(1)}, u32[]{:S(2)}, u32[]{:S(2)}) collective-permute-start(bf16[128,512]{1,0:T(8,128)(2,1)S(1)} %get-tuple-element.64), channel_id=1, source_target_pairs={{0,1},{1,2},{2,3},{3,0},{4,5},{5,6},{6,7},{7,4},{8,9},{9,10},{10,1... | collective-permute-start | bytes 393224 | tf_op jit(solution)/shard_map/ppermute | solution.py:409
  23.2 8.5 %collective-permute-start.1 = (bf16[128,512]{1,0:T(8,128)(2,1)S(1)}, bf16[128,512]{1,0:T(8,128)(2,1)S(1)}, u32[]{:S(2)}, u32[]{:S(2)}) collective-permute-start(bf16[128,512]{1,0:T(8,128)(2,1)S(1)} %get-tuple-element.65), channel_id=1, source_target_pairs={{0,2},{1,3},{2,0},{3,1},{4,6},{5,7},{6,4},{7,5},{8,10},{9,11},{10,... | collective-permute-start | bytes 393224 | tf_op jit(solution)/shard_map/ppermute | solution.py:409
  23.4 9.1 %collective-permute-start.2 = (bf16[128,512]{1,0:T(8,128)(2,1)S(1)}, bf16[128,512]{1,0:T(8,128)(2,1)S(1)}, u32[]{:S(2)}, u32[]{:S(2)}) collective-permute-start(bf16[128,512]{1,0:T(8,128)(2,1)S(1)} %get-tuple-element.66), channel_id=1, source_target_pairs={{0,3},{1,0},{2,1},{3,2},{4,7},{5,4},{6,5},{7,6},{8,11},{9,8},{10,9... | collective-permute-start | bytes 393224 | tf_op jit(solution)/shard_map/ppermute | solution.py:409
  26.0 6.5 %collective-permute-start.7 = (bf16[80,512]{1,0:T(8,128)(2,1)S(1)}, bf16[80,512]{1,0:T(8,128)(2,1)S(1)}, u32[]{:S(2)}, u32[]{:S(2)}) collective-permute-start(bf16[80,512]{1,0:T(8,128)(2,1)S(1)} %get-tuple-element.71), channel_id=1, source_target_pairs={{0,4},{4,8},{8,12},{12,16},{16,20},{20,24},{24,28},{28,32},{32,36}... | collective-permute-start | bytes 245768 | tf_op jit(solution)/shard_map/ppermute | solution.py:402
  29.7 3.4 %collective-permute-start.8 = (bf16[80,512]{1,0:T(8,128)(2,1)S(1)}, bf16[80,512]{1,0:T(8,128)(2,1)S(1)}, u32[]{:S(2)}, u32[]{:S(2)}) collective-permute-start(bf16[80,512]{1,0:T(8,128)(2,1)S(1)} %get-tuple-element.72), channel_id=1, source_target_pairs={{0,4},{4,8},{8,12},{12,16},{16,20},{20,24},{24,28},{28,32},{32,36}... | collective-permute-start | bytes 245768 | tf_op jit(solution)/shard_map/ppermute | solution.py:402
  35.4 30.2 %all-to-all-start = ((bf16[128,8,512]{2,1,0:T(8,128)(2,1)}), bf16[128,8,512]{2,1,0:T(8,128)(2,1)S(1)}, u32[]{:S(2)}, u32[]{:S(2)}) async-start(bf16[128,8,512]{2,1,0:T(8,128)(2,1)} %bitcast.5), calls=%async_computation | async-start | bytes 2097152 | tf_op jit(solution)/shard_map/all_to_all | solution.py:478
  46.0 4.2 %copy-start.1 = (s32[1,2,4,128]{3,2,1,0:T(4,128)S(1)}, s32[1,2,4,128]{3,2,1,0:T(4,128)}, u32[]{:S(2)}) copy-start(s32[1,2,4,128]{3,2,1,0:T(4,128)} %param.31) | copy-start | bytes 12292
  50.2 5.3 %collective-permute-start.9 = (s32[2,4,128]{2,1,0:T(4,128)S(1)}, s32[2,4,128]{2,1,0:T(4,128)S(1)}, u32[]{:S(2)}, u32[]{:S(2)}) collective-permute-start(s32[2,4,128]{2,1,0:T(4,128)S(1)} %bitcast.19), channel_id=1, source_target_pairs={{4,0},{8,4},{12,8},{16,12},{20,16},{24,20},{28,24},{32,28},{36,32}... | collective-permute-start | bytes 12296 | tf_op jit(solution)/shard_map/ppermute | solution.py:402
  70.9 23.6 %all-to-all-start.1 = ((bf16[128,8,512]{2,1,0:T(8,128)(2,1)}), bf16[128,8,512]{2,1,0:T(8,128)(2,1)S(1)}, u32[]{:S(2)}, u32[]{:S(2)}) async-start(bf16[128,8,512]{2,1,0:T(8,128)(2,1)} %bitcast.10), calls=%async_computation.1 | async-start | bytes 2097152 | tf_op jit(solution)/shard_map/all_to_all | solution.py:478
  98.9 6.9 %collective-permute-start.10 = (bf16[160,512]{1,0:T(8,128)(2,1)S(1)}, bf16[160,512]{1,0:T(8,128)(2,1)S(1)}, u32[]{:S(2)}, u32[]{:S(2)}) collective-permute-start(bf16[160,512]{1,0:T(8,128)(2,1)S(1)} %get-tuple-element.102), channel_id=1, source_target_pairs={{4,0},{8,4},{12,8},{16,12},{20,16},{24,20},{28,24},{32,28},{36,32}... | collective-permute-start | bytes 491528 | tf_op jit(solution)/shard_map/ppermute | solution.py:402
  101.2 9.6 %collective-permute-start.14 = (bf16[128,512]{1,0:T(8,128)(2,1)S(1)}, bf16[128,512]{1,0:T(8,128)(2,1)S(1)}, u32[]{:S(2)}, u32[]{:S(2)}) collective-permute-start(bf16[128,512]{1,0:T(8,128)(2,1)S(1)} %get-tuple-element.108), channel_id=1, source_target_pairs={{0,1},{1,2},{2,3},{3,0},{4,5},{5,6},{6,7},{7,4},{8,9},{9,10},{10,1... | collective-permute-start | bytes 393224 | tf_op jit(solution)/shard_map/ppermute | solution.py:409
  101.9 9.0 %collective-permute-start.15 = (bf16[128,512]{1,0:T(8,128)(2,1)S(1)}, bf16[128,512]{1,0:T(8,128)(2,1)S(1)}, u32[]{:S(2)}, u32[]{:S(2)}) collective-permute-start(bf16[128,512]{1,0:T(8,128)(2,1)S(1)} %get-tuple-element.109), channel_id=1, source_target_pairs={{0,2},{1,3},{2,0},{3,1},{4,6},{5,7},{6,4},{7,5},{8,10},{9,11},{10,... | collective-permute-start | bytes 393224 | tf_op jit(solution)/shard_map/ppermute | solution.py:409
  103.4 8.0 %collective-permute-start.16 = (bf16[128,512]{1,0:T(8,128)(2,1)S(1)}, bf16[128,512]{1,0:T(8,128)(2,1)S(1)}, u32[]{:S(2)}, u32[]{:S(2)}) collective-permute-start(bf16[128,512]{1,0:T(8,128)(2,1)S(1)} %get-tuple-element.110), channel_id=1, source_target_pairs={{0,3},{1,0},{2,1},{3,2},{4,7},{5,4},{6,5},{7,6},{8,11},{9,8},{10,9... | collective-permute-start | bytes 393224 | tf_op jit(solution)/shard_map/ppermute | solution.py:409
  106.2 9.9 %collective-permute-start.11 = (bf16[128,512]{1,0:T(8,128)(2,1)S(1)}, bf16[128,512]{1,0:T(8,128)(2,1)S(1)}, u32[]{:S(2)}, u32[]{:S(2)}) collective-permute-start(bf16[128,512]{1,0:T(8,128)(2,1)S(1)} %get-tuple-element.104), channel_id=1, source_target_pairs={{0,1},{1,2},{2,3},{3,0},{4,5},{5,6},{6,7},{7,4},{8,9},{9,10},{10,1... | collective-permute-start | bytes 393224 | tf_op jit(solution)/shard_map/ppermute | solution.py:409
  106.9 9.3 %collective-permute-start.12 = (bf16[128,512]{1,0:T(8,128)(2,1)S(1)}, bf16[128,512]{1,0:T(8,128)(2,1)S(1)}, u32[]{:S(2)}, u32[]{:S(2)}) collective-permute-start(bf16[128,512]{1,0:T(8,128)(2,1)S(1)} %get-tuple-element.105), channel_id=1, source_target_pairs={{0,2},{1,3},{2,0},{3,1},{4,6},{5,7},{6,4},{7,5},{8,10},{9,11},{10,... | collective-permute-start | bytes 393224 | tf_op jit(solution)/shard_map/ppermute | solution.py:409
  110.9 6.1 %collective-permute-start.13 = (bf16[128,512]{1,0:T(8,128)(2,1)S(1)}, bf16[128,512]{1,0:T(8,128)(2,1)S(1)}, u32[]{:S(2)}, u32[]{:S(2)}) collective-permute-start(bf16[128,512]{1,0:T(8,128)(2,1)S(1)} %get-tuple-element.106), channel_id=1, source_target_pairs={{0,3},{1,0},{2,1},{3,2},{4,7},{5,4},{6,5},{7,6},{8,11},{9,8},{10,9... | collective-permute-start | bytes 393224 | tf_op jit(solution)/shard_map/ppermute | solution.py:409

commit v2 on v1

--- a/solution.py
+++ b/solution.py
@@ -15,6 +15,9 @@
 ANY = pl.BlockSpec(memory_space=pl.ANY)
 MIB = 1024 * 1024
 BLOCK = 512
+OPPOSITE = 2
+EXTRA = 16
+PREP = 10**10
 
 
 def mm(a, b):
@@ -32,16 +35,16 @@
 
 
 def lane_hits(columns, at):
-    return columns - jnp.int16(at) == lax.broadcasted_iota(jnp.int16, columns.shape, 1)
+    return columns == lax.broadcasted_iota(jnp.int16, columns.shape, 1) + jnp.int16(at)
 
 
 def as_ones(hits):
     return jnp.where(hits, jnp.ones(hits.shape, BF), jnp.zeros(hits.shape, BF))
 
 
-def pick_matrix(columns, width):
+def pick_matrix(columns, width, start=0):
     col = columns.astype(jnp.int16)
-    return jnp.concatenate([as_ones(lane_hits(col, at)) for at in range(0, width, 128)], axis=1)
+    return jnp.concatenate([as_ones(lane_hits(col, at)) for at in range(start, start + width, 128)], axis=1)
 
 
 def add_matrix(row, height):
@@ -117,6 +120,10 @@
         if name in self.copies:
             self.copies.pop(name).wait()
         return self.refs[name]
+
+    def wait(self):
+        for name in list(self.copies):
+            self(name)
 
 
 class Sent:
@@ -169,34 +176,38 @@
 def encode_kernel(count_ref, grid_hbm, src_hbm, slot_hbm, geo_hbm, w_hbm, lift_hbm, message_ref, slot_out, *rest):
     outs, (grid_ref, src_ref, slot_ref, geo_ref, w0_ref, w1_ref, lift_ref, table_ref, sems) = rest[:4], rest[4:]
     nodes, edges = grid_ref.shape[0], message_ref.shape[0]
-    cuts = [slice(at, at + 256) for at in range(0, nodes, 256)]
     held = Held(
-        sems, w0=(w_hbm.at[0], w0_ref), **{f"g{i}": (grid_hbm.at[cut, :], grid_ref.at[cut, :]) for i, cut in enumerate(cuts)},
-        src=(src_hbm, src_ref), geo=(geo_hbm, geo_ref), lift=(lift_hbm, lift_ref), w1=(w_hbm.at[1], w1_ref),
-        slot=(slot_hbm, slot_ref),
-    )
-    held("w0")
-    for i, cut in enumerate(cuts):
-        table_ref[cut, :] = (mm(held(f"g{i}")[...], w0_ref[...]) * 0.5).astype(BF)
-    held("src"), held("geo"), held("w1")
-    right = lift_right(held("lift")[...] * 0.5)
-    for at in range(0, edges, BLOCK):
-        cut = slice(at, at + BLOCK)
-        half = mm(pick_matrix(to_columns(lanes(src_ref, at, BLOCK)), nodes), table_ref[...]) + lift(geo_ref[:, cut], right)
-        message_ref[cut, :] = norm(mm(half_silu(half).astype(BF), w1_ref[...])).astype(BF)
-    slot = lanes(held("slot"), 0, edges)
+        sems, grid=(grid_hbm, grid_ref), w0=(w_hbm.at[0], w0_ref), src=(src_hbm, src_ref), geo=(geo_hbm, geo_ref),
+        lift=(lift_hbm, lift_ref), w1=(w_hbm.at[1], w1_ref), slot=(slot_hbm, slot_ref),
+    )
+    held.wait()
+    table_ref[...] = (mm(grid_ref[...], w0_ref[...]) * 0.5).astype(BF)
+    right = lift_right(lift_ref[...] * 0.5)
+    cuts = [slice(at, at + BLOCK) for at in range(0, edges, BLOCK)]
+    hidden = None
+    for i in range(len(cuts) + 1):
+        ahead = hidden
+        if i < len(cuts):
+            picks = pick_matrix(to_columns(lanes(src_ref, cuts[i].start, BLOCK)), nodes)
+            hidden = half_silu(mm(picks, table_ref[...]) + lift(geo_ref[:, cuts[i]], right)).astype(BF)
+        if i > 0:
+            message_ref[cuts[i - 1], :] = norm(mm(ahead, w1_ref[...])).astype(BF)
+    slot = lanes(slot_ref, 0, edges)
     slot = jnp.where(lax.broadcasted_iota(jnp.int32, slot.shape, 1) < count_ref[0], slot, -1)
     slot_out[...] = slot
     slot_sums(slot, 1, len(outs), message_ref[...], outs)
 
 
-def near_kernel(message_ref, slot_ref, halo_hbm, latent_hbm, w_hbm, next_hbm, *rest):
-    outs, (latent_out, own_ref, wb_out, wc_out, wn_out, hot_ref, hot_hbm, halo_ref, wa_ref, wc_ref, sems, out_sems) = rest[:4], rest[4:]
+def near_kernel(message_ref, slot_ref, *outs):
+    slot_sums(slot_ref[...], 0, len(outs), message_ref[...], outs)
+
+
+def prep_kernel(_, halo_hbm, latent_hbm, w_hbm, next_hbm, *rest):
+    latent_out, own_ref, wb_out, wc_out, wn_out, hot_ref, hot_hbm, halo_ref, wa_ref, wc_ref, sems, out_sems = rest
     held = Held(
         sems, halo=(halo_hbm, halo_ref), latent=(latent_hbm, latent_out), wa=(w_hbm.at[2], wa_ref), wc=(w_hbm.at[4], wc_ref),
         wb=(w_hbm.at[3], wb_out), wn=(next_hbm.at[0, 0], wn_out),
     )
-    slot_sums(slot_ref[...], 0, len(outs), message_ref[...], outs)
     halo = held("halo")[...].astype(F32).astype(BF)
     places, owners = halo.shape
     row = lax.broadcasted_iota(jnp.int32, (places * owners, 128), 0)
@@ -215,41 +226,50 @@
 
 
 def far_kernel(*refs):
-    *blocks, rows_ref, _, low_ref, high_ref = refs
+    *blocks, rows_ref, _, out_ref = refs
     rows = rows_from(rows_ref[1], lax.axis_index("mesh"))
     table = jnp.concatenate([b[...] for b in blocks], axis=0)
-    total = mm(add_matrix(rows, 2 * low_ref.shape[0]), table).astype(BF)
-    low_ref[...] = total[:low_ref.shape[0]]
-    high_ref[...] = total[low_ref.shape[0]:]
+    out_ref[...] = mm(add_matrix(rows, out_ref.shape[0]), table).astype(BF)
+
+
+def send_rows(hot_ref, table, sent_ref, sent_hbm, sems):
+    table = padded(table, hot_ref.shape[1])
+    sent = Sent(sems)
+    step = sent_ref.shape[0] // sems.shape[0]
+    for at in range(0, sent_ref.shape[0], step):
+        cut = slice(at, at + step)
+        sent_ref[cut, :] = mm(hot_ref[cut, :], table).astype(BF)
+        sent(sent_ref.at[cut, :], sent_hbm.at[cut, :])
+    sent.wait()
 
 
 def first_kernel(*refs):
-    *blocks, low_ref, high_ref, rows_ref, latent_ref, own_ref, wb_ref, wc_ref, wn_ref, hot_ref, out_ref, sender_ref, sent_ref = refs
+    *blocks, far_ref, rows_ref, latent_ref, own_ref, wb_ref, wc_ref, wn_ref, hot_ref, out_ref, sender_ref, sent_hbm, sent_ref, out_sems = refs
     rows = rows_from(rows_ref[0], lax.axis_index("mesh"))
     table = jnp.concatenate([b[...] for b in blocks], axis=0)
     total = mm(add_matrix(rows, out_ref.shape[0]), table)
-    total = total + jnp.concatenate([low_ref[...], high_ref[...]], axis=0).astype(F32)
+    total = total + far_ref[...].astype(F32)
     latent = node_update(latent_ref[...], own_ref[...], total, wb_ref[...], wc_ref[...])
     out_ref[...] = latent
     sender = (mm(latent, wn_ref[...]) * 0.5).astype(BF)
     sender_ref[...] = sender
-    sent_ref[...] = mm(hot_ref[...], padded(sender, hot_ref.shape[1])).astype(BF)
+    send_rows(hot_ref, sender, sent_ref, sent_hbm, out_sems)
 
 
 def before_kernel(latent_ref, sender_ref, src_hbm, tgt_hbm, geo_hbm, lift_hbm, w_hbm, *rest, layer, last):
     if last:
-        (grid_hbm, decgeo_hbm, declift_hbm, dec_hbm), rest = rest[:4], rest[4:]
-        (*shares, decw_out), rest = rest[:4], rest[4:]
+        (grid_hbm, decgeo_hbm, declift_hbm, dec_hbm, decsrc_hbm, rows_ref), rest = rest[:6], rest[6:]
+        (*shares, decw_out, deccol_out, rowcol_out), rest = rest[:6], rest[6:]
     own_ref, src_ref, tgt_ref, *bases = rest[:5]
     (wc_out, wf_out), rest = rest[5:7], rest[7:]
     if last:
-        (grid_ref, decgeo_ref, declift_ref, decv_ref, decw_ref, total_ref, share_ref), rest = rest[:7], rest[7:]
+        (grid_ref, decgeo_ref, declift_ref, decv_ref, decw_ref, total_ref, share_ref, decsrc_ref, deccol_ref, rowcol_ref), rest = rest[:10], rest[10:]
     geo_ref, lift_ref, wb_ref, wd_ref, wc_ref, wf_ref, sems, out_sems = rest
     more = {}
     if last:
         more = dict(
             grid=(grid_hbm, grid_ref), decgeo=(decgeo_hbm, decgeo_ref), declift=(declift_hbm, declift_ref),
-            decv=(dec_hbm.at[1], decv_ref), decw=(dec_hbm.at[2], decw_ref),
+            decv=(dec_hbm.at[1], decv_ref), decw=(dec_hbm.at[2], decw_ref), decsrc=(decsrc_hbm, decsrc_ref),
         )
     held = Held(
         sems, wb=(w_hbm.at[layer, 1], wb_ref), src=(src_hbm, src_ref), tgt=(tgt_hbm, tgt_ref), geo=(geo_hbm, geo_ref),
@@ -273,7 +293,7 @@
             groups = [as_ones(lane_hits(src_col, lane) | lane_hits(tgt_col, lane)) for lane in range(0, wide, 128)]
             base = mm(jnp.concatenate(groups, axis=1), table) + lift(geo_ref[:, near:near + 128], right)
             base_ref[at:at + 128, :] = base.astype(BF)
-    own_ref[...] = mm(latent, held("wd")[...])
+    own_ref[...] = mm(latent, held("wd")[...]).astype(BF)
     wc_ref[...] = centered(held("wc")[...])
     sent(wc_ref, wc_out)
     wf_ref[...] = centered(held("wf")[...])
@@ -283,6 +303,13 @@
         total_ref[...] = mm(held("grid")[...], held("decv")[...]) * 0.5
         decw_ref[...] = centered(held("decw")[...])
         sent(decw_ref, decw_out)
+        n_mesh, count = rows_ref.shape[1:]
+        rowcol_ref[...] = to_columns(rows_to(rows_ref[0], lax.axis_index("mesh"))).astype(jnp.int16)
+        sent(rowcol_ref, rowcol_out)
+        held("decsrc")
+        for which in range(decsrc_ref.shape[0]):
+            deccol_ref[which] = place_columns(decsrc_ref[which:which + 1, :], n_mesh, count).astype(jnp.int16)
+            sent(deccol_ref.at[which], deccol_out.at[which])
         held("decgeo")
         for which, out in enumerate(shares):
             for at in range(0, out.shape[0], 256):
@@ -293,75 +320,83 @@
 
 
 def layer_kernel(latent_ref, came_ref, own_ref, src_ref, tgt_ref, *rest, layer, last):
-    (*bases, wc_hbm, wf_hbm, w_hbm, next_hbm, pick_ref, _), rest = rest[:8], rest[8:]
-    outs, (message_ref, wc_ref, we_ref, wf_ref, wn_ref, hot_ref, sems) = rest[:-7], rest[-7:]
-    more = {} if last else dict(hot=(pick_ref, hot_ref))
+    (*bases, wc_hbm, wf_hbm, w_hbm, next_hbm, pick_ref, places_ref), rest = rest[:8], rest[8:]
+    outs, (message_ref, wc_ref, we_ref, wf_ref, wn_ref, hot_ref, sent_ref, sems, out_sems) = rest[:-9], rest[-9:]
     held = Held(
         sems, wc=(wc_hbm, wc_ref), we=(w_hbm.at[layer, 4], we_ref), wf=(wf_hbm, wf_ref),
-        wn=(next_hbm.at[0] if last else next_hbm.at[layer + 1, 0], wn_ref), **more,
+        wn=(next_hbm.at[0] if last else next_hbm.at[layer + 1, 0], wn_ref), **({} if last else dict(hot=(pick_ref, hot_ref))),
     )
     rows = latent_ref.shape[0]
     for part, base_ref in enumerate(bases):
         count = base_ref.shape[0]
-        hits = pick_matrix(to_columns(lanes(src_ref, part * count, count) - rows), came_ref.shape[0])
-        half = mm(hits, came_ref[...]) + base_ref[...].astype(F32)
-        message = scaled(mm(half_silu(half).astype(BF), held("wc")[...]))
-        message_ref[part * count:(part + 1) * count, :] = message.astype(BF)
+        cut = slice(part * count, (part + 1) * count)
+        columns = to_columns(lanes(src_ref, part * count, count)) - rows
+        half = mm(pick_matrix(columns, came_ref.shape[0]), came_ref[...]) + base_ref[...].astype(F32)
+        message_ref[cut, :] = scaled(mm(half_silu(half).astype(BF), held("wc")[...])).astype(BF)
     total = mm(add_matrix(lanes(tgt_ref, 0, message_ref.shape[0]), rows), message_ref[...])
-    latent = node_update(latent_ref[...], own_ref[...], total, held("we")[...], held("wf")[...])
+    latent = node_update(latent_ref[...], own_ref[...].astype(F32), total, held("we")[...], held("wf")[...])
     outs[0][...] = latent
     onward = mm(latent, held("wn")[...])
     if last:
         onward = onward.astype(BF)
-        outs[1][...] = onward
-        spread(rows_to(pick_ref[0], lax.axis_index("mesh")), onward, outs[2:])
+        outs[1][:rows, :] = onward
+        places = jnp.concatenate([places_ref[1, m:m + 1, :] for m in range(places_ref.shape[1])], axis=1).astype(F32)
+        outs[1][rows:, :] = jnp.broadcast_to(places, (outs[1].shape[0] - rows, places.shape[1])).astype(BF)
+        spread(to_columns(rows_to(places_ref[0], lax.axis_index("mesh"))), onward, outs[2:])
     else:
         onward = (onward * 0.5).astype(BF)
         outs[1][...] = onward
-        outs[2][...] = mm(held("hot")[...], padded(onward, hot_ref.shape[1])).astype(BF)
-
-
-def spread(row, table, outs):
-    picked = pick_rows(row, table)
+        send_rows(held("hot"), onward, sent_ref, outs[2], out_sems)
+
+
+def spread(columns, table, outs):
+    wide = -(-table.shape[0] // 128) * 128
+    picked = mm(pick_matrix(columns, wide), padded(table, wide)).astype(BF)
     count = outs[0].shape[0]
     for dz, out in enumerate(outs):
-        out[...] = picked[dz * count:(dz + 1) * count]
-
-
-def spread_kernel(table_ref, rows_ref, *outs):
-    spread(rows_to(rows_ref[1], lax.axis_index("mesh")), table_ref[...], outs)
-
-
-def place_columns(place, part, n_mesh, count):
+        out[out.shape[0] - count:, :] = picked[dz * count:(dz + 1) * count]
+
+
+def spread_kernel(moved_ref, opposite_ref, *outs):
+    rows = moved_ref.shape[0] - EXTRA
+    count = outs[0].shape[0]
+    places = moved_ref[rows:rows + 16, :].astype(F32).astype(jnp.int32)[:1, :]
+    places = jnp.concatenate([places[:, m * count:(m + 1) * count] for m in range(len(outs))], axis=0)
+    outs[OPPOSITE][:count, :] = opposite_ref[...]
+    spread(to_columns(rows_to(places, lax.axis_index("mesh"))), moved_ref[:rows, :], outs)
+
+
+def place_columns(place, n_mesh, count):
     me = lax.axis_index("mesh")
-    local = place - part * n_mesh * count
-    turn = lax.bitwise_and(me - lax.div(local, count), n_mesh - 1) * count + lax.bitwise_and(local, count - 1)
-    return to_columns(jnp.where((local >= 0) & (local < n_mesh * count), turn, -1))
+    block = lax.div(place, count)
+    turn = lax.bitwise_and(me - block, n_mesh - 1) + lax.bitwise_and(block, -n_mesh)
+    turn = jnp.where(turn == OPPOSITE, n_mesh - 1, jnp.where(turn == n_mesh - 1, OPPOSITE, turn))
+    return to_columns(turn * count + lax.bitwise_and(place, count - 1))
 
 
 def decode_near_kernel(*refs):
-    *blocks, dec0, dec1, dec2, src_hbm, base_ref, hot0, hot1, hot2, src_ref, share_ref, sems = refs
-    held = Held(sems, src=(src_hbm, src_ref), **{
-        f"d{i}": (dec, share_ref.at[i]) for i, dec in enumerate((dec0, dec1, dec2))
+    *blocks, dec0, dec1, dec2, col_hbm, base_ref, hot0, hot1, hot2, col_ref, share_ref, sems = refs
+    held = Held(sems, **{
+        name: pair for i, dec in enumerate((dec0, dec1, dec2))
+        for name, pair in ((f"c{i}", (col_hbm.at[i], col_ref.at[i])), (f"d{i}", (dec, share_ref.at[i])))
     })
     table = jnp.concatenate([b[...] for b in blocks], axis=0) * 0.5
-    count = blocks[0].shape[0]
-    held("src")
+    width, rest = table.shape[0], hot0.shape[1]
     for which, hot in enumerate((hot0, hot1, hot2)):
+        held(f"c{which}"), held(f"d{which}")
         for at in range(0, base_ref.shape[1], BLOCK):
             cut = slice(at, at + BLOCK)
-            place = src_ref[which:which + 1, cut]
-            hits = pick_matrix(place_columns(place, 0, len(blocks), count), table.shape[0])
-            near = mm(hits, table)
-            held(f"d{which}")
-            base_ref[which, cut, :] = near + share_ref[which, cut, :].astype(F32)
-            hot[cut, :] = pick_matrix(place_columns(place, 1, len(blocks), count), table.shape[0])
+            column = col_ref[which, cut, :]
+            base_ref[which, cut, :] = mm(pick_matrix(column, width), table) + share_ref[which, cut, :].astype(F32)
+            hot[cut, :] = pick_matrix(column, rest, width)
 
 
 def decode_kernel(*refs):
     *blocks, base_ref, hot0, hot1, hot2, w_hbm, grid_hbm, out_hbm, w_ref, grid_ref, out_ref, sems, out_sems = refs
     held = Held(sems, w=(w_hbm, w_ref), grid=(grid_hbm, grid_ref))
-    table = jnp.concatenate([b[...] for b in blocks], axis=0) * 0.5
+    count = blocks[0].shape[0]
+    table = [blocks[OPPOSITE][:count, :]] + [b[b.shape[0] - count:, :] for b in blocks]
+    table = jnp.concatenate(table, axis=0) * 0.5
     step = out_ref.shape[0] // out_sems.shape[0]
     sent = []
     for at in range(0, out_ref.shape[0], step):
@@ -402,11 +437,12 @@
     return lax.ppermute(value, "grid", pairs)
 
 
-def exchange(blocks):
-    length = len(blocks)
-    moved = [blocks[0]]
-    for dz in range(1, length):
-        moved.append(lax.ppermute(blocks[dz], "mesh", [(i, (i + dz) % length) for i in range(length)]))
+def exchange(blocks, steps=None):
+    length = lax.axis_size("mesh")
+    moved = []
+    for dz, block in zip(steps or range(length), blocks):
+        pairs = [(i, (i + dz) % length) for i in range(length)]
+        moved.append(lax.ppermute(block, "mesh", pairs) if dz else block)
     return moved
 
 
@@ -456,22 +492,24 @@
     )
     far = exchange(far)
     halo = halo_rows[0].T
-    sends = shape((halo.size, width), BF)
+    sends = pltpu.HBM((halo.size, width), BF)
+    sending = pltpu.VMEM((halo.size, width), BF)
     hot = shape((halo.size, -(-mesh_rows // 128) * 128), BF)
-    *near, start, own, wb, wc, wn, hot, hot_far = call(
-        near_kernel, "near", (block,) * n_mesh + (row, wide_row, weight, weight, weight, hot, pltpu.HBM(hot.shape, BF)),
-        [VM] * 2 + [HB] * 4, (message, slot, halo, mesh_latent, enc_weights, proc_weights),
-        [pltpu.VMEM(halo.shape, jnp.int32), square, square], flops=10**9, outs=(VM,) * (n_mesh + 6) + (HB,), copies=1,
-    )
-    part = shape((mesh_rows // 2, width), BF)
-    up = call(far_kernel, "far", (part, part), [VM] * (n_mesh + 1) + [ANY], (*far, above, near[0]), flops=10**8)
+    near = call(near_kernel, "near", (block,) * n_mesh, [VM] * 2, (message, slot), flops=10**9)
+    up = call(far_kernel, "far", (row,), [VM] * (n_mesh + 1) + [ANY], (*far, above, near[0]), flops=10**8)
     near = exchange(near)
-    up = [strip_shift(up[0], 1), strip_shift(up[1], 1)]
+    start, own, wb, wc, wn, hot, hot_far = call(
+        prep_kernel, "prep", (row, wide_row, weight, weight, weight, hot, pltpu.HBM(hot.shape, BF)),
+        [ANY] + [HB] * 4, (up[0], halo, mesh_latent, enc_weights, proc_weights),
+        [pltpu.VMEM(halo.shape, jnp.int32), square, square], flops=PREP, outs=(VM,) * 6 + (HB,), copies=1,
+    )
+    up = strip_shift(up[0], 1)
     latent, sender, sent = call(
-        first_kernel, "first", (row, row, sends), [VM] * (n_mesh + 9),
-        (*near, *up, slot_row[0], start, own, wb, wc, wn, hot), flops=10**9,
+        first_kernel, "first", (row, row, sends), [VM] * (n_mesh + 8),
+        (*near, up, slot_row[0], start, own, wb, wc, wn, hot), [sending], flops=10**9, outs=(VM, VM, HB), copies=4, wait=False,
     )
     layers = proc_weights.shape[0]
+    moved = shape((mesh_rows + EXTRA, width), BF)
     half = shape((links // 2, width), BF)
     index = shape((links // 128, 128), jnp.int32)
     for layer in range(layers):
@@ -482,47 +520,54 @@
         operands = [
             latent, sender, proc_source.reshape(-1, 128), proc_target.reshape(-1, 128), proc_geometry, proc_lift, proc_weights,
         ]
-        outs = (wide_row, index, index, half, half) + (pltpu.HBM(weight.shape, BF),) * 2
+        outs = (row, index, index, half, half) + (pltpu.HBM(weight.shape, BF),) * 2
         out_specs = (VM,) * 5 + (HB,) * 2
         scratch = [pltpu.VMEM((4, links), F32), lifts, square, square, square, square]
         specs = [VM] * 2 + [HB] * 5
         if last:
-            operands += [grid_latent, dec_geometry.transpose(1, 0, 2), dec_lift, dec_weights]
-            specs += [HB] * 4
-            outs = (pltpu.HBM((nodes, width), BF),) * near_of + (pltpu.HBM(weight.shape, BF),) + outs
-            out_specs = (HB,) * (near_of + 1) + out_specs
+            operands += [grid_latent, dec_geometry.transpose(1, 0, 2), dec_lift, dec_weights, dec_source.T, return_rows[0]]
+            specs += [HB] * 5 + [VM]
+            outs = (pltpu.HBM((nodes, width), BF),) * near_of + (
+                pltpu.HBM(weight.shape, BF), pltpu.HBM((near_of, nodes, 128), jnp.int16), pltpu.HBM((n_mesh * count, 128), jnp.int16),
+            ) + outs
+            out_specs = (HB,) * (near_of + 3) + out_specs
             scratch = [
                 pltpu.VMEM((nodes, width), BF), pltpu.VMEM((near_of, 4, nodes), F32), lifts, square, square,
-                pltpu.VMEM((nodes, width), F32), pltpu.VMEM((near_of, nodes, width), BF),
+                pltpu.VMEM((nodes, width), F32), pltpu.VMEM((near_of, nodes, width), BF), pltpu.VMEM((near_of, nodes), jnp.int32),
+                pltpu.VMEM((near_of, nodes, 128), jnp.int16), pltpu.VMEM((n_mesh * count, 128), jnp.int16),
             ] + scratch
         held = list(call(
             functools.partial(before_kernel, layer=layer, last=last), "before", outs, specs, operands, scratch, flops=10**9,
-            outs=out_specs, copies=3 + near_of,
+            outs=out_specs, copies=4 + 2 * near_of,
         ))
         if last:
-            *shares, dec_out = held[:near_of + 1]
-            held = held[near_of + 1:]
-        if layer == 0:
-            places, held[0] = lax.optimization_barrier((return_rows[0], held[0]))
-            places = strip_shift(places, -1)
+            *shares, dec_out, places_out, rows_out = held[:near_of + 3]
+            held = held[near_of + 3:]
         out = call(
             functools.partial(layer_kernel, layer=layer, last=last), "layer",
-            (row, row) + ((block,) * n_mesh if last else (sends,)), [VM] * 7 + [HB] * 4 + [VM if last else HB, ANY],
-            (latent, came, *held, proc_weights, dec_weights if last else proc_weights, return_rows[0] if last else hot_far, places),
-            [pltpu.VMEM((links, width), BF)] + [square] * 4 + [pltpu.VMEM(hot.shape, BF)], flops=4 * 10**9,
+            (row, moved) + (block,) * n_mesh if last else (row, row, sends), [VM] * 7 + [HB] * 5 + [VM],
+            (latent, came, *held, proc_weights, dec_weights if last else proc_weights, rows_out if last else hot_far, return_rows[0]),
+            [pltpu.VMEM((links, width), BF)] + [square] * 4
+            + [pltpu.VMEM((n_mesh * count, 128), jnp.int16) if last else pltpu.VMEM(hot.shape, BF), sending], flops=4 * 10**9,
+            outs=(VM,) * (2 + n_mesh) if last else (VM, VM, HB), copies=4,
         )
         if last:
             latent, proj, *back = out
         else:
             latent, sender, sent = out
     proj = strip_shift(proj, -1)
-    back = exchange(back)
-    ahead = exchange(call(spread_kernel, "spread", (block,) * n_mesh, [VM] * 2, (proj, places), flops=10**8))
+    opposite = back.pop(OPPOSITE)
+    back = exchange(back, (0, 1, 3))
+    ahead = call(
+        spread_kernel, "spread", tuple(shape((2 * count if dz == OPPOSITE else count, width), BF) for dz in range(n_mesh)), [VM] * 2,
+        (proj, opposite), flops=10**8,
+    )
+    ahead = exchange(ahead)
     base, *hots = call(
         decode_near_kernel, "decode_near",
-        (shape((near_of, nodes, width), F32),) + (shape((nodes, n_mesh * count), BF),) * near_of,
-        [VM] * n_mesh + [HB] * (near_of + 1), (*back, *shares, dec_source.T),
-        [pltpu.VMEM((near_of, nodes), jnp.int32), pltpu.VMEM((near_of, nodes, width), BF)], flops=3 * 10**9,
+        (shape((near_of, nodes, width), F32),) + (shape((nodes, (n_mesh + 1) * count), BF),) * near_of,
+        [VM] * (n_mesh - 1) + [HB] * (near_of + 1), (*back, *shares, places_out),
+        [pltpu.VMEM((near_of, nodes, 128), jnp.int16), pltpu.VMEM((near_of, nodes, width), BF)], flops=3 * 10**9,
     )
     grid_out = call(
         decode_kernel, "decode", pltpu.HBM(grid_latent.shape, BF), [VM] * (n_mesh + 4) + [HB] * 2,

time: 122 us -> 119 us (0.975)
  starting transfers between devices: 43.6 us -> 38.3 us
  waiting for transfers between devices: 34 us -> 35.7 us
    ppermute x5 -> x3, starting transfers between devices: 14.5 us -> 8.06 us  [strip_shift(): return lax.ppermute(value, 'grid', pairs)]
    all_to_all x2, waiting for transfers between devices: 23.4 us -> 28.1 us  [shards(): lax.all_to_all(sent.reshape(lax.axis_size('grid') * n_mesh, -1, width), (...]
    ppermute x12 -> x11, starting transfers between devices: 14.7 us -> 16.3 us  [exchange(): moved.append(lax.ppermute(block, 'mesh', pairs) if dz else block)]
    ppermute x12 -> x11, waiting for transfers between devices: 6.45 us -> 4.94 us  [exchange(): moved.append(lax.ppermute(block, 'mesh', pairs) if dz else block)]
    ppermute x5 -> x3, waiting for transfers between devices: 4.19 us -> 2.7 us  [strip_shift(): return lax.ppermute(value, 'grid', pairs)]
    pallas_call x11 -> x12, Pallas kernels: 42.6 us -> 43.2 us  [call(): pl.pallas_call(kernel, out_shape=out, in_specs=specs, out_specs=jax.tree....]
  transfers between devices with their start and end apart: 19 -> 16, of which waited for: 11 -> 9; matrix products, arithmetic and copies ran while one was open for 0% -> 0% of each run, Pallas kernels for 15% -> 16%
where the time goes in v2:
time: 119 us
  Pallas kernels  43.2 us (36%)
  starting transfers between devices  38.3 us (32%)
  waiting for transfers between devices  35.7 us (30%)
  between operations  1.62 us (1%)
    pallas_call x12, Pallas kernels, call(): pl.pallas_call(kernel, out_shape=out, in_specs=specs, out_specs=jax.tree....  43.2 us
    all_to_all x2, waiting for transfers between devices, shards(): lax.all_to_all(sent.reshape(lax.axis_size('grid') * n_mesh, -1, width), (...  28.1 us
    ppermute x11, starting transfers between devices, exchange(): moved.append(lax.ppermute(block, 'mesh', pairs) if dz else block)  16.3 us
    all_to_all x2, starting transfers between devices, shards(): lax.all_to_all(sent.reshape(lax.axis_size('grid') * n_mesh, -1, width), (...  13.9 us
    ppermute x3, starting transfers between devices, strip_shift(): return lax.ppermute(value, 'grid', pairs)  8.06 us
    ppermute x11, waiting for transfers between devices, exchange(): moved.append(lax.ppermute(block, 'mesh', pairs) if dz else block)  4.94 us
    ppermute x3, waiting for transfers between devices, strip_shift(): return lax.ppermute(value, 'grid', pairs)  2.7 us
  transfers between devices with their start and end apart: 16, of which 9 were waited for; matrix products, arithmetic and copies ran while one was open for 0% of the time, Pallas kernels for 16%

profile of v2, /device:TPU:1, one launch (start us, length us, event | category | flops | bytes accessed | tf_op | source)
XLA Modules:
  0.0 118.9 jit_solution(16365581119403629569)
XLA Ops:
  1.3 7.4 %encode.1 = (bf16[2048,512]{1,0:T(8,128)(2,1)S(1)}, s32[1,2048]{1,0:T(1,128)S(1)}, bf16[128,512]{1,0:T(8,128)(2,1)S(1)}, bf16[128,512]{1,0:T(8,128)(2,1)S(1)}, b...) custom-call(s32[1]{0:T(128)S(6)} %copy.22.count_ref, bf16[1024,512]{1,0:T(8,128)(2,1)} %refs_9_.1, ...), custom_call_target="tpu_custom_call" | custom-call | flops 5000000000 | bytes 4194304 | tf_op jit(solution)/shard_map/encode/pallas_call | solution.py:422
  8.7 2.5 %collective-permute-start.3 = (bf16[128,512]{1,0:T(8,128)(2,1)S(1)}, bf16[128,512]{1,0:T(8,128)(2,1)S(1)}, u32[]{:S(2)}, u32[]{:S(2)}) collective-permute-start(bf16[128,512]{1,0:T(8,128)(2,1)S(1)} %get-tuple-element.66), channel_id=1, source_target_pairs={{0,1},{1,2},{2,3},{3,0},{4,5},{5,6},{6,7},{7,4},{8,9},{9,10},{10,1... | collective-permute-start | bytes 393224 | tf_op jit(solution)/shard_map/ppermute | solution.py:445
  11.2 3.3 %collective-permute-start.4 = (bf16[128,512]{1,0:T(8,128)(2,1)S(1)}, bf16[128,512]{1,0:T(8,128)(2,1)S(1)}, u32[]{:S(2)}, u32[]{:S(2)}) collective-permute-start(bf16[128,512]{1,0:T(8,128)(2,1)S(1)} %get-tuple-element.67), channel_id=1, source_target_pairs={{0,2},{1,3},{2,0},{3,1},{4,6},{5,7},{6,4},{7,5},{8,10},{9,11},{10,... | collective-permute-start | bytes 393224 | tf_op jit(solution)/shard_map/ppermute | solution.py:445
  14.6 0.7 collective-permute-start.5
  15.3 3.4 %collective-permute-start.6 = (s32[2,4,128]{2,1,0:T(4,128)S(1)}, s32[2,4,128]{2,1,0:T(4,128)S(1)}, u32[]{:S(2)}, u32[]{:S(2)}) collective-permute-start(s32[2,4,128]{2,1,0:T(4,128)S(1)} %bitcast.20), channel_id=1, source_target_pairs={{4,0},{8,4},{12,8},{16,12},{20,16},{24,20},{28,24},{32,28},{36,32}... | collective-permute-start | bytes 12296 | tf_op jit(solution)/shard_map/ppermute | solution.py:437
  18.7 1.2 %near.1 = (bf16[128,512]{1,0:T(8,128)(2,1)S(1)}, bf16[128,512]{1,0:T(8,128)(2,1)S(1)}, bf16[128,512]{1,0:T(8,128)(2,1)S(1)}, bf16[128,512]{1,0:T(8,128)(2,1)S(1)}) custom-call(bf16[2048,512]{1,0:T(8,128)(2,1)S(1)} %get-tuple-element.59.message_ref, s32[1,2048]{1,0:T(1,128)S(1)} %get-tuple-element.60.slot_ref), custom_call_target="tpu_custom_call" | custom-call | flops 1000000000 | bytes 4194304 | tf_op jit(solution)/shard_map/near/pallas_call | solution.py:422
  20.0 0.8 collective-permute-start
  20.8 0.7 collective-permute-done.6.refs_4_
  21.6 3.0 %collective-permute-start.2 = (bf16[128,512]{1,0:T(8,128)(2,1)S(1)}, bf16[128,512]{1,0:T(8,128)(2,1)S(1)}, u32[]{:S(2)}, u32[]{:S(2)}) collective-permute-start(bf16[128,512]{1,0:T(8,128)(2,1)S(1)} %get-tuple-element.64), channel_id=1, source_target_pairs={{0,3},{1,0},{2,1},{3,2},{4,7},{5,4},{6,5},{7,6},{8,11},{9,8},{10,9... | collective-permute-start | bytes 393224 | tf_op jit(solution)/shard_map/ppermute | solution.py:445
  24.9 2.3 %collective-permute-start.7 = (bf16[160,512]{1,0:T(8,128)(2,1)S(1)}, bf16[160,512]{1,0:T(8,128)(2,1)S(1)}, u32[]{:S(2)}, u32[]{:S(2)}) collective-permute-start(bf16[160,512]{1,0:T(8,128)(2,1)S(1)} %far.1._), channel_id=1, source_target_pairs={{0,4},{4,8},{8,12},{12,16},{16,20},{20,24},{24,28},{28,32},{32,36}... | collective-permute-start | bytes 491528 | tf_op jit(solution)/shard_map/ppermute | solution.py:437
  27.2 2.0 %prep.1 = (bf16[160,512]{1,0:T(8,128)(2,1)S(1)}, f32[160,512]{1,0:T(8,128)S(1)}, bf16[512,512]{1,0:T(8,128)(2,1)S(1)}, bf16[512,512]{1,0:T(8,128)(2,1)S(1)}, bf1...) custom-call(bf16[160,512]{1,0:T(8,128)(2,1)S(1)} %far.1._, s32[8,128]{1,0:T(8,128)} %bitcast.32, ...), custom_call_target="tpu_custom_call" | custom-call | flops 10000000000 | bytes 4194304 | tf_op jit(solution)/shard_map/prep/pallas_call | solution.py:422
  29.3 0.8 collective-permute-done.2.refs_3_
  30.1 2.1 %first.1 = (bf16[160,512]{1,0:T(8,128)(2,1)S(1)}, bf16[160,512]{1,0:T(8,128)(2,1)S(1)}, bf16[1024,512]{1,0:T(8,128)(2,1)}) custom-call(bf16[128,512]{1,0:T(8,128)(2,1)S(1)} %get-tuple-element.61.refs_5_.refs_0_, bf16[128,512]{1,0:T(8,128)(2,1)S(1)} %collective-permute-done.refs_1_, bf16[128,512]{1,0:T(8,128)(2,1)S(1)} %collective-permute-done.1.refs_2_, ...), custom_call_target="tpu_custom_call" | custom-call | flops 1000000000 | bytes 4194304 | tf_op jit(solution)/shard_map/first/pallas_call | solution.py:422
  32.2 10.1 %all-to-all-start = ((bf16[128,8,512]{2,1,0:T(8,128)(2,1)}), bf16[128,8,512]{2,1,0:T(8,128)(2,1)S(1)}, u32[]{:S(2)}, u32[]{:S(2)}) async-start(bf16[128,8,512]{2,1,0:T(8,128)(2,1)} %bitcast.23), calls=%async_computation | async-start | bytes 2097152 | tf_op jit(solution)/shard_map/all_to_all | solution.py:516
  42.3 4.2 %before.2 = (bf16[160,512]{1,0:T(8,128)(2,1)S(1)}, s32[10,128]{1,0:T(8,128)S(1)}, s32[10,128]{1,0:T(8,128)S(1)}, bf16[640,512]{1,0:T(8,128)(2,1)S(1)}, bf16[640,...) custom-call(bf16[160,512]{1,0:T(8,128)(2,1)S(1)} %get-tuple-element.75.latent_ref, ...), custom_call_target="tpu_custom_call" | custom-call | flops 1000000000 | bytes 4194304 | tf_op jit(solution)/shard_map/before/pallas_call | solution.py:422
  46.5 15.3 %all-to-all-done = bf16[128,8,512]{2,1,0:T(8,128)(2,1)S(1)} async-done(((bf16[128,8,512]{2,1,0:T(8,128)(2,1)}), bf16[128,8,512]{2,1,0:T(8,128)(2,1)S(1)}, u32[]{:S(2)}, u32[]{:S(2)}) %all-to-all-start) | async-done | bytes 1048608 | tf_op jit(solution)/shard_map/all_to_all | solution.py:516
  61.9 5.1 %layer.2 = (bf16[160,512]{1,0:T(8,128)(2,1)S(1)}, bf16[160,512]{1,0:T(8,128)(2,1)S(1)}, bf16[1024,512]{1,0:T(8,128)(2,1)}) custom-call(bf16[160,512]{1,0:T(8,128)(2,1)S(1)} %get-tuple-element.75.latent_ref, bf16[1024,512]{1,0:T(8,128)(2,1)S(1)} %bitcast.15, bf16[160,512]{1,0:T(8,128)(2,1)S(1)} %get-tuple-element.78.own_ref, ...), custom_call_target="tpu_custom_call" | custom-call | flops 4000000000 | bytes 4194304 | tf_op jit(solution)/shard_map/layer/pallas_call | solution.py:422
  67.0 3.9 %all-to-all-start.1 = ((bf16[128,8,512]{2,1,0:T(8,128)(2,1)}), bf16[128,8,512]{2,1,0:T(8,128)(2,1)S(1)}, u32[]{:S(2)}, u32[]{:S(2)}) async-start(bf16[128,8,512]{2,1,0:T(8,128)(2,1)} %bitcast.22), calls=%async_computation.1 | async-start | bytes 2097152 | tf_op jit(solution)/shard_map/all_to_all | solution.py:516
  70.9 7.0 %before.3 = (bf16[1024,512]{1,0:T(8,128)(2,1)}, bf16[1024,512]{1,0:T(8,128)(2,1)}, bf16[1024,512]{1,0:T(8,128)(2,1)}, bf16[512,512]{1,0:T(8,128)(2,1)}, s16[3,10...) custom-call(bf16[160,512]{1,0:T(8,128)(2,1)S(1)} %get-tuple-element., ...), custom_call_target="tpu_custom_call" | custom-call | flops 1000000000 | bytes 4194304 | tf_op jit(solution)/shard_map/before/pallas_call | solution.py:422
  77.9 12.7 %all-to-all-done.1 = bf16[128,8,512]{2,1,0:T(8,128)(2,1)S(1)} async-done(((bf16[128,8,512]{2,1,0:T(8,128)(2,1)}), bf16[128,8,512]{2,1,0:T(8,128)(2,1)S(1)}, u32[]{:S(2)}, u32[]{:S(2)}) %all-to-all-start.1) | async-done | bytes 1048608 | tf_op jit(solution)/shard_map/all_to_all | solution.py:516
  90.6 4.5 %layer.3 = (bf16[160,512]{1,0:T(8,128)(2,1)}, bf16[176,512]{1,0:T(8,128)(2,1)S(1)}, bf16[128,512]{1,0:T(8,128)(2,1)S(1)}, bf16[128,512]{1,0:T(8,128)(2,1)S(1)}, ...) custom-call(bf16[160,512]{1,0:T(8,128)(2,1)S(1)} %get-tuple-element.86.latent_ref, ...), custom_call_target="tpu_custom_call" | custom-call | flops 4000000000 | bytes 4194304 | tf_op jit(solution)/shard_map/layer/pallas_call | solution.py:422
  95.1 2.3 %collective-permute-start.8 = (bf16[176,512]{1,0:T(8,128)(2,1)S(1)}, bf16[176,512]{1,0:T(8,128)(2,1)S(1)}, u32[]{:S(2)}, u32[]{:S(2)}) collective-permute-start(bf16[176,512]{1,0:T(8,128)(2,1)S(1)} %get-tuple-element.97), channel_id=1, source_target_pairs={{4,0},{8,4},{12,8},{16,12},{20,16},{24,20},{28,24},{32,28},{36,32}... | collective-permute-start | bytes 540680 | tf_op jit(solution)/shard_map/ppermute | solution.py:437
  97.4 0.6 collective-permute-start.12
  98.1 2.1 %collective-permute-start.13 = (bf16[128,512]{1,0:T(8,128)(2,1)S(1)}, bf16[128,512]{1,0:T(8,128)(2,1)S(1)}, u32[]{:S(2)}, u32[]{:S(2)}) collective-permute-start(bf16[128,512]{1,0:T(8,128)(2,1)S(1)} %get-tuple-element.105), channel_id=1, source_target_pairs={{0,3},{1,0},{2,1},{3,2},{4,7},{5,4},{6,5},{7,6},{8,11},{9,8},{10,9... | collective-permute-start | bytes 393224 | tf_op jit(solution)/shard_map/ppermute | solution.py:445
  100.2 2.0 %collective-permute-done.8.moved_ref = bf16[176,512]{1,0:T(8,128)(2,1)S(1)} collective-permute-done((bf16[176,512]{1,0:T(8,128)(2,1)S(1)}, bf16[176,512]{1,0:T(8,128)(2,1)S(1)}, u32[]{:S(2)}, u32[]{:S(2)}) %collective-permute-start.8) | collective-permute-done | bytes 180256 | tf_op jit(solution)/shard_map/ppermute | solution.py:437
  102.2 0.4 spread.1
  102.7 2.9 %collective-permute-start.11 = (bf16[128,512]{1,0:T(8,128)(2,1)S(1)}, bf16[128,512]{1,0:T(8,128)(2,1)S(1)}, u32[]{:S(2)}, u32[]{:S(2)}) collective-permute-start(bf16[128,512]{1,0:T(8,128)(2,1)S(1)} %get-tuple-element.102), channel_id=1, source_target_pairs={{0,3},{1,0},{2,1},{3,2},{4,7},{5,4},{6,5},{7,6},{8,11},{9,8},{10,9... | collective-permute-start | bytes 393224 | tf_op jit(solution)/shard_map/ppermute | solution.py:445
  105.6 2.2 %collective-permute-done.13.refs_2_ = bf16[128,512]{1,0:T(8,128)(2,1)S(1)} collective-permute-done((bf16[128,512]{1,0:T(8,128)(2,1)S(1)}, bf16[128,512]{1,0:T(8,128)(2,1)S(1)}, u32[]{:S(2)}, u32[]{:S(2)}) %collective-permute-start.13) | collective-permute-done | bytes 131104 | tf_op jit(solution)/shard_map/ppermute | solution.py:445
  107.9 3.7 %decode_near.1 = (f32[3,1024,512]{2,1,0:T(8,128)S(1)}, bf16[1024,640]{1,0:T(8,128)(2,1)S(1)}, bf16[1024,640]{1,0:T(8,128)(2,1)S(1)}, bf16[1024,640]{1,0:T(8,128)(2,1)S(1)}) custom-call(bf16[128,512]{1,0:T(8,128)(2,1)S(1)} %get-tuple-element.103.refs_0_, bf16[128,512]{1,0:T(8,128)(2,1)S(1)} %collective-permute-done.12.refs_1_, ...), custom_call_target="tpu_custom_call" | custom-call | flops 3000000000 | bytes 4194304 | tf_op jit(solution)/shard_map/decode_near/pallas_call | solution.py:422
  111.6 0.4 collective-permute-done.11.refs_3_
  112.1 1.4 %collective-permute-done.9.refs_1_ = bf16[128,512]{1,0:T(8,128)(2,1)S(1)} collective-permute-done((bf16[128,512]{1,0:T(8,128)(2,1)S(1)}, bf16[128,512]{1,0:T(8,128)(2,1)S(1)}, u32[]{:S(2)}, u32[]{:S(2)}) %collective-permute-start.9) | collective-permute-done | bytes 131104 | tf_op jit(solution)/shard_map/ppermute | solution.py:445
  113.5 5.3 %decode.1 = bf16[1024,512]{1,0:T(8,128)(2,1)} custom-call(bf16[128,512]{1,0:T(8,128)(2,1)S(1)} %get-tuple-element.99.refs_0_, bf16[128,512]{1,0:T(8,128)(2,1)S(1)} %collective-permute-done.9.refs_1_, bf16[256,512]{1,0:T(8,128)(2,1)S(1)} %collective-permute-done.10.refs_2_, bf16[128,512]{1,0:T(8,128)(2,1)S(1)} %collective-permute-done.11.refs_3_, ...), custom_call_target="tpu_custom_call" | custom-call | flops 3000000000 | bytes 4194304 | tf_op jit(solution)/shard_map/decode/pallas_call | solution.py:422
  (16 shorter events, 0.6 us)
Async XLA Ops:
  1.3 14.0 %copy-start.1 = (s32[1,2,4,128]{3,2,1,0:T(4,128)S(1)}, s32[1,2,4,128]{3,2,1,0:T(4,128)}, u32[]{:S(2)}) copy-start(s32[1,2,4,128]{3,2,1,0:T(4,128)} %param.26) | copy-start | bytes 12292
  8.7 12.9 %collective-permute-start.3 = (bf16[128,512]{1,0:T(8,128)(2,1)S(1)}, bf16[128,512]{1,0:T(8,128)(2,1)S(1)}, u32[]{:S(2)}, u32[]{:S(2)}) collective-permute-start(bf16[128,512]{1,0:T(8,128)(2,1)S(1)} %get-tuple-element.66), channel_id=1, source_target_pairs={{0,1},{1,2},{2,3},{3,0},{4,5},{5,6},{6,7},{7,4},{8,9},{9,10},{10,1... | collective-permute-start | bytes 393224 | tf_op jit(solution)/shard_map/ppermute | solution.py:445
  11.2 13.3 %collective-permute-start.4 = (bf16[128,512]{1,0:T(8,128)(2,1)S(1)}, bf16[128,512]{1,0:T(8,128)(2,1)S(1)}, u32[]{:S(2)}, u32[]{:S(2)}) collective-permute-start(bf16[128,512]{1,0:T(8,128)(2,1)S(1)} %get-tuple-element.67), channel_id=1, source_target_pairs={{0,2},{1,3},{2,0},{3,1},{4,6},{5,7},{6,4},{7,5},{8,10},{9,11},{10,... | collective-permute-start | bytes 393224 | tf_op jit(solution)/shard_map/ppermute | solution.py:445
  14.6 10.0 %collective-permute-start.5 = (bf16[128,512]{1,0:T(8,128)(2,1)S(1)}, bf16[128,512]{1,0:T(8,128)(2,1)S(1)}, u32[]{:S(2)}, u32[]{:S(2)}) collective-permute-start(bf16[128,512]{1,0:T(8,128)(2,1)S(1)} %get-tuple-element.68), channel_id=1, source_target_pairs={{0,3},{1,0},{2,1},{3,2},{4,7},{5,4},{6,5},{7,6},{8,11},{9,8},{10,9... | collective-permute-start | bytes 393224 | tf_op jit(solution)/shard_map/ppermute | solution.py:445
  15.3 6.1 %collective-permute-start.6 = (s32[2,4,128]{2,1,0:T(4,128)S(1)}, s32[2,4,128]{2,1,0:T(4,128)S(1)}, u32[]{:S(2)}, u32[]{:S(2)}) collective-permute-start(s32[2,4,128]{2,1,0:T(4,128)S(1)} %bitcast.20), channel_id=1, source_target_pairs={{4,0},{8,4},{12,8},{16,12},{20,16},{24,20},{28,24},{32,28},{36,32}... | collective-permute-start | bytes 12296 | tf_op jit(solution)/shard_map/ppermute | solution.py:437
  20.0 9.3 %collective-permute-start = (bf16[128,512]{1,0:T(8,128)(2,1)S(1)}, bf16[128,512]{1,0:T(8,128)(2,1)S(1)}, u32[]{:S(2)}, u32[]{:S(2)}) collective-permute-start(bf16[128,512]{1,0:T(8,128)(2,1)S(1)} %get-tuple-element.62), channel_id=1, source_target_pairs={{0,1},{1,2},{2,3},{3,0},{4,5},{5,6},{6,7},{7,4},{8,9},{9,10},{10,1... | collective-permute-start | bytes 393224 | tf_op jit(solution)/shard_map/ppermute | solution.py:445
  21.4 7.8 %collective-permute-start.1 = (bf16[128,512]{1,0:T(8,128)(2,1)S(1)}, bf16[128,512]{1,0:T(8,128)(2,1)S(1)}, u32[]{:S(2)}, u32[]{:S(2)}) collective-permute-start(bf16[128,512]{1,0:T(8,128)(2,1)S(1)} %get-tuple-element.63), channel_id=1, source_target_pairs={{0,2},{1,3},{2,0},{3,1},{4,6},{5,7},{6,4},{7,5},{8,10},{9,11},{10,... | collective-permute-start | bytes 393224 | tf_op jit(solution)/shard_map/ppermute | solution.py:445
  21.6 8.5 %collective-permute-start.2 = (bf16[128,512]{1,0:T(8,128)(2,1)S(1)}, bf16[128,512]{1,0:T(8,128)(2,1)S(1)}, u32[]{:S(2)}, u32[]{:S(2)}) collective-permute-start(bf16[128,512]{1,0:T(8,128)(2,1)S(1)} %get-tuple-element.64), channel_id=1, source_target_pairs={{0,3},{1,0},{2,1},{3,2},{4,7},{5,4},{6,5},{7,6},{8,11},{9,8},{10,9... | collective-permute-start | bytes 393224 | tf_op jit(solution)/shard_map/ppermute | solution.py:445
  24.9 5.2 %collective-permute-start.7 = (bf16[160,512]{1,0:T(8,128)(2,1)S(1)}, bf16[160,512]{1,0:T(8,128)(2,1)S(1)}, u32[]{:S(2)}, u32[]{:S(2)}) collective-permute-start(bf16[160,512]{1,0:T(8,128)(2,1)S(1)} %far.1._), channel_id=1, source_target_pairs={{0,4},{4,8},{8,12},{12,16},{16,20},{20,24},{24,28},{28,32},{32,36}... | collective-permute-start | bytes 491528 | tf_op jit(solution)/shard_map/ppermute | solution.py:437
  32.2 29.7 %all-to-all-start = ((bf16[128,8,512]{2,1,0:T(8,128)(2,1)}), bf16[128,8,512]{2,1,0:T(8,128)(2,1)S(1)}, u32[]{:S(2)}, u32[]{:S(2)}) async-start(bf16[128,8,512]{2,1,0:T(8,128)(2,1)} %bitcast.23), calls=%async_computation | async-start | bytes 2097152 | tf_op jit(solution)/shard_map/all_to_all | solution.py:516
  42.3 19.6 %copy-start = (s32[1,2,4,128]{3,2,1,0:T(4,128)S(1)}, s32[1,2,4,128]{3,2,1,0:T(4,128)}, u32[]{:S(2)}) copy-start(s32[1,2,4,128]{3,2,1,0:T(4,128)} %param.31) | copy-start | bytes 12292
  67.0 23.6 %all-to-all-start.1 = ((bf16[128,8,512]{2,1,0:T(8,128)(2,1)}), bf16[128,8,512]{2,1,0:T(8,128)(2,1)S(1)}, u32[]{:S(2)}, u32[]{:S(2)}) async-start(bf16[128,8,512]{2,1,0:T(8,128)(2,1)} %bitcast.22), calls=%async_computation.1 | async-start | bytes 2097152 | tf_op jit(solution)/shard_map/all_to_all | solution.py:516
  95.1 7.1 %collective-permute-start.8 = (bf16[176,512]{1,0:T(8,128)(2,1)S(1)}, bf16[176,512]{1,0:T(8,128)(2,1)S(1)}, u32[]{:S(2)}, u32[]{:S(2)}) collective-permute-start(bf16[176,512]{1,0:T(8,128)(2,1)S(1)} %get-tuple-element.97), channel_id=1, source_target_pairs={{4,0},{8,4},{12,8},{16,12},{20,16},{24,20},{28,24},{32,28},{36,32}... | collective-permute-start | bytes 540680 | tf_op jit(solution)/shard_map/ppermute | solution.py:437
  97.4 8.2 %collective-permute-start.12 = (bf16[128,512]{1,0:T(8,128)(2,1)S(1)}, bf16[128,512]{1,0:T(8,128)(2,1)S(1)}, u32[]{:S(2)}, u32[]{:S(2)}) collective-permute-start(bf16[128,512]{1,0:T(8,128)(2,1)S(1)} %get-tuple-element.104), channel_id=1, source_target_pairs={{0,1},{1,2},{2,3},{3,0},{4,5},{5,6},{6,7},{7,4},{8,9},{9,10},{10,1... | collective-permute-start | bytes 393224 | tf_op jit(solution)/shard_map/ppermute | solution.py:445
  98.1 9.8 %collective-permute-start.13 = (bf16[128,512]{1,0:T(8,128)(2,1)S(1)}, bf16[128,512]{1,0:T(8,128)(2,1)S(1)}, u32[]{:S(2)}, u32[]{:S(2)}) collective-permute-start(bf16[128,512]{1,0:T(8,128)(2,1)S(1)} %get-tuple-element.105), channel_id=1, source_target_pairs={{0,3},{1,0},{2,1},{3,2},{4,7},{5,4},{6,5},{7,6},{8,11},{9,8},{10,9... | collective-permute-start | bytes 393224 | tf_op jit(solution)/shard_map/ppermute | solution.py:445
  102.6 10.9 %collective-permute-start.10 = (bf16[256,512]{1,0:T(8,128)(2,1)S(1)}, bf16[256,512]{1,0:T(8,128)(2,1)S(1)}, u32[]{:S(2)}, u32[]{:S(2)}) collective-permute-start(bf16[256,512]{1,0:T(8,128)(2,1)S(1)} %get-tuple-element.101), channel_id=1, source_target_pairs={{0,2},{1,3},{2,0},{3,1},{4,6},{5,7},{6,4},{7,5},{8,10},{9,11},{10,... | collective-permute-start | bytes 786440 | tf_op jit(solution)/shard_map/ppermute | solution.py:445
  102.7 9.4 %collective-permute-start.11 = (bf16[128,512]{1,0:T(8,128)(2,1)S(1)}, bf16[128,512]{1,0:T(8,128)(2,1)S(1)}, u32[]{:S(2)}, u32[]{:S(2)}) collective-permute-start(bf16[128,512]{1,0:T(8,128)(2,1)S(1)} %get-tuple-element.102), channel_id=1, source_target_pairs={{0,3},{1,0},{2,1},{3,2},{4,7},{5,4},{6,5},{7,6},{8,11},{9,8},{10,9... | collective-permute-start | bytes 393224 | tf_op jit(solution)/shard_map/ppermute | solution.py:445
  105.6 7.8 %collective-permute-start.9 = (bf16[128,512]{1,0:T(8,128)(2,1)S(1)}, bf16[128,512]{1,0:T(8,128)(2,1)S(1)}, u32[]{:S(2)}, u32[]{:S(2)}) collective-permute-start(bf16[128,512]{1,0:T(8,128)(2,1)S(1)} %get-tuple-element.100), channel_id=1, source_target_pairs={{0,1},{1,2},{2,3},{3,0},{4,5},{5,6},{6,7},{7,4},{8,9},{9,10},{10,1... | collective-permute-start | bytes 393224 | tf_op jit(solution)/shard_map/ppermute | solution.py:445

commit v3 on v2

--- a/solution.py
+++ b/solution.py
@@ -15,7 +15,7 @@
 ANY = pl.BlockSpec(memory_space=pl.ANY)
 MIB = 1024 * 1024
 BLOCK = 512
-OPPOSITE = 2
+RIDING = 3
 EXTRA = 16
 PREP = 10**10
 
@@ -357,12 +357,12 @@
         out[out.shape[0] - count:, :] = picked[dz * count:(dz + 1) * count]
 
 
-def spread_kernel(moved_ref, opposite_ref, *outs):
+def spread_kernel(moved_ref, riding_ref, *outs):
     rows = moved_ref.shape[0] - EXTRA
     count = outs[0].shape[0]
     places = moved_ref[rows:rows + 16, :].astype(F32).astype(jnp.int32)[:1, :]
     places = jnp.concatenate([places[:, m * count:(m + 1) * count] for m in range(len(outs))], axis=0)
-    outs[OPPOSITE][:count, :] = opposite_ref[...]
+    outs[RIDING][:count, :] = riding_ref[...]
     spread(to_columns(rows_to(places, lax.axis_index("mesh"))), moved_ref[:rows, :], outs)
 
 
@@ -370,16 +370,16 @@
     me = lax.axis_index("mesh")
     block = lax.div(place, count)
     turn = lax.bitwise_and(me - block, n_mesh - 1) + lax.bitwise_and(block, -n_mesh)
-    turn = jnp.where(turn == OPPOSITE, n_mesh - 1, jnp.where(turn == n_mesh - 1, OPPOSITE, turn))
+    turn = jnp.where(turn == RIDING, n_mesh, jnp.where((turn > RIDING) & (turn <= n_mesh), turn - 1, turn))
     return to_columns(turn * count + lax.bitwise_and(place, count - 1))
 
 
 def decode_near_kernel(*refs):
-    *blocks, dec0, dec1, dec2, col_hbm, base_ref, hot0, hot1, hot2, col_ref, share_ref, sems = refs
-    held = Held(sems, **{
-        name: pair for i, dec in enumerate((dec0, dec1, dec2))
-        for name, pair in ((f"c{i}", (col_hbm.at[i], col_ref.at[i])), (f"d{i}", (dec, share_ref.at[i])))
-    })
+    *blocks, dec0, dec1, dec2, col_hbm, w_hbm, grid_hbm, base_ref, hot0, hot1, hot2, w_out, grid_out, col_ref, share_ref, sems = refs
+    pairs = {}
+    for i, dec in enumerate((dec0, dec1, dec2)):
+        pairs.update({f"c{i}": (col_hbm.at[i], col_ref.at[i]), f"d{i}": (dec, share_ref.at[i])})
+    held = Held(sems, **pairs, w=(w_hbm, w_out), grid=(grid_hbm, grid_out))
     table = jnp.concatenate([b[...] for b in blocks], axis=0) * 0.5
     width, rest = table.shape[0], hot0.shape[1]
     for which, hot in enumerate((hot0, hot1, hot2)):
@@ -389,13 +389,13 @@
             column = col_ref[which, cut, :]
             base_ref[which, cut, :] = mm(pick_matrix(column, width), table) + share_ref[which, cut, :].astype(F32)
             hot[cut, :] = pick_matrix(column, rest, width)
+    held("w"), held("grid")
 
 
 def decode_kernel(*refs):
-    *blocks, base_ref, hot0, hot1, hot2, w_hbm, grid_hbm, out_hbm, w_ref, grid_ref, out_ref, sems, out_sems = refs
-    held = Held(sems, w=(w_hbm, w_ref), grid=(grid_hbm, grid_ref))
+    *blocks, base_ref, hot0, hot1, hot2, w_ref, grid_ref, out_hbm, out_ref, out_sems = refs
     count = blocks[0].shape[0]
-    table = [blocks[OPPOSITE][:count, :]] + [b[b.shape[0] - count:, :] for b in blocks]
+    table = [blocks[RIDING - 1][:count, :]] + [b[b.shape[0] - count:, :] for b in blocks]
     table = jnp.concatenate(table, axis=0) * 0.5
     step = out_ref.shape[0] // out_sems.shape[0]
     sent = []
@@ -405,8 +405,8 @@
         for which, hot in enumerate((hot0, hot1, hot2)):
             more = half_silu(base_ref[which, cut, :] + mm(hot[cut, :], table))
             hidden = more if hidden is None else hidden + more
-        update = scaled(mm(hidden.astype(BF), held("w")[...]))
-        out_ref[cut, :] = (held("grid")[cut, :].astype(F32) + update).astype(BF)
+        update = scaled(mm(hidden.astype(BF), w_ref[...]))
+        out_ref[cut, :] = (grid_ref[cut, :].astype(F32) + update).astype(BF)
         sent.append(pltpu.make_async_copy(out_ref.at[cut, :], out_hbm.at[cut, :], out_sems.at[at // step]))
         sent[-1].start()
     for copy in sent:
@@ -556,24 +556,24 @@
         else:
             latent, sender, sent = out
     proj = strip_shift(proj, -1)
-    opposite = back.pop(OPPOSITE)
-    back = exchange(back, (0, 1, 3))
+    riding = back.pop(RIDING)
+    back = exchange(back, (0, 1, 2))
     ahead = call(
-        spread_kernel, "spread", tuple(shape((2 * count if dz == OPPOSITE else count, width), BF) for dz in range(n_mesh)), [VM] * 2,
-        (proj, opposite), flops=10**8,
+        spread_kernel, "spread", tuple(shape((2 * count if dz == RIDING else count, width), BF) for dz in range(n_mesh)), [VM] * 2,
+        (proj, riding), flops=10**8,
     )
     ahead = exchange(ahead)
-    base, *hots = call(
+    base, *hots, dec_out, rows = call(
         decode_near_kernel, "decode_near",
-        (shape((near_of, nodes, width), F32),) + (shape((nodes, (n_mesh + 1) * count), BF),) * near_of,
-        [VM] * (n_mesh - 1) + [HB] * (near_of + 1), (*back, *shares, places_out),
+        (shape((near_of, nodes, width), F32),) + (shape((nodes, n_mesh * count), BF),) * near_of + (weight, shape((nodes, width), BF)),
+        [VM] * n_mesh + [HB] * (near_of + 3), (*back, ahead.pop(0), *shares, places_out, dec_out, grid_latent),
         [pltpu.VMEM((near_of, nodes, 128), jnp.int16), pltpu.VMEM((near_of, nodes, width), BF)], flops=3 * 10**9,
     )
     grid_out = call(
-        decode_kernel, "decode", pltpu.HBM(grid_latent.shape, BF), [VM] * (n_mesh + 4) + [HB] * 2,
-        (*ahead, base, *hots, dec_out, grid_latent),
-        [square, pltpu.VMEM((nodes, width), BF), pltpu.VMEM((nodes, width), BF)],
-        flops=3 * 10**9, outs=HB, copies=4,
+        decode_kernel, "decode", pltpu.HBM(grid_latent.shape, BF), [VM] * (n_mesh + 5),
+        (*ahead, base, *hots, dec_out, rows),
+        [pltpu.VMEM((nodes, width), BF)],
+        flops=3 * 10**9, outs=HB, copies=4, wait=False,
     )
     return (grid_out, latent)
 

time: 119 us -> 118 us (level)
  Pallas kernels: 43.2 us -> 41.6 us
    pallas_call x12, Pallas kernels: 43.2 us -> 41.6 us  [call(): pl.pallas_call(kernel, out_shape=out, in_specs=specs, out_specs=jax.tree....]
where the time goes in v3:
time: 118 us; the launch traced here: 117 us
  Pallas kernels  41.6 us (35%)
  starting transfers between devices  37.8 us (32%)
  waiting for transfers between devices  36.2 us (31%)
  between operations  1.61 us (1%)
    pallas_call x12, Pallas kernels, call(): pl.pallas_call(kernel, out_shape=out, in_specs=specs, out_specs=jax.tree....  41.6 us
    all_to_all x2, waiting for transfers between devices, shards(): lax.all_to_all(sent.reshape(lax.axis_size('grid') * n_mesh, -1, width), (...  28.1 us
    ppermute x11, starting transfers between devices, exchange(): moved.append(lax.ppermute(block, 'mesh', pairs) if dz else block)  15.8 us
    all_to_all x2, starting transfers between devices, shards(): lax.all_to_all(sent.reshape(lax.axis_size('grid') * n_mesh, -1, width), (...  13.9 us
    ppermute x3, starting transfers between devices, strip_shift(): return lax.ppermute(value, 'grid', pairs)  8.06 us
    ppermute x11, waiting for transfers between devices, exchange(): moved.append(lax.ppermute(block, 'mesh', pairs) if dz else block)  4.77 us
    ppermute x3, waiting for transfers between devices, strip_shift(): return lax.ppermute(value, 'grid', pairs)  3.33 us
  transfers between devices with their start and end apart: 16, of which 9 were waited for; matrix products, arithmetic and copies ran while one was open for 0% of the time, Pallas kernels for 16%

profile of v3, /device:TPU:1, one launch (start us, length us, event | category | flops | bytes accessed | tf_op | source)
XLA Modules:
  0.0 117.1 jit_solution(17382709728322310591)
XLA Ops:
  1.3 7.4 %encode.1 = (bf16[2048,512]{1,0:T(8,128)(2,1)S(1)}, s32[1,2048]{1,0:T(1,128)S(1)}, bf16[128,512]{1,0:T(8,128)(2,1)S(1)}, bf16[128,512]{1,0:T(8,128)(2,1)S(1)}, b...) custom-call(s32[1]{0:T(128)S(6)} %copy.22.count_ref, bf16[1024,512]{1,0:T(8,128)(2,1)} %refs_9_.1, ...), custom_call_target="tpu_custom_call" | custom-call | flops 5000000000 | bytes 4194304 | tf_op jit(solution)/shard_map/encode/pallas_call | solution.py:422
  8.7 2.5 %collective-permute-start.3 = (bf16[128,512]{1,0:T(8,128)(2,1)S(1)}, bf16[128,512]{1,0:T(8,128)(2,1)S(1)}, u32[]{:S(2)}, u32[]{:S(2)}) collective-permute-start(bf16[128,512]{1,0:T(8,128)(2,1)S(1)} %get-tuple-element.68), channel_id=1, source_target_pairs={{0,1},{1,2},{2,3},{3,0},{4,5},{5,6},{6,7},{7,4},{8,9},{9,10},{10,1... | collective-permute-start | bytes 393224 | tf_op jit(solution)/shard_map/ppermute | solution.py:445
  11.2 3.3 %collective-permute-start.4 = (bf16[128,512]{1,0:T(8,128)(2,1)S(1)}, bf16[128,512]{1,0:T(8,128)(2,1)S(1)}, u32[]{:S(2)}, u32[]{:S(2)}) collective-permute-start(bf16[128,512]{1,0:T(8,128)(2,1)S(1)} %get-tuple-element.69), channel_id=1, source_target_pairs={{0,2},{1,3},{2,0},{3,1},{4,6},{5,7},{6,4},{7,5},{8,10},{9,11},{10,... | collective-permute-start | bytes 393224 | tf_op jit(solution)/shard_map/ppermute | solution.py:445
  14.6 0.7 collective-permute-start.5
  15.3 3.4 %collective-permute-start.6 = (s32[2,4,128]{2,1,0:T(4,128)S(1)}, s32[2,4,128]{2,1,0:T(4,128)S(1)}, u32[]{:S(2)}, u32[]{:S(2)}) collective-permute-start(s32[2,4,128]{2,1,0:T(4,128)S(1)} %bitcast.20), channel_id=1, source_target_pairs={{4,0},{8,4},{12,8},{16,12},{20,16},{24,20},{28,24},{32,28},{36,32}... | collective-permute-start | bytes 12296 | tf_op jit(solution)/shard_map/ppermute | solution.py:437
  18.7 1.2 %near.1 = (bf16[128,512]{1,0:T(8,128)(2,1)S(1)}, bf16[128,512]{1,0:T(8,128)(2,1)S(1)}, bf16[128,512]{1,0:T(8,128)(2,1)S(1)}, bf16[128,512]{1,0:T(8,128)(2,1)S(1)}) custom-call(bf16[2048,512]{1,0:T(8,128)(2,1)S(1)} %get-tuple-element.61.message_ref, s32[1,2048]{1,0:T(1,128)S(1)} %get-tuple-element.62.slot_ref), custom_call_target="tpu_custom_call" | custom-call | flops 1000000000 | bytes 4194304 | tf_op jit(solution)/shard_map/near/pallas_call | solution.py:422
  20.0 0.8 collective-permute-start
  20.8 0.7 collective-permute-done.6.refs_4_
  21.6 3.0 %collective-permute-start.2 = (bf16[128,512]{1,0:T(8,128)(2,1)S(1)}, bf16[128,512]{1,0:T(8,128)(2,1)S(1)}, u32[]{:S(2)}, u32[]{:S(2)}) collective-permute-start(bf16[128,512]{1,0:T(8,128)(2,1)S(1)} %get-tuple-element.66), channel_id=1, source_target_pairs={{0,3},{1,0},{2,1},{3,2},{4,7},{5,4},{6,5},{7,6},{8,11},{9,8},{10,9... | collective-permute-start | bytes 393224 | tf_op jit(solution)/shard_map/ppermute | solution.py:445
  24.9 2.3 %collective-permute-start.7 = (bf16[160,512]{1,0:T(8,128)(2,1)S(1)}, bf16[160,512]{1,0:T(8,128)(2,1)S(1)}, u32[]{:S(2)}, u32[]{:S(2)}) collective-permute-start(bf16[160,512]{1,0:T(8,128)(2,1)S(1)} %far.1._), channel_id=1, source_target_pairs={{0,4},{4,8},{8,12},{12,16},{16,20},{20,24},{24,28},{28,32},{32,36}... | collective-permute-start | bytes 491528 | tf_op jit(solution)/shard_map/ppermute | solution.py:437
  27.2 2.0 %prep.1 = (bf16[160,512]{1,0:T(8,128)(2,1)S(1)}, f32[160,512]{1,0:T(8,128)S(1)}, bf16[512,512]{1,0:T(8,128)(2,1)S(1)}, bf16[512,512]{1,0:T(8,128)(2,1)S(1)}, bf1...) custom-call(bf16[160,512]{1,0:T(8,128)(2,1)S(1)} %far.1._, s32[8,128]{1,0:T(8,128)} %bitcast.32, ...), custom_call_target="tpu_custom_call" | custom-call | flops 10000000000 | bytes 4194304 | tf_op jit(solution)/shard_map/prep/pallas_call | solution.py:422
  29.3 0.8 collective-permute-done.2.refs_3_
  30.1 2.1 %first.1 = (bf16[160,512]{1,0:T(8,128)(2,1)S(1)}, bf16[160,512]{1,0:T(8,128)(2,1)S(1)}, bf16[1024,512]{1,0:T(8,128)(2,1)}) custom-call(bf16[128,512]{1,0:T(8,128)(2,1)S(1)} %get-tuple-element.63.refs_5_.refs_0_, bf16[128,512]{1,0:T(8,128)(2,1)S(1)} %collective-permute-done.refs_1_, bf16[128,512]{1,0:T(8,128)(2,1)S(1)} %collective-permute-done.1.refs_2_, ...), custom_call_target="tpu_custom_call" | custom-call | flops 1000000000 | bytes 4194304 | tf_op jit(solution)/shard_map/first/pallas_call | solution.py:422
  32.2 10.1 %all-to-all-start = ((bf16[128,8,512]{2,1,0:T(8,128)(2,1)}), bf16[128,8,512]{2,1,0:T(8,128)(2,1)S(1)}, u32[]{:S(2)}, u32[]{:S(2)}) async-start(bf16[128,8,512]{2,1,0:T(8,128)(2,1)} %bitcast.23), calls=%async_computation | async-start | bytes 2097152 | tf_op jit(solution)/shard_map/all_to_all | solution.py:516
  42.3 4.2 %before.2 = (bf16[160,512]{1,0:T(8,128)(2,1)S(1)}, s32[10,128]{1,0:T(8,128)S(1)}, s32[10,128]{1,0:T(8,128)S(1)}, bf16[640,512]{1,0:T(8,128)(2,1)S(1)}, bf16[640,...) custom-call(bf16[160,512]{1,0:T(8,128)(2,1)S(1)} %get-tuple-element.77.latent_ref, ...), custom_call_target="tpu_custom_call" | custom-call | flops 1000000000 | bytes 4194304 | tf_op jit(solution)/shard_map/before/pallas_call | solution.py:422
  46.5 15.3 %all-to-all-done = bf16[128,8,512]{2,1,0:T(8,128)(2,1)S(1)} async-done(((bf16[128,8,512]{2,1,0:T(8,128)(2,1)}), bf16[128,8,512]{2,1,0:T(8,128)(2,1)S(1)}, u32[]{:S(2)}, u32[]{:S(2)}) %all-to-all-start) | async-done | bytes 1048608 | tf_op jit(solution)/shard_map/all_to_all | solution.py:516
  61.9 5.1 %layer.2 = (bf16[160,512]{1,0:T(8,128)(2,1)S(1)}, bf16[160,512]{1,0:T(8,128)(2,1)S(1)}, bf16[1024,512]{1,0:T(8,128)(2,1)}) custom-call(bf16[160,512]{1,0:T(8,128)(2,1)S(1)} %get-tuple-element.77.latent_ref, bf16[1024,512]{1,0:T(8,128)(2,1)S(1)} %bitcast.15, bf16[160,512]{1,0:T(8,128)(2,1)S(1)} %get-tuple-element.80.own_ref, ...), custom_call_target="tpu_custom_call" | custom-call | flops 4000000000 | bytes 4194304 | tf_op jit(solution)/shard_map/layer/pallas_call | solution.py:422
  67.0 3.9 %all-to-all-start.1 = ((bf16[128,8,512]{2,1,0:T(8,128)(2,1)}), bf16[128,8,512]{2,1,0:T(8,128)(2,1)S(1)}, u32[]{:S(2)}, u32[]{:S(2)}) async-start(bf16[128,8,512]{2,1,0:T(8,128)(2,1)} %bitcast.22), calls=%async_computation.1 | async-start | bytes 2097152 | tf_op jit(solution)/shard_map/all_to_all | solution.py:516
  70.9 7.0 %before.3 = (bf16[1024,512]{1,0:T(8,128)(2,1)}, bf16[1024,512]{1,0:T(8,128)(2,1)}, bf16[1024,512]{1,0:T(8,128)(2,1)}, bf16[512,512]{1,0:T(8,128)(2,1)}, s16[3,10...) custom-call(bf16[160,512]{1,0:T(8,128)(2,1)S(1)} %get-tuple-element., ...), custom_call_target="tpu_custom_call" | custom-call | flops 1000000000 | bytes 4194304 | tf_op jit(solution)/shard_map/before/pallas_call | solution.py:422
  77.9 12.7 %all-to-all-done.1 = bf16[128,8,512]{2,1,0:T(8,128)(2,1)S(1)} async-done(((bf16[128,8,512]{2,1,0:T(8,128)(2,1)}), bf16[128,8,512]{2,1,0:T(8,128)(2,1)S(1)}, u32[]{:S(2)}, u32[]{:S(2)}) %all-to-all-start.1) | async-done | bytes 1048608 | tf_op jit(solution)/shard_map/all_to_all | solution.py:516
  90.6 4.5 %layer.3 = (bf16[160,512]{1,0:T(8,128)(2,1)}, bf16[176,512]{1,0:T(8,128)(2,1)S(1)}, bf16[128,512]{1,0:T(8,128)(2,1)S(1)}, bf16[128,512]{1,0:T(8,128)(2,1)S(1)}, ...) custom-call(bf16[160,512]{1,0:T(8,128)(2,1)S(1)} %get-tuple-element.88.latent_ref, ...), custom_call_target="tpu_custom_call" | custom-call | flops 4000000000 | bytes 4194304 | tf_op jit(solution)/shard_map/layer/pallas_call | solution.py:422
  95.1 2.3 %collective-permute-start.8 = (bf16[176,512]{1,0:T(8,128)(2,1)S(1)}, bf16[176,512]{1,0:T(8,128)(2,1)S(1)}, u32[]{:S(2)}, u32[]{:S(2)}) collective-permute-start(bf16[176,512]{1,0:T(8,128)(2,1)S(1)} %get-tuple-element.99), channel_id=1, source_target_pairs={{4,0},{8,4},{12,8},{16,12},{20,16},{24,20},{28,24},{32,28},{36,32}... | collective-permute-start | bytes 540680 | tf_op jit(solution)/shard_map/ppermute | solution.py:437
  98.1 1.5 %collective-permute-start.13 = (bf16[128,512]{1,0:T(8,128)(2,1)S(1)}, bf16[128,512]{1,0:T(8,128)(2,1)S(1)}, u32[]{:S(2)}, u32[]{:S(2)}) collective-permute-start(bf16[128,512]{1,0:T(8,128)(2,1)S(1)} %get-tuple-element.106), channel_id=1, source_target_pairs={{0,2},{1,3},{2,0},{3,1},{4,6},{5,7},{6,4},{7,5},{8,10},{9,11},{10,... | collective-permute-start | bytes 393224 | tf_op jit(solution)/shard_map/ppermute | solution.py:445
  99.6 2.7 %collective-permute-done.8.moved_ref = bf16[176,512]{1,0:T(8,128)(2,1)S(1)} collective-permute-done((bf16[176,512]{1,0:T(8,128)(2,1)S(1)}, bf16[176,512]{1,0:T(8,128)(2,1)S(1)}, u32[]{:S(2)}, u32[]{:S(2)}) %collective-permute-start.8) | collective-permute-done | bytes 180256 | tf_op jit(solution)/shard_map/ppermute | solution.py:437
  102.6 0.6 collective-permute-start.9
  103.2 1.1 collective-permute-start.10
  104.3 1.4 %collective-permute-start.11 = (bf16[256,512]{1,0:T(8,128)(2,1)S(1)}, bf16[256,512]{1,0:T(8,128)(2,1)S(1)}, u32[]{:S(2)}, u32[]{:S(2)}) collective-permute-start(bf16[256,512]{1,0:T(8,128)(2,1)S(1)} %get-tuple-element.103), channel_id=1, source_target_pairs={{0,3},{1,0},{2,1},{3,2},{4,7},{5,4},{6,5},{7,6},{8,11},{9,8},{10,9... | collective-permute-start | bytes 786440 | tf_op jit(solution)/shard_map/ppermute | solution.py:445
  105.7 1.3 %collective-permute-done.12.refs_1_ = bf16[128,512]{1,0:T(8,128)(2,1)S(1)} collective-permute-done((bf16[128,512]{1,0:T(8,128)(2,1)S(1)}, bf16[128,512]{1,0:T(8,128)(2,1)S(1)}, u32[]{:S(2)}, u32[]{:S(2)}) %collective-permute-start.12) | collective-permute-done | bytes 131104 | tf_op jit(solution)/shard_map/ppermute | solution.py:445
  107.0 3.7 %decode_near.1 = (f32[3,1024,512]{2,1,0:T(8,128)S(1)}, bf16[1024,512]{1,0:T(8,128)(2,1)S(1)}, bf16[1024,512]{1,0:T(8,128)(2,1)S(1)}, bf16[1024,512]{1,0:T(8,128)...) custom-call(bf16[128,512]{1,0:T(8,128)(2,1)S(1)} %get-tuple-element.104.refs_0_, ...), custom_call_target="tpu_custom_call" | custom-call | flops 3000000000 | bytes 4194304 | tf_op jit(solution)/shard_map/decode_near/pallas_call | solution.py:422
  110.8 1.6 %collective-permute-done.9.refs_0_ = bf16[128,512]{1,0:T(8,128)(2,1)S(1)} collective-permute-done((bf16[128,512]{1,0:T(8,128)(2,1)S(1)}, bf16[128,512]{1,0:T(8,128)(2,1)S(1)}, u32[]{:S(2)}, u32[]{:S(2)}) %collective-permute-start.9) | collective-permute-done | bytes 131104 | tf_op jit(solution)/shard_map/ppermute | solution.py:445
  112.4 1.0 collective-permute-done.11.refs_2_
  113.3 3.7 %decode.1 = bf16[1024,512]{1,0:T(8,128)(2,1)} custom-call(bf16[128,512]{1,0:T(8,128)(2,1)S(1)} %collective-permute-done.9.refs_0_, bf16[128,512]{1,0:T(8,128)(2,1)S(1)} %collective-permute-done.10.refs_1_, bf16[256,512]{1,0:T(8,128)(2,1)S(1)} %collective-permute-done.11.refs_2_, f32[3,1024,512]{2,1,0:T(8,128)S(1)} %get-tuple-element.113.refs_3_, ...), custom_call_target="tpu_custom_call" | custom-call | flops 3000000000 | bytes 4194304 | tf_op jit(solution)/shard_map/decode/pallas_call | solution.py:422
  (16 shorter events, 1.5 us)
Async XLA Ops:
  1.3 14.0 %copy-start.1 = (s32[1,2,4,128]{3,2,1,0:T(4,128)S(1)}, s32[1,2,4,128]{3,2,1,0:T(4,128)}, u32[]{:S(2)}) copy-start(s32[1,2,4,128]{3,2,1,0:T(4,128)} %param.26) | copy-start | bytes 12292
  8.7 12.9 %collective-permute-start.3 = (bf16[128,512]{1,0:T(8,128)(2,1)S(1)}, bf16[128,512]{1,0:T(8,128)(2,1)S(1)}, u32[]{:S(2)}, u32[]{:S(2)}) collective-permute-start(bf16[128,512]{1,0:T(8,128)(2,1)S(1)} %get-tuple-element.68), channel_id=1, source_target_pairs={{0,1},{1,2},{2,3},{3,0},{4,5},{5,6},{6,7},{7,4},{8,9},{9,10},{10,1... | collective-permute-start | bytes 393224 | tf_op jit(solution)/shard_map/ppermute | solution.py:445
  11.2 13.3 %collective-permute-start.4 = (bf16[128,512]{1,0:T(8,128)(2,1)S(1)}, bf16[128,512]{1,0:T(8,128)(2,1)S(1)}, u32[]{:S(2)}, u32[]{:S(2)}) collective-permute-start(bf16[128,512]{1,0:T(8,128)(2,1)S(1)} %get-tuple-element.69), channel_id=1, source_target_pairs={{0,2},{1,3},{2,0},{3,1},{4,6},{5,7},{6,4},{7,5},{8,10},{9,11},{10,... | collective-permute-start | bytes 393224 | tf_op jit(solution)/shard_map/ppermute | solution.py:445
  14.6 10.0 %collective-permute-start.5 = (bf16[128,512]{1,0:T(8,128)(2,1)S(1)}, bf16[128,512]{1,0:T(8,128)(2,1)S(1)}, u32[]{:S(2)}, u32[]{:S(2)}) collective-permute-start(bf16[128,512]{1,0:T(8,128)(2,1)S(1)} %get-tuple-element.70), channel_id=1, source_target_pairs={{0,3},{1,0},{2,1},{3,2},{4,7},{5,4},{6,5},{7,6},{8,11},{9,8},{10,9... | collective-permute-start | bytes 393224 | tf_op jit(solution)/shard_map/ppermute | solution.py:445
  15.3 6.1 %collective-permute-start.6 = (s32[2,4,128]{2,1,0:T(4,128)S(1)}, s32[2,4,128]{2,1,0:T(4,128)S(1)}, u32[]{:S(2)}, u32[]{:S(2)}) collective-permute-start(s32[2,4,128]{2,1,0:T(4,128)S(1)} %bitcast.20), channel_id=1, source_target_pairs={{4,0},{8,4},{12,8},{16,12},{20,16},{24,20},{28,24},{32,28},{36,32}... | collective-permute-start | bytes 12296 | tf_op jit(solution)/shard_map/ppermute | solution.py:437
  20.0 9.3 %collective-permute-start = (bf16[128,512]{1,0:T(8,128)(2,1)S(1)}, bf16[128,512]{1,0:T(8,128)(2,1)S(1)}, u32[]{:S(2)}, u32[]{:S(2)}) collective-permute-start(bf16[128,512]{1,0:T(8,128)(2,1)S(1)} %get-tuple-element.64), channel_id=1, source_target_pairs={{0,1},{1,2},{2,3},{3,0},{4,5},{5,6},{6,7},{7,4},{8,9},{9,10},{10,1... | collective-permute-start | bytes 393224 | tf_op jit(solution)/shard_map/ppermute | solution.py:445
  21.4 7.8 %collective-permute-start.1 = (bf16[128,512]{1,0:T(8,128)(2,1)S(1)}, bf16[128,512]{1,0:T(8,128)(2,1)S(1)}, u32[]{:S(2)}, u32[]{:S(2)}) collective-permute-start(bf16[128,512]{1,0:T(8,128)(2,1)S(1)} %get-tuple-element.65), channel_id=1, source_target_pairs={{0,2},{1,3},{2,0},{3,1},{4,6},{5,7},{6,4},{7,5},{8,10},{9,11},{10,... | collective-permute-start | bytes 393224 | tf_op jit(solution)/shard_map/ppermute | solution.py:445
  21.6 8.5 %collective-permute-start.2 = (bf16[128,512]{1,0:T(8,128)(2,1)S(1)}, bf16[128,512]{1,0:T(8,128)(2,1)S(1)}, u32[]{:S(2)}, u32[]{:S(2)}) collective-permute-start(bf16[128,512]{1,0:T(8,128)(2,1)S(1)} %get-tuple-element.66), channel_id=1, source_target_pairs={{0,3},{1,0},{2,1},{3,2},{4,7},{5,4},{6,5},{7,6},{8,11},{9,8},{10,9... | collective-permute-start | bytes 393224 | tf_op jit(solution)/shard_map/ppermute | solution.py:445
  24.9 5.2 %collective-permute-start.7 = (bf16[160,512]{1,0:T(8,128)(2,1)S(1)}, bf16[160,512]{1,0:T(8,128)(2,1)S(1)}, u32[]{:S(2)}, u32[]{:S(2)}) collective-permute-start(bf16[160,512]{1,0:T(8,128)(2,1)S(1)} %far.1._), channel_id=1, source_target_pairs={{0,4},{4,8},{8,12},{12,16},{16,20},{20,24},{24,28},{28,32},{32,36}... | collective-permute-start | bytes 491528 | tf_op jit(solution)/shard_map/ppermute | solution.py:437
  32.2 29.7 %all-to-all-start = ((bf16[128,8,512]{2,1,0:T(8,128)(2,1)}), bf16[128,8,512]{2,1,0:T(8,128)(2,1)S(1)}, u32[]{:S(2)}, u32[]{:S(2)}) async-start(bf16[128,8,512]{2,1,0:T(8,128)(2,1)} %bitcast.23), calls=%async_computation | async-start | bytes 2097152 | tf_op jit(solution)/shard_map/all_to_all | solution.py:516
  42.3 19.6 %copy-start = (s32[1,2,4,128]{3,2,1,0:T(4,128)S(1)}, s32[1,2,4,128]{3,2,1,0:T(4,128)}, u32[]{:S(2)}) copy-start(s32[1,2,4,128]{3,2,1,0:T(4,128)} %param.31) | copy-start | bytes 12292
  67.0 23.6 %all-to-all-start.1 = ((bf16[128,8,512]{2,1,0:T(8,128)(2,1)}), bf16[128,8,512]{2,1,0:T(8,128)(2,1)S(1)}, u32[]{:S(2)}, u32[]{:S(2)}) async-start(bf16[128,8,512]{2,1,0:T(8,128)(2,1)} %bitcast.22), calls=%async_computation.1 | async-start | bytes 2097152 | tf_op jit(solution)/shard_map/all_to_all | solution.py:516
  95.1 7.1 %collective-permute-start.8 = (bf16[176,512]{1,0:T(8,128)(2,1)S(1)}, bf16[176,512]{1,0:T(8,128)(2,1)S(1)}, u32[]{:S(2)}, u32[]{:S(2)}) collective-permute-start(bf16[176,512]{1,0:T(8,128)(2,1)S(1)} %get-tuple-element.99), channel_id=1, source_target_pairs={{4,0},{8,4},{12,8},{16,12},{20,16},{24,20},{28,24},{32,28},{36,32}... | collective-permute-start | bytes 540680 | tf_op jit(solution)/shard_map/ppermute | solution.py:437
  97.4 9.6 %collective-permute-start.12 = (bf16[128,512]{1,0:T(8,128)(2,1)S(1)}, bf16[128,512]{1,0:T(8,128)(2,1)S(1)}, u32[]{:S(2)}, u32[]{:S(2)}) collective-permute-start(bf16[128,512]{1,0:T(8,128)(2,1)S(1)} %get-tuple-element.105), channel_id=1, source_target_pairs={{0,1},{1,2},{2,3},{3,0},{4,5},{5,6},{6,7},{7,4},{8,9},{9,10},{10,1... | collective-permute-start | bytes 393224 | tf_op jit(solution)/shard_map/ppermute | solution.py:445
  98.1 9.0 %collective-permute-start.13 = (bf16[128,512]{1,0:T(8,128)(2,1)S(1)}, bf16[128,512]{1,0:T(8,128)(2,1)S(1)}, u32[]{:S(2)}, u32[]{:S(2)}) collective-permute-start(bf16[128,512]{1,0:T(8,128)(2,1)S(1)} %get-tuple-element.106), channel_id=1, source_target_pairs={{0,2},{1,3},{2,0},{3,1},{4,6},{5,7},{6,4},{7,5},{8,10},{9,11},{10,... | collective-permute-start | bytes 393224 | tf_op jit(solution)/shard_map/ppermute | solution.py:445
  102.6 9.7 %collective-permute-start.9 = (bf16[128,512]{1,0:T(8,128)(2,1)S(1)}, bf16[128,512]{1,0:T(8,128)(2,1)S(1)}, u32[]{:S(2)}, u32[]{:S(2)}) collective-permute-start(bf16[128,512]{1,0:T(8,128)(2,1)S(1)} %get-tuple-element.101), channel_id=1, source_target_pairs={{0,1},{1,2},{2,3},{3,0},{4,5},{5,6},{6,7},{7,4},{8,9},{9,10},{10,1... | collective-permute-start | bytes 393224 | tf_op jit(solution)/shard_map/ppermute | solution.py:445
  103.2 9.1 %collective-permute-start.10 = (bf16[128,512]{1,0:T(8,128)(2,1)S(1)}, bf16[128,512]{1,0:T(8,128)(2,1)S(1)}, u32[]{:S(2)}, u32[]{:S(2)}) collective-permute-start(bf16[128,512]{1,0:T(8,128)(2,1)S(1)} %get-tuple-element.102), channel_id=1, source_target_pairs={{0,2},{1,3},{2,0},{3,1},{4,6},{5,7},{6,4},{7,5},{8,10},{9,11},{10,... | collective-permute-start | bytes 393224 | tf_op jit(solution)/shard_map/ppermute | solution.py:445
  104.3 9.0 %collective-permute-start.11 = (bf16[256,512]{1,0:T(8,128)(2,1)S(1)}, bf16[256,512]{1,0:T(8,128)(2,1)S(1)}, u32[]{:S(2)}, u32[]{:S(2)}) collective-permute-start(bf16[256,512]{1,0:T(8,128)(2,1)S(1)} %get-tuple-element.103), channel_id=1, source_target_pairs={{0,3},{1,0},{2,1},{3,2},{4,7},{5,4},{6,5},{7,6},{8,11},{9,8},{10,9... | collective-permute-start | bytes 786440 | tf_op jit(solution)/shard_map/ppermute | solution.py:445

commit v4 on v3

--- a/solution.py
+++ b/solution.py
@@ -202,12 +202,13 @@
     slot_sums(slot_ref[...], 0, len(outs), message_ref[...], outs)
 
 
-def prep_kernel(_, halo_hbm, latent_hbm, w_hbm, next_hbm, *rest):
-    latent_out, own_ref, wb_out, wc_out, wn_out, hot_ref, hot_hbm, halo_ref, wa_ref, wc_ref, sems, out_sems = rest
+def prep_kernel(_, rows_ref, halo_hbm, latent_hbm, w_hbm, next_hbm, *rest):
+    latent_out, own_ref, wb_out, wc_out, wn_out, hot_ref, adds_ref, hot_hbm, halo_ref, wa_ref, wc_ref, sems, out_sems = rest
     held = Held(
         sems, halo=(halo_hbm, halo_ref), latent=(latent_hbm, latent_out), wa=(w_hbm.at[2], wa_ref), wc=(w_hbm.at[4], wc_ref),
         wb=(w_hbm.at[3], wb_out), wn=(next_hbm.at[0, 0], wn_out),
     )
+    adds_ref[...] = add_matrix(rows_from(rows_ref[0], lax.axis_index("mesh")), adds_ref.shape[0])
     halo = held("halo")[...].astype(F32).astype(BF)
     places, owners = halo.shape
     row = lax.broadcasted_iota(jnp.int32, (places * owners, 128), 0)
@@ -244,10 +245,9 @@
 
 
 def first_kernel(*refs):
-    *blocks, far_ref, rows_ref, latent_ref, own_ref, wb_ref, wc_ref, wn_ref, hot_ref, out_ref, sender_ref, sent_hbm, sent_ref, out_sems = refs
-    rows = rows_from(rows_ref[0], lax.axis_index("mesh"))
+    *blocks, far_ref, adds_ref, latent_ref, own_ref, wb_ref, wc_ref, wn_ref, hot_ref, out_ref, sender_ref, sent_hbm, sent_ref, out_sems = refs
     table = jnp.concatenate([b[...] for b in blocks], axis=0)
-    total = mm(add_matrix(rows, out_ref.shape[0]), table)
+    total = mm(adds_ref[...], table)
     total = total + far_ref[...].astype(F32)
     latent = node_update(latent_ref[...], own_ref[...], total, wb_ref[...], wc_ref[...])
     out_ref[...] = latent
@@ -498,15 +498,15 @@
     near = call(near_kernel, "near", (block,) * n_mesh, [VM] * 2, (message, slot), flops=10**9)
     up = call(far_kernel, "far", (row,), [VM] * (n_mesh + 1) + [ANY], (*far, above, near[0]), flops=10**8)
     near = exchange(near)
-    start, own, wb, wc, wn, hot, hot_far = call(
-        prep_kernel, "prep", (row, wide_row, weight, weight, weight, hot, pltpu.HBM(hot.shape, BF)),
-        [ANY] + [HB] * 4, (up[0], halo, mesh_latent, enc_weights, proc_weights),
-        [pltpu.VMEM(halo.shape, jnp.int32), square, square], flops=PREP, outs=(VM,) * 6 + (HB,), copies=1,
+    start, own, wb, wc, wn, hot, adds, hot_far = call(
+        prep_kernel, "prep", (row, wide_row, weight, weight, weight, hot, shape((mesh_rows, n_mesh * count), BF), pltpu.HBM(hot.shape, BF)),
+        [ANY, VM] + [HB] * 4, (up[0], slot_row[0], halo, mesh_latent, enc_weights, proc_weights),
+        [pltpu.VMEM(halo.shape, jnp.int32), square, square], flops=PREP, outs=(VM,) * 7 + (HB,), copies=1,
     )
     up = strip_shift(up[0], 1)
     latent, sender, sent = call(
         first_kernel, "first", (row, row, sends), [VM] * (n_mesh + 8),
-        (*near, up, slot_row[0], start, own, wb, wc, wn, hot), [sending], flops=10**9, outs=(VM, VM, HB), copies=4, wait=False,
+        (*near, up, adds, start, own, wb, wc, wn, hot), [sending], flops=10**9, outs=(VM, VM, HB), copies=4, wait=False,
     )
     layers = proc_weights.shape[0]
     moved = shape((mesh_rows + EXTRA, width), BF)

time: 118 us -> 118 us (level)
  no operation moved by 1% of the time
where the time goes in v4:
time: 118 us; the launch traced here: 117 us
  Pallas kernels  41.6 us (35%)
  starting transfers between devices  37.8 us (32%)
  waiting for transfers between devices  36.2 us (31%)
  between operations  1.61 us (1%)
    pallas_call x12, Pallas kernels, call(): pl.pallas_call(kernel, out_shape=out, in_specs=specs, out_specs=jax.tree....  41.6 us
    all_to_all x2, waiting for transfers between devices, shards(): lax.all_to_all(sent.reshape(lax.axis_size('grid') * n_mesh, -1, width), (...  28.1 us
    ppermute x11, starting transfers between devices, exchange(): moved.append(lax.ppermute(block, 'mesh', pairs) if dz else block)  15.8 us
    all_to_all x2, starting transfers between devices, shards(): lax.all_to_all(sent.reshape(lax.axis_size('grid') * n_mesh, -1, width), (...  14 us
    ppermute x3, starting transfers between devices, strip_shift(): return lax.ppermute(value, 'grid', pairs)  8.06 us
    ppermute x11, waiting for transfers between devices, exchange(): moved.append(lax.ppermute(block, 'mesh', pairs) if dz else block)  4.78 us
    ppermute x3, waiting for transfers between devices, strip_shift(): return lax.ppermute(value, 'grid', pairs)  3.32 us
  transfers between devices with their start and end apart: 16, of which 9 were waited for; matrix products, arithmetic and copies ran while one was open for 0% of the time, Pallas kernels for 16%

profile of v4, /device:TPU:1, one launch (start us, length us, event | category | flops | bytes accessed | tf_op | source)
XLA Modules:
  0.0 117.2 jit_solution(6089929454318694255)
XLA Ops:
  1.3 7.4 %encode.1 = (bf16[2048,512]{1,0:T(8,128)(2,1)S(1)}, s32[1,2048]{1,0:T(1,128)S(1)}, bf16[128,512]{1,0:T(8,128)(2,1)S(1)}, bf16[128,512]{1,0:T(8,128)(2,1)S(1)}, b...) custom-call(s32[1]{0:T(128)S(6)} %copy.22.count_ref, bf16[1024,512]{1,0:T(8,128)(2,1)} %refs_9_.1, ...), custom_call_target="tpu_custom_call" | custom-call | flops 5000000000 | bytes 4194304 | tf_op jit(solution)/shard_map/encode/pallas_call | solution.py:422
  8.7 2.5 %collective-permute-start.3 = (bf16[128,512]{1,0:T(8,128)(2,1)S(1)}, bf16[128,512]{1,0:T(8,128)(2,1)S(1)}, u32[]{:S(2)}, u32[]{:S(2)}) collective-permute-start(bf16[128,512]{1,0:T(8,128)(2,1)S(1)} %get-tuple-element.69), channel_id=1, source_target_pairs={{0,1},{1,2},{2,3},{3,0},{4,5},{5,6},{6,7},{7,4},{8,9},{9,10},{10,1... | collective-permute-start | bytes 393224 | tf_op jit(solution)/shard_map/ppermute | solution.py:445
  11.2 3.3 %collective-permute-start.4 = (bf16[128,512]{1,0:T(8,128)(2,1)S(1)}, bf16[128,512]{1,0:T(8,128)(2,1)S(1)}, u32[]{:S(2)}, u32[]{:S(2)}) collective-permute-start(bf16[128,512]{1,0:T(8,128)(2,1)S(1)} %get-tuple-element.70), channel_id=1, source_target_pairs={{0,2},{1,3},{2,0},{3,1},{4,6},{5,7},{6,4},{7,5},{8,10},{9,11},{10,... | collective-permute-start | bytes 393224 | tf_op jit(solution)/shard_map/ppermute | solution.py:445
  14.6 0.7 collective-permute-start.5
  15.3 3.4 %collective-permute-start.6 = (s32[2,4,128]{2,1,0:T(4,128)S(1)}, s32[2,4,128]{2,1,0:T(4,128)S(1)}, u32[]{:S(2)}, u32[]{:S(2)}) collective-permute-start(s32[2,4,128]{2,1,0:T(4,128)S(1)} %bitcast.20), channel_id=1, source_target_pairs={{4,0},{8,4},{12,8},{16,12},{20,16},{24,20},{28,24},{32,28},{36,32}... | collective-permute-start | bytes 12296 | tf_op jit(solution)/shard_map/ppermute | solution.py:437
  18.7 1.2 %near.1 = (bf16[128,512]{1,0:T(8,128)(2,1)S(1)}, bf16[128,512]{1,0:T(8,128)(2,1)S(1)}, bf16[128,512]{1,0:T(8,128)(2,1)S(1)}, bf16[128,512]{1,0:T(8,128)(2,1)S(1)}) custom-call(bf16[2048,512]{1,0:T(8,128)(2,1)S(1)} %get-tuple-element.62.message_ref, s32[1,2048]{1,0:T(1,128)S(1)} %get-tuple-element.63.slot_ref), custom_call_target="tpu_custom_call" | custom-call | flops 1000000000 | bytes 4194304 | tf_op jit(solution)/shard_map/near/pallas_call | solution.py:422
  20.0 0.8 collective-permute-start
  20.8 0.7 collective-permute-done.6.refs_4_
  21.6 3.0 %collective-permute-start.2 = (bf16[128,512]{1,0:T(8,128)(2,1)S(1)}, bf16[128,512]{1,0:T(8,128)(2,1)S(1)}, u32[]{:S(2)}, u32[]{:S(2)}) collective-permute-start(bf16[128,512]{1,0:T(8,128)(2,1)S(1)} %get-tuple-element.67), channel_id=1, source_target_pairs={{0,3},{1,0},{2,1},{3,2},{4,7},{5,4},{6,5},{7,6},{8,11},{9,8},{10,9... | collective-permute-start | bytes 393224 | tf_op jit(solution)/shard_map/ppermute | solution.py:445
  24.9 2.3 %collective-permute-start.7 = (bf16[160,512]{1,0:T(8,128)(2,1)S(1)}, bf16[160,512]{1,0:T(8,128)(2,1)S(1)}, u32[]{:S(2)}, u32[]{:S(2)}) collective-permute-start(bf16[160,512]{1,0:T(8,128)(2,1)S(1)} %far.1._), channel_id=1, source_target_pairs={{0,4},{4,8},{8,12},{12,16},{16,20},{20,24},{24,28},{28,32},{32,36}... | collective-permute-start | bytes 491528 | tf_op jit(solution)/shard_map/ppermute | solution.py:437
  27.2 2.0 %prep.1 = (bf16[160,512]{1,0:T(8,128)(2,1)S(1)}, f32[160,512]{1,0:T(8,128)S(1)}, bf16[512,512]{1,0:T(8,128)(2,1)S(1)}, bf16[512,512]{1,0:T(8,128)(2,1)S(1)}, bf1...) custom-call(bf16[160,512]{1,0:T(8,128)(2,1)S(1)} %far.1._, ...), custom_call_target="tpu_custom_call" | custom-call | flops 10000000000 | bytes 4194304 | tf_op jit(solution)/shard_map/prep/pallas_call | solution.py:422
  29.3 0.8 collective-permute-done.2.refs_3_
  30.1 2.1 %first.1 = (bf16[160,512]{1,0:T(8,128)(2,1)S(1)}, bf16[160,512]{1,0:T(8,128)(2,1)S(1)}, bf16[1024,512]{1,0:T(8,128)(2,1)}) custom-call(bf16[128,512]{1,0:T(8,128)(2,1)S(1)} %get-tuple-element.64.refs_5_.refs_0_, bf16[128,512]{1,0:T(8,128)(2,1)S(1)} %collective-permute-done.refs_1_, bf16[128,512]{1,0:T(8,128)(2,1)S(1)} %collective-permute-done.1.refs_2_, ...), custom_call_target="tpu_custom_call" | custom-call | flops 1000000000 | bytes 4194304 | tf_op jit(solution)/shard_map/first/pallas_call | solution.py:422
  32.2 10.1 %all-to-all-start = ((bf16[128,8,512]{2,1,0:T(8,128)(2,1)}), bf16[128,8,512]{2,1,0:T(8,128)(2,1)S(1)}, u32[]{:S(2)}, u32[]{:S(2)}) async-start(bf16[128,8,512]{2,1,0:T(8,128)(2,1)} %bitcast.23), calls=%async_computation | async-start | bytes 2097152 | tf_op jit(solution)/shard_map/all_to_all | solution.py:516
  42.3 4.2 %before.2 = (bf16[160,512]{1,0:T(8,128)(2,1)S(1)}, s32[10,128]{1,0:T(8,128)S(1)}, s32[10,128]{1,0:T(8,128)S(1)}, bf16[640,512]{1,0:T(8,128)(2,1)S(1)}, bf16[640,...) custom-call(bf16[160,512]{1,0:T(8,128)(2,1)S(1)} %get-tuple-element.79.latent_ref, ...), custom_call_target="tpu_custom_call" | custom-call | flops 1000000000 | bytes 4194304 | tf_op jit(solution)/shard_map/before/pallas_call | solution.py:422
  46.5 15.3 %all-to-all-done = bf16[128,8,512]{2,1,0:T(8,128)(2,1)S(1)} async-done(((bf16[128,8,512]{2,1,0:T(8,128)(2,1)}), bf16[128,8,512]{2,1,0:T(8,128)(2,1)S(1)}, u32[]{:S(2)}, u32[]{:S(2)}) %all-to-all-start) | async-done | bytes 1048608 | tf_op jit(solution)/shard_map/all_to_all | solution.py:516
  61.9 5.1 %layer.2 = (bf16[160,512]{1,0:T(8,128)(2,1)S(1)}, bf16[160,512]{1,0:T(8,128)(2,1)S(1)}, bf16[1024,512]{1,0:T(8,128)(2,1)}) custom-call(bf16[160,512]{1,0:T(8,128)(2,1)S(1)} %get-tuple-element.79.latent_ref, bf16[1024,512]{1,0:T(8,128)(2,1)S(1)} %bitcast.15, bf16[160,512]{1,0:T(8,128)(2,1)S(1)} %get-tuple-element.82.own_ref, ...), custom_call_target="tpu_custom_call" | custom-call | flops 4000000000 | bytes 4194304 | tf_op jit(solution)/shard_map/layer/pallas_call | solution.py:422
  67.0 3.9 %all-to-all-start.1 = ((bf16[128,8,512]{2,1,0:T(8,128)(2,1)}), bf16[128,8,512]{2,1,0:T(8,128)(2,1)S(1)}, u32[]{:S(2)}, u32[]{:S(2)}) async-start(bf16[128,8,512]{2,1,0:T(8,128)(2,1)} %bitcast.22), calls=%async_computation.1 | async-start | bytes 2097152 | tf_op jit(solution)/shard_map/all_to_all | solution.py:516
  70.9 7.0 %before.3 = (bf16[1024,512]{1,0:T(8,128)(2,1)}, bf16[1024,512]{1,0:T(8,128)(2,1)}, bf16[1024,512]{1,0:T(8,128)(2,1)}, bf16[512,512]{1,0:T(8,128)(2,1)}, s16[3,10...) custom-call(bf16[160,512]{1,0:T(8,128)(2,1)S(1)} %get-tuple-element., ...), custom_call_target="tpu_custom_call" | custom-call | flops 1000000000 | bytes 4194304 | tf_op jit(solution)/shard_map/before/pallas_call | solution.py:422
  77.9 12.7 %all-to-all-done.1 = bf16[128,8,512]{2,1,0:T(8,128)(2,1)S(1)} async-done(((bf16[128,8,512]{2,1,0:T(8,128)(2,1)}), bf16[128,8,512]{2,1,0:T(8,128)(2,1)S(1)}, u32[]{:S(2)}, u32[]{:S(2)}) %all-to-all-start.1) | async-done | bytes 1048608 | tf_op jit(solution)/shard_map/all_to_all | solution.py:516
  90.6 4.5 %layer.3 = (bf16[160,512]{1,0:T(8,128)(2,1)}, bf16[176,512]{1,0:T(8,128)(2,1)S(1)}, bf16[128,512]{1,0:T(8,128)(2,1)S(1)}, bf16[128,512]{1,0:T(8,128)(2,1)S(1)}, ...) custom-call(bf16[160,512]{1,0:T(8,128)(2,1)S(1)} %get-tuple-element.90.latent_ref, ...), custom_call_target="tpu_custom_call" | custom-call | flops 4000000000 | bytes 4194304 | tf_op jit(solution)/shard_map/layer/pallas_call | solution.py:422
  95.1 2.3 %collective-permute-start.8 = (bf16[176,512]{1,0:T(8,128)(2,1)S(1)}, bf16[176,512]{1,0:T(8,128)(2,1)S(1)}, u32[]{:S(2)}, u32[]{:S(2)}) collective-permute-start(bf16[176,512]{1,0:T(8,128)(2,1)S(1)} %get-tuple-element.101), channel_id=1, source_target_pairs={{4,0},{8,4},{12,8},{16,12},{20,16},{24,20},{28,24},{32,28},{36,32}... | collective-permute-start | bytes 540680 | tf_op jit(solution)/shard_map/ppermute | solution.py:437
  98.1 1.5 %collective-permute-start.13 = (bf16[128,512]{1,0:T(8,128)(2,1)S(1)}, bf16[128,512]{1,0:T(8,128)(2,1)S(1)}, u32[]{:S(2)}, u32[]{:S(2)}) collective-permute-start(bf16[128,512]{1,0:T(8,128)(2,1)S(1)} %get-tuple-element.108), channel_id=1, source_target_pairs={{0,2},{1,3},{2,0},{3,1},{4,6},{5,7},{6,4},{7,5},{8,10},{9,11},{10,... | collective-permute-start | bytes 393224 | tf_op jit(solution)/shard_map/ppermute | solution.py:445
  99.6 2.7 %collective-permute-done.8.moved_ref = bf16[176,512]{1,0:T(8,128)(2,1)S(1)} collective-permute-done((bf16[176,512]{1,0:T(8,128)(2,1)S(1)}, bf16[176,512]{1,0:T(8,128)(2,1)S(1)}, u32[]{:S(2)}, u32[]{:S(2)}) %collective-permute-start.8) | collective-permute-done | bytes 180256 | tf_op jit(solution)/shard_map/ppermute | solution.py:437
  102.6 0.6 collective-permute-start.9
  103.2 1.1 collective-permute-start.10
  104.3 1.4 %collective-permute-start.11 = (bf16[256,512]{1,0:T(8,128)(2,1)S(1)}, bf16[256,512]{1,0:T(8,128)(2,1)S(1)}, u32[]{:S(2)}, u32[]{:S(2)}) collective-permute-start(bf16[256,512]{1,0:T(8,128)(2,1)S(1)} %get-tuple-element.105), channel_id=1, source_target_pairs={{0,3},{1,0},{2,1},{3,2},{4,7},{5,4},{6,5},{7,6},{8,11},{9,8},{10,9... | collective-permute-start | bytes 786440 | tf_op jit(solution)/shard_map/ppermute | solution.py:445
  105.7 1.3 %collective-permute-done.12.refs_1_ = bf16[128,512]{1,0:T(8,128)(2,1)S(1)} collective-permute-done((bf16[128,512]{1,0:T(8,128)(2,1)S(1)}, bf16[128,512]{1,0:T(8,128)(2,1)S(1)}, u32[]{:S(2)}, u32[]{:S(2)}) %collective-permute-start.12) | collective-permute-done | bytes 131104 | tf_op jit(solution)/shard_map/ppermute | solution.py:445
  107.1 3.7 %decode_near.1 = (f32[3,1024,512]{2,1,0:T(8,128)S(1)}, bf16[1024,512]{1,0:T(8,128)(2,1)S(1)}, bf16[1024,512]{1,0:T(8,128)(2,1)S(1)}, bf16[1024,512]{1,0:T(8,128)...) custom-call(bf16[128,512]{1,0:T(8,128)(2,1)S(1)} %get-tuple-element.106.refs_0_, ...), custom_call_target="tpu_custom_call" | custom-call | flops 3000000000 | bytes 4194304 | tf_op jit(solution)/shard_map/decode_near/pallas_call | solution.py:422
  110.7 1.6 %collective-permute-done.9.refs_0_ = bf16[128,512]{1,0:T(8,128)(2,1)S(1)} collective-permute-done((bf16[128,512]{1,0:T(8,128)(2,1)S(1)}, bf16[128,512]{1,0:T(8,128)(2,1)S(1)}, u32[]{:S(2)}, u32[]{:S(2)}) %collective-permute-start.9) | collective-permute-done | bytes 131104 | tf_op jit(solution)/shard_map/ppermute | solution.py:445
  112.4 1.0 collective-permute-done.11.refs_2_
  113.3 3.7 %decode.1 = bf16[1024,512]{1,0:T(8,128)(2,1)} custom-call(bf16[128,512]{1,0:T(8,128)(2,1)S(1)} %collective-permute-done.9.refs_0_, bf16[128,512]{1,0:T(8,128)(2,1)S(1)} %collective-permute-done.10.refs_1_, bf16[256,512]{1,0:T(8,128)(2,1)S(1)} %collective-permute-done.11.refs_2_, f32[3,1024,512]{2,1,0:T(8,128)S(1)} %get-tuple-element.115.refs_3_, ...), custom_call_target="tpu_custom_call" | custom-call | flops 3000000000 | bytes 4194304 | tf_op jit(solution)/shard_map/decode/pallas_call | solution.py:422
  (16 shorter events, 1.5 us)
Async XLA Ops:
  1.3 14.0 %copy-start.1 = (s32[1,2,4,128]{3,2,1,0:T(4,128)S(1)}, s32[1,2,4,128]{3,2,1,0:T(4,128)}, u32[]{:S(2)}) copy-start(s32[1,2,4,128]{3,2,1,0:T(4,128)} %param.26) | copy-start | bytes 12292
  8.7 12.9 %collective-permute-start.3 = (bf16[128,512]{1,0:T(8,128)(2,1)S(1)}, bf16[128,512]{1,0:T(8,128)(2,1)S(1)}, u32[]{:S(2)}, u32[]{:S(2)}) collective-permute-start(bf16[128,512]{1,0:T(8,128)(2,1)S(1)} %get-tuple-element.69), channel_id=1, source_target_pairs={{0,1},{1,2},{2,3},{3,0},{4,5},{5,6},{6,7},{7,4},{8,9},{9,10},{10,1... | collective-permute-start | bytes 393224 | tf_op jit(solution)/shard_map/ppermute | solution.py:445
  11.2 13.3 %collective-permute-start.4 = (bf16[128,512]{1,0:T(8,128)(2,1)S(1)}, bf16[128,512]{1,0:T(8,128)(2,1)S(1)}, u32[]{:S(2)}, u32[]{:S(2)}) collective-permute-start(bf16[128,512]{1,0:T(8,128)(2,1)S(1)} %get-tuple-element.70), channel_id=1, source_target_pairs={{0,2},{1,3},{2,0},{3,1},{4,6},{5,7},{6,4},{7,5},{8,10},{9,11},{10,... | collective-permute-start | bytes 393224 | tf_op jit(solution)/shard_map/ppermute | solution.py:445
  14.6 10.0 %collective-permute-start.5 = (bf16[128,512]{1,0:T(8,128)(2,1)S(1)}, bf16[128,512]{1,0:T(8,128)(2,1)S(1)}, u32[]{:S(2)}, u32[]{:S(2)}) collective-permute-start(bf16[128,512]{1,0:T(8,128)(2,1)S(1)} %get-tuple-element.71), channel_id=1, source_target_pairs={{0,3},{1,0},{2,1},{3,2},{4,7},{5,4},{6,5},{7,6},{8,11},{9,8},{10,9... | collective-permute-start | bytes 393224 | tf_op jit(solution)/shard_map/ppermute | solution.py:445
  15.3 6.1 %collective-permute-start.6 = (s32[2,4,128]{2,1,0:T(4,128)S(1)}, s32[2,4,128]{2,1,0:T(4,128)S(1)}, u32[]{:S(2)}, u32[]{:S(2)}) collective-permute-start(s32[2,4,128]{2,1,0:T(4,128)S(1)} %bitcast.20), channel_id=1, source_target_pairs={{4,0},{8,4},{12,8},{16,12},{20,16},{24,20},{28,24},{32,28},{36,32}... | collective-permute-start | bytes 12296 | tf_op jit(solution)/shard_map/ppermute | solution.py:437
  20.0 9.3 %collective-permute-start = (bf16[128,512]{1,0:T(8,128)(2,1)S(1)}, bf16[128,512]{1,0:T(8,128)(2,1)S(1)}, u32[]{:S(2)}, u32[]{:S(2)}) collective-permute-start(bf16[128,512]{1,0:T(8,128)(2,1)S(1)} %get-tuple-element.65), channel_id=1, source_target_pairs={{0,1},{1,2},{2,3},{3,0},{4,5},{5,6},{6,7},{7,4},{8,9},{9,10},{10,1... | collective-permute-start | bytes 393224 | tf_op jit(solution)/shard_map/ppermute | solution.py:445
  21.4 7.8 %collective-permute-start.1 = (bf16[128,512]{1,0:T(8,128)(2,1)S(1)}, bf16[128,512]{1,0:T(8,128)(2,1)S(1)}, u32[]{:S(2)}, u32[]{:S(2)}) collective-permute-start(bf16[128,512]{1,0:T(8,128)(2,1)S(1)} %get-tuple-element.66), channel_id=1, source_target_pairs={{0,2},{1,3},{2,0},{3,1},{4,6},{5,7},{6,4},{7,5},{8,10},{9,11},{10,... | collective-permute-start | bytes 393224 | tf_op jit(solution)/shard_map/ppermute | solution.py:445
  21.6 8.5 %collective-permute-start.2 = (bf16[128,512]{1,0:T(8,128)(2,1)S(1)}, bf16[128,512]{1,0:T(8,128)(2,1)S(1)}, u32[]{:S(2)}, u32[]{:S(2)}) collective-permute-start(bf16[128,512]{1,0:T(8,128)(2,1)S(1)} %get-tuple-element.67), channel_id=1, source_target_pairs={{0,3},{1,0},{2,1},{3,2},{4,7},{5,4},{6,5},{7,6},{8,11},{9,8},{10,9... | collective-permute-start | bytes 393224 | tf_op jit(solution)/shard_map/ppermute | solution.py:445
  24.9 5.2 %collective-permute-start.7 = (bf16[160,512]{1,0:T(8,128)(2,1)S(1)}, bf16[160,512]{1,0:T(8,128)(2,1)S(1)}, u32[]{:S(2)}, u32[]{:S(2)}) collective-permute-start(bf16[160,512]{1,0:T(8,128)(2,1)S(1)} %far.1._), channel_id=1, source_target_pairs={{0,4},{4,8},{8,12},{12,16},{16,20},{20,24},{24,28},{28,32},{32,36}... | collective-permute-start | bytes 491528 | tf_op jit(solution)/shard_map/ppermute | solution.py:437
  32.2 29.7 %all-to-all-start = ((bf16[128,8,512]{2,1,0:T(8,128)(2,1)}), bf16[128,8,512]{2,1,0:T(8,128)(2,1)S(1)}, u32[]{:S(2)}, u32[]{:S(2)}) async-start(bf16[128,8,512]{2,1,0:T(8,128)(2,1)} %bitcast.23), calls=%async_computation | async-start | bytes 2097152 | tf_op jit(solution)/shard_map/all_to_all | solution.py:516
  42.3 19.6 %copy-start = (s32[1,2,4,128]{3,2,1,0:T(4,128)S(1)}, s32[1,2,4,128]{3,2,1,0:T(4,128)}, u32[]{:S(2)}) copy-start(s32[1,2,4,128]{3,2,1,0:T(4,128)} %param.31) | copy-start | bytes 12292
  67.0 23.6 %all-to-all-start.1 = ((bf16[128,8,512]{2,1,0:T(8,128)(2,1)}), bf16[128,8,512]{2,1,0:T(8,128)(2,1)S(1)}, u32[]{:S(2)}, u32[]{:S(2)}) async-start(bf16[128,8,512]{2,1,0:T(8,128)(2,1)} %bitcast.22), calls=%async_computation.1 | async-start | bytes 2097152 | tf_op jit(solution)/shard_map/all_to_all | solution.py:516
  95.1 7.1 %collective-permute-start.8 = (bf16[176,512]{1,0:T(8,128)(2,1)S(1)}, bf16[176,512]{1,0:T(8,128)(2,1)S(1)}, u32[]{:S(2)}, u32[]{:S(2)}) collective-permute-start(bf16[176,512]{1,0:T(8,128)(2,1)S(1)} %get-tuple-element.101), channel_id=1, source_target_pairs={{4,0},{8,4},{12,8},{16,12},{20,16},{24,20},{28,24},{32,28},{36,32}... | collective-permute-start | bytes 540680 | tf_op jit(solution)/shard_map/ppermute | solution.py:437
  97.4 9.6 %collective-permute-start.12 = (bf16[128,512]{1,0:T(8,128)(2,1)S(1)}, bf16[128,512]{1,0:T(8,128)(2,1)S(1)}, u32[]{:S(2)}, u32[]{:S(2)}) collective-permute-start(bf16[128,512]{1,0:T(8,128)(2,1)S(1)} %get-tuple-element.107), channel_id=1, source_target_pairs={{0,1},{1,2},{2,3},{3,0},{4,5},{5,6},{6,7},{7,4},{8,9},{9,10},{10,1... | collective-permute-start | bytes 393224 | tf_op jit(solution)/shard_map/ppermute | solution.py:445
  98.1 9.0 %collective-permute-start.13 = (bf16[128,512]{1,0:T(8,128)(2,1)S(1)}, bf16[128,512]{1,0:T(8,128)(2,1)S(1)}, u32[]{:S(2)}, u32[]{:S(2)}) collective-permute-start(bf16[128,512]{1,0:T(8,128)(2,1)S(1)} %get-tuple-element.108), channel_id=1, source_target_pairs={{0,2},{1,3},{2,0},{3,1},{4,6},{5,7},{6,4},{7,5},{8,10},{9,11},{10,... | collective-permute-start | bytes 393224 | tf_op jit(solution)/shard_map/ppermute | solution.py:445
  102.6 9.8 %collective-permute-start.9 = (bf16[128,512]{1,0:T(8,128)(2,1)S(1)}, bf16[128,512]{1,0:T(8,128)(2,1)S(1)}, u32[]{:S(2)}, u32[]{:S(2)}) collective-permute-start(bf16[128,512]{1,0:T(8,128)(2,1)S(1)} %get-tuple-element.103), channel_id=1, source_target_pairs={{0,1},{1,2},{2,3},{3,0},{4,5},{5,6},{6,7},{7,4},{8,9},{9,10},{10,1... | collective-permute-start | bytes 393224 | tf_op jit(solution)/shard_map/ppermute | solution.py:445
  103.2 9.1 %collective-permute-start.10 = (bf16[128,512]{1,0:T(8,128)(2,1)S(1)}, bf16[128,512]{1,0:T(8,128)(2,1)S(1)}, u32[]{:S(2)}, u32[]{:S(2)}) collective-permute-start(bf16[128,512]{1,0:T(8,128)(2,1)S(1)} %get-tuple-element.104), channel_id=1, source_target_pairs={{0,2},{1,3},{2,0},{3,1},{4,6},{5,7},{6,4},{7,5},{8,10},{9,11},{10,... | collective-permute-start | bytes 393224 | tf_op jit(solution)/shard_map/ppermute | solution.py:445
  104.3 9.0 %collective-permute-start.11 = (bf16[256,512]{1,0:T(8,128)(2,1)S(1)}, bf16[256,512]{1,0:T(8,128)(2,1)S(1)}, u32[]{:S(2)}, u32[]{:S(2)}) collective-permute-start(bf16[256,512]{1,0:T(8,128)(2,1)S(1)} %get-tuple-element.105), channel_id=1, source_target_pairs={{0,3},{1,0},{2,1},{3,2},{4,7},{5,4},{6,5},{7,6},{8,11},{9,8},{10,9... | collective-permute-start | bytes 786440 | tf_op jit(solution)/shard_map/ppermute | solution.py:445
